TPU v7x, 128 devices: a whole 4x4x4 slice. The times are simulated.
128 devices in a mesh: heads: 8 (over x, y_hi), blk: 16 (over z, y_lo, core).
Axes of the slice: x: 4, y: 4 (y_hi: 2, y_lo: 2; y = y_hi * 2 + y_lo), z: 4, core: 2. Of those that a mesh axis runs over, the one named last changes fastest.
Arguments:
- queries: bfloat16 [32768, 64, 128], P(('blk', 'heads')), may hold values from -22 to 22
- key_states: bfloat16 [32768, 8, 128], P(('blk', 'heads')), may hold values from -4 to 4
- value_states: bfloat16 [32768, 8, 128], P(('blk', 'heads')), may hold values from -6 to 6
- block_lists: int32 [256, 64, 8], P(('blk', 'heads')), may hold values from 0 to 255, as said below
Outputs:
- attended: bfloat16 [32768, 64, 128], P(('blk', 'heads'))
Inputs may be any that keep to these rules, and one draw needn't show every extreme that they name: block_lists[j, h] holds 8 distinct blocks, each in the shard of 16 blocks that holds j or in the shard before it; j itself is always listed; every query block outside the first shard lists at least one block of the shard before; over the query blocks of one shard and the 8 query heads of one key head, exactly 4 distinct blocks of the shard before are listed (none for the first shard).
All inputs are finite; a program needn't handle non-finite values.
Results may differ from a plain program's by a relative error of at most 0.0049.
Values may be sent and summed in bfloat16 or wider, within the bound.
No kernel may reach another device: no remote copies, remote signals or barrier semaphores. Data moves between devices by JAX's collectives and lax.ppermute only.
A program may use at most 128 MiB of HBM per device.

v0:
```python
import jax
import jax.numpy as jnp
from jax import lax
from jax.sharding import PartitionSpec as P

BLOCK = 128


def from_behind(block, axis, distance):
    devices = range(lax.axis_size(axis))
    route = [(i - distance, i) for i in devices if i - distance in devices]
    return lax.ppermute(block, axis, route)


def attend_blocks(query_rows, key_table, value_table, listing):
    members = listing.shape[0]
    picked_keys = key_table[listing].reshape(members, -1, key_table.shape[-1])
    picked_values = value_table[listing].reshape(members, -1, value_table.shape[-1])
    scores = jnp.einsum(
        "qbd,qkd->qbk", query_rows, picked_keys, preferred_element_type=jnp.float32
    ) * query_rows.shape[-1] ** (-0.5)
    highest = jnp.max(scores, axis=-1, keepdims=True)
    powers = jnp.exp(scores - highest)
    totals = jnp.sum(powers, axis=-1, keepdims=True)
    weights = (powers / totals).astype(jnp.bfloat16)
    mixed = jnp.einsum("qbk,qkd->qbd", weights, picked_values, preferred_element_type=jnp.float32)
    return mixed.astype(jnp.bfloat16)


def on_device(queries, key_states, value_states, block_lists):
    local_tokens, all_heads, head_width = queries.shape
    sharing = all_heads // key_states.shape[1]
    position = lax.axis_index("blk")
    moved = lax.all_to_all(queries, "heads", split_axis=1, concat_axis=0, tiled=True)
    shard_tokens, local_heads = (moved.shape[0], moved.shape[1])
    shard_blocks = shard_tokens // BLOCK
    local_kv = local_heads // sharing
    first_block = (position - 1) * shard_blocks
    own_keys, own_values, listing = (
        lax.all_to_all(key_states, "heads", split_axis=1, concat_axis=0, tiled=True),
        lax.all_to_all(value_states, "heads", split_axis=1, concat_axis=0, tiled=True),
        lax.all_to_all(block_lists, "heads", split_axis=1, concat_axis=0, tiled=True),
    )
    prev_keys, prev_values = from_behind((own_keys, own_values), "blk", 1)
    key_table = jnp.concatenate([prev_keys, own_keys], 0).reshape(
        2 * shard_blocks, BLOCK, local_kv, head_width
    )
    value_table = jnp.concatenate([prev_values, own_values], 0).reshape(
        2 * shard_blocks, BLOCK, local_kv, head_width
    )
    local_lists = listing - first_block
    query_blocks = moved.reshape(shard_blocks, BLOCK, local_heads, head_width)

    def one_head(head):
        rows = lax.dynamic_index_in_dim(query_blocks, head, 2, keepdims=False)
        key_one = lax.dynamic_index_in_dim(key_table, head // sharing, 2, keepdims=False)
        value_one = lax.dynamic_index_in_dim(value_table, head // sharing, 2, keepdims=False)
        selected = lax.dynamic_index_in_dim(local_lists, head, 1, keepdims=False)
        return attend_blocks(rows, key_one, value_one, selected)

    results = lax.map(one_head, jnp.arange(local_heads, dtype=jnp.int32))
    arranged = jnp.transpose(results, (1, 2, 0, 3)).reshape(shard_tokens, local_heads, head_width)
    return lax.all_to_all(arranged, "heads", split_axis=0, concat_axis=1, tiled=True)


def solution(mesh):
    return jax.shard_map(
        on_device,
        mesh=mesh,
        in_specs=(
            P(("blk", "heads"), None, None),
            P(("blk", "heads"), None, None),
            P(("blk", "heads"), None, None),
            P(("blk", "heads"), None, None),
        ),
        out_specs=P(("blk", "heads"), None, None),
        check_vma=False,
    )
```

profile of v0, /device:TPU:1, one launch (start us, length us, event | category | flops | bytes accessed | tf_op | source)
XLA Modules:
  0.0 392.6 jit_solution(15673001020538131188)
XLA Ops:
  1.5 7.5 %all-to-all-start.2 = ((s32[8,1,128]{2,1,0:T(1,128)}), s32[8,1,128]{2,1,0:T(1,128)S(1)}, u32[]{:S(2)}, u32[]{:S(2)}) async-start(s32[8,1,128]{2,1,0:T(1,128)} %reshape.77), calls=%async_computation.2 | async-start | bytes 8192 | tf_op jit(solution)/shard_map/all_to_all | solution.py:42
  9.0 1.9 copy.26
  10.9 4.4 %all-to-all-done.2 = s32[8,1,128]{2,1,0:T(1,128)S(1)} async-done(((s32[8,1,128]{2,1,0:T(1,128)}), s32[8,1,128]{2,1,0:T(1,128)S(1)}, u32[]{:S(2)}, u32[]{:S(2)}) %all-to-all-start.2) | async-done | bytes 4128 | tf_op jit(solution)/shard_map/all_to_all | solution.py:42
  15.4 3.5 all-to-all-start.1
  18.9 1.9 copy.29
  20.8 6.6 %all-to-all-done.1 = bf16[256,8,128]{2,0,1:T(8,128)(2,1)S(1)} async-done(((bf16[256,8,128]{2,0,1:T(8,128)(2,1)}), bf16[256,8,128]{2,0,1:T(8,128)(2,1)S(1)}, u32[]{:S(2)}, u32[]{:S(2)}) %all-to-all-start.1) | async-done | bytes 524320 | tf_op jit(solution)/shard_map/all_to_all | solution.py:40
  27.4 3.5 all-to-all-start.3
  30.9 6.9 %copy.24 = bf16[256,64,128]{2,0,1:T(8,128)(2,1)} copy(bf16[256,64,128]{2,1,0:T(8,128)(2,1)} %param.6) | data formatting | bytes 8388608 | tf_op args[0]
  37.8 1.6 all-to-all-done.3
  39.4 4.9 %all-to-all-start = ((bf16[256,64,128]{2,0,1:T(8,128)(2,1)}), bf16[256,64,128]{2,0,1:T(8,128)(2,1)}, u32[]{:S(2)}, u32[]{:S(2)}) async-start(bf16[256,64,128]{2,0,1:T(8,128)(2,1)} %copy.24), calls=%async_computation | async-start | bytes 8388608 | tf_op jit(solution)/shard_map/all_to_all | solution.py:34
  44.3 6.4 %collective-permute-start = (bf16[2048,1,128]{2,0,1:T(8,128)(2,1)S(1)}, bf16[2048,1,128]{2,0,1:T(8,128)(2,1)S(1)}, u32[]{:S(2)}, u32[]{:S(2)}) collective-permute-start(bf16[2048,1,128]{2,0,1:T(8,128)(2,1)S(1)} %bitcast.79), channel_id=1, source_target_pairs={{0,1},{1,2},{2,3},{3,4},{4,5},{5,6},{6,7},{7,8},{8,9},{9,10},{10,1... | collective-permute-start | bytes 1572872 | tf_op jit(solution)/shard_map/ppermute | solution.py:12
  52.1 2.1 collective-permute-start.1
  54.3 41.3 %collective-permute-done = bf16[2048,1,128]{2,0,1:T(8,128)(2,1)S(1)} collective-permute-done((bf16[2048,1,128]{2,0,1:T(8,128)(2,1)S(1)}, bf16[2048,1,128]{2,0,1:T(8,128)(2,1)S(1)}, u32[]{:S(2)}, u32[]{:S(2)}) %collective-permute-start) | collective-permute-done | bytes 524320 | tf_op jit(solution)/shard_map/ppermute | solution.py:12
  95.7 5.5 %collective-permute-done.1 = bf16[2048,1,128]{2,0,1:T(8,128)(2,1)S(1)} collective-permute-done((bf16[2048,1,128]{2,0,1:T(8,128)(2,1)S(1)}, bf16[2048,1,128]{2,0,1:T(8,128)(2,1)S(1)}, u32[]{:S(2)}, u32[]{:S(2)}) %collective-permute-start.1) | collective-permute-done | bytes 524320 | tf_op jit(solution)/shard_map/ppermute | solution.py:12
  101.7 4.7 %copy.25 = bf16[8,256,8,128]{3,1,0,2:T(8,128)(2,1)} copy(bf16[8,256,8,128]{3,1,2,0:T(8,128)(2,1)} %bitcast.9) | data formatting | bytes 8388608 | tf_op jit(solution)/shard_map/all_to_all | solution.py:34
  106.4 220.4 %while.10 = (s32[]{:T(128)}, bf16[8,16,128,128]{3,2,1,0:T(8,128)(2,1)}, s32[8]{0:T(128)S(1)}, bf16[16,128,8,128]{3,1,0,2:T(8,128)(2,1)}, bf16[32,128,1,128]{3,1,...) while((s32[]{:T(128)}, ...), condition=%wide.region_3.4_spmd, body=%wide.region_0.3_spmd.sunk | while | flops 1092883840 | bytes 93349048 | solution.py:61
  109.3 3.0 gather_fusion.1
  112.3 3.6 fusion.35
  115.9 2.3 fusion.36
  118.2 0.9 copy-done
  119.1 3.0 gather_fusion
  122.1 11.8 %fusion.37 = bf16[8,16,128,128]{3,2,1,0:T(8,128)(2,1)} fusion(bf16[8,16,128,128]{3,2,1,0:T(8,128)(2,1)} %get-tuple-element.132, s32[]{:T(128)} %get-tuple-element.131, bf16[16,1024,128]{2,1,0:T(8,128)(2,1)} %bitcast.74, f32[16,128]{1,0:T(8,128)S(1)} %fusion.36, f32[16,128,1024]{2,1,0:T(8,128)} %copy-done), kind=kOutput, calls=%fused_computation.11.clone.1 | convolution fusion | flops 547621888 | bytes 21504512 | tf_op jit(solution)/shard_map/while/body/eval_jaxpr/qbk,qkd->qbd/dot_general | solution.py:26
  136.8 3.0 gather_fusion.1
  139.8 3.6 fusion.35
  143.4 2.3 fusion.36
  145.8 0.9 copy-done
  146.7 3.0 gather_fusion
  149.7 11.8 %fusion.37 = bf16[8,16,128,128]{3,2,1,0:T(8,128)(2,1)} fusion(bf16[8,16,128,128]{3,2,1,0:T(8,128)(2,1)} %get-tuple-element.132, s32[]{:T(128)} %get-tuple-element.131, bf16[16,1024,128]{2,1,0:T(8,128)(2,1)} %bitcast.74, f32[16,128]{1,0:T(8,128)S(1)} %fusion.36, f32[16,128,1024]{2,1,0:T(8,128)} %copy-done), kind=kOutput, calls=%fused_computation.11.clone.1 | convolution fusion | flops 547621888 | bytes 21504512 | tf_op jit(solution)/shard_map/while/body/eval_jaxpr/qbk,qkd->qbd/dot_general | solution.py:26
  164.4 3.0 gather_fusion.1
  167.4 3.6 fusion.35
  171.0 2.3 fusion.36
  173.3 0.9 copy-done
  174.2 3.0 gather_fusion
  177.2 11.8 %fusion.37 = bf16[8,16,128,128]{3,2,1,0:T(8,128)(2,1)} fusion(bf16[8,16,128,128]{3,2,1,0:T(8,128)(2,1)} %get-tuple-element.132, s32[]{:T(128)} %get-tuple-element.131, bf16[16,1024,128]{2,1,0:T(8,128)(2,1)} %bitcast.74, f32[16,128]{1,0:T(8,128)S(1)} %fusion.36, f32[16,128,1024]{2,1,0:T(8,128)} %copy-done), kind=kOutput, calls=%fused_computation.11.clone.1 | convolution fusion | flops 547621888 | bytes 21504512 | tf_op jit(solution)/shard_map/while/body/eval_jaxpr/qbk,qkd->qbd/dot_general | solution.py:26
  191.9 3.0 gather_fusion.1
  194.9 3.6 fusion.35
  198.5 2.3 fusion.36
  200.9 0.9 copy-done
  201.8 3.0 gather_fusion
  204.8 11.8 %fusion.37 = bf16[8,16,128,128]{3,2,1,0:T(8,128)(2,1)} fusion(bf16[8,16,128,128]{3,2,1,0:T(8,128)(2,1)} %get-tuple-element.132, s32[]{:T(128)} %get-tuple-element.131, bf16[16,1024,128]{2,1,0:T(8,128)(2,1)} %bitcast.74, f32[16,128]{1,0:T(8,128)S(1)} %fusion.36, f32[16,128,1024]{2,1,0:T(8,128)} %copy-done), kind=kOutput, calls=%fused_computation.11.clone.1 | convolution fusion | flops 547621888 | bytes 21504512 | tf_op jit(solution)/shard_map/while/body/eval_jaxpr/qbk,qkd->qbd/dot_general | solution.py:26
  219.5 3.0 gather_fusion.1
  222.5 3.6 fusion.35
  226.1 2.3 fusion.36
  228.4 0.9 copy-done
  229.3 3.0 gather_fusion
  232.3 11.8 %fusion.37 = bf16[8,16,128,128]{3,2,1,0:T(8,128)(2,1)} fusion(bf16[8,16,128,128]{3,2,1,0:T(8,128)(2,1)} %get-tuple-element.132, s32[]{:T(128)} %get-tuple-element.131, bf16[16,1024,128]{2,1,0:T(8,128)(2,1)} %bitcast.74, f32[16,128]{1,0:T(8,128)S(1)} %fusion.36, f32[16,128,1024]{2,1,0:T(8,128)} %copy-done), kind=kOutput, calls=%fused_computation.11.clone.1 | convolution fusion | flops 547621888 | bytes 21504512 | tf_op jit(solution)/shard_map/while/body/eval_jaxpr/qbk,qkd->qbd/dot_general | solution.py:26
  247.0 3.0 gather_fusion.1
  250.0 3.6 fusion.35
  253.6 2.3 fusion.36
  256.9 3.0 gather_fusion
  259.9 11.8 %fusion.37 = bf16[8,16,128,128]{3,2,1,0:T(8,128)(2,1)} fusion(bf16[8,16,128,128]{3,2,1,0:T(8,128)(2,1)} %get-tuple-element.132, s32[]{:T(128)} %get-tuple-element.131, bf16[16,1024,128]{2,1,0:T(8,128)(2,1)} %bitcast.74, f32[16,128]{1,0:T(8,128)S(1)} %fusion.36, f32[16,128,1024]{2,1,0:T(8,128)} %copy-done), kind=kOutput, calls=%fused_computation.11.clone.1 | convolution fusion | flops 547621888 | bytes 21504512 | tf_op jit(solution)/shard_map/while/body/eval_jaxpr/qbk,qkd->qbd/dot_general | solution.py:26
  274.6 3.0 gather_fusion.1
  277.6 3.6 fusion.35
  281.2 2.3 fusion.36
  284.4 3.0 gather_fusion
  287.4 11.8 %fusion.37 = bf16[8,16,128,128]{3,2,1,0:T(8,128)(2,1)} fusion(bf16[8,16,128,128]{3,2,1,0:T(8,128)(2,1)} %get-tuple-element.132, s32[]{:T(128)} %get-tuple-element.131, bf16[16,1024,128]{2,1,0:T(8,128)(2,1)} %bitcast.74, f32[16,128]{1,0:T(8,128)S(1)} %fusion.36, f32[16,128,1024]{2,1,0:T(8,128)} %copy-done), kind=kOutput, calls=%fused_computation.11.clone.1 | convolution fusion | flops 547621888 | bytes 21504512 | tf_op jit(solution)/shard_map/while/body/eval_jaxpr/qbk,qkd->qbd/dot_general | solution.py:26
  302.1 3.0 gather_fusion.1
  305.1 3.6 fusion.35
  308.7 2.3 fusion.36
  312.0 3.0 gather_fusion
  315.0 11.8 %fusion.37 = bf16[8,16,128,128]{3,2,1,0:T(8,128)(2,1)} fusion(bf16[8,16,128,128]{3,2,1,0:T(8,128)(2,1)} %get-tuple-element.132, s32[]{:T(128)} %get-tuple-element.131, bf16[16,1024,128]{2,1,0:T(8,128)(2,1)} %bitcast.74, f32[16,128]{1,0:T(8,128)S(1)} %fusion.36, f32[16,128,1024]{2,1,0:T(8,128)} %copy-done), kind=kOutput, calls=%fused_computation.11.clone.1 | convolution fusion | flops 547621888 | bytes 21504512 | tf_op jit(solution)/shard_map/while/body/eval_jaxpr/qbk,qkd->qbd/dot_general | solution.py:26
  326.8 5.7 %copy.31 = bf16[16,128,8,128]{3,2,1,0:T(8,128)(2,1)S(1)} copy(bf16[16,128,8,128]{3,1,0,2:T(8,128)(2,1)} %bitcast.78) | data formatting | bytes 8388608 | tf_op jit(solution)/shard_map/transpose | solution.py:62
  332.5 56.9 %all_to_all.78 = bf16[2048,8,128]{2,1,0:T(8,128)(2,1)S(1)} all-to-all(bf16[2048,8,128]{2,1,0:T(8,128)(2,1)S(1)} %bitcast.75), channel_id=1, replica_groups=mesh['heads'=8,'blk'=16] {'heads'}, dimensions={0} | all-to-all | bytes 8388608 | tf_op jit(solution)/shard_map/all_to_all | solution.py:63
  389.4 3.2 copy.34
  (64 shorter events, 12.8 us)
Async XLA Ops:
  1.5 13.8 %all-to-all-start.2 = ((s32[8,1,128]{2,1,0:T(1,128)}), s32[8,1,128]{2,1,0:T(1,128)S(1)}, u32[]{:S(2)}, u32[]{:S(2)}) async-start(s32[8,1,128]{2,1,0:T(1,128)} %reshape.77), calls=%async_computation.2 | async-start | bytes 8192 | tf_op jit(solution)/shard_map/all_to_all | solution.py:42
  15.4 12.0 %all-to-all-start.1 = ((bf16[256,8,128]{2,0,1:T(8,128)(2,1)}), bf16[256,8,128]{2,0,1:T(8,128)(2,1)S(1)}, u32[]{:S(2)}, u32[]{:S(2)}) async-start(bf16[256,8,128]{2,0,1:T(8,128)(2,1)} %copy.26), calls=%async_computation.1 | async-start | bytes 1048576 | tf_op jit(solution)/shard_map/all_to_all | solution.py:40
  27.4 12.0 %all-to-all-start.3 = ((bf16[256,8,128]{2,0,1:T(8,128)(2,1)}), bf16[256,8,128]{2,0,1:T(8,128)(2,1)S(1)}, u32[]{:S(2)}, u32[]{:S(2)}) async-start(bf16[256,8,128]{2,0,1:T(8,128)(2,1)} %copy.29), calls=%async_computation.3 | async-start | bytes 1048576 | tf_op jit(solution)/shard_map/all_to_all | solution.py:41
  39.4 62.3 %all-to-all-start = ((bf16[256,64,128]{2,0,1:T(8,128)(2,1)}), bf16[256,64,128]{2,0,1:T(8,128)(2,1)}, u32[]{:S(2)}, u32[]{:S(2)}) async-start(bf16[256,64,128]{2,0,1:T(8,128)(2,1)} %copy.24), calls=%async_computation | async-start | bytes 8388608 | tf_op jit(solution)/shard_map/all_to_all | solution.py:34
  44.3 51.3 %collective-permute-start = (bf16[2048,1,128]{2,0,1:T(8,128)(2,1)S(1)}, bf16[2048,1,128]{2,0,1:T(8,128)(2,1)S(1)}, u32[]{:S(2)}, u32[]{:S(2)}) collective-permute-start(bf16[2048,1,128]{2,0,1:T(8,128)(2,1)S(1)} %bitcast.79), channel_id=1, source_target_pairs={{0,1},{1,2},{2,3},{3,4},{4,5},{5,6},{6,7},{7,8},{8,9},{9,10},{10,1... | collective-permute-start | bytes 1572872 | tf_op jit(solution)/shard_map/ppermute | solution.py:12
  52.1 49.1 %collective-permute-start.1 = (bf16[2048,1,128]{2,0,1:T(8,128)(2,1)S(1)}, bf16[2048,1,128]{2,0,1:T(8,128)(2,1)S(1)}, u32[]{:S(2)}, u32[]{:S(2)}) collective-permute-start(bf16[2048,1,128]{2,0,1:T(8,128)(2,1)S(1)} %bitcast.81), channel_id=1, source_target_pairs={{0,1},{1,2},{2,3},{3,4},{4,5},{5,6},{6,7},{7,8},{8,9},{9,10},{10,1... | collective-permute-start | bytes 1572872 | tf_op jit(solution)/shard_map/ppermute | solution.py:12
  115.9 3.2 copy-start
  143.4 3.2 copy-start
  171.0 3.2 copy-start
  198.5 3.2 copy-start
  226.1 3.2 copy-start
  253.6 3.2 copy-start
  281.2 3.2 copy-start
  308.7 3.2 copy-start
where the time goes:
time: 394 us; the launch traced here: 393 us
  matrix products  123 us (31%)
  local copies, waits for them, and re-layouts  88.6 us (22%)
  waiting for transfers between devices  60 us (15%)
  blocking collectives  56.9 us (14%)
  starting transfers between devices  27.9 us (7%)
  other arithmetic  19.4 us (5%)
  loops' own time  16.6 us (4%)
    dot_general x8, matrix products, attend_blocks(): jnp.einsum('qbk,qkd->qbd', weights, picked_values, preferred_element_type...  94.3 us
    all_to_all x1, blocking collectives, on_device(): lax.all_to_all(arranged, 'heads', split_axis=0, concat_axis=1, tiled=True)  56.9 us
    ppermute x2, waiting for transfers between devices, from_behind(): return lax.ppermute(block, axis, route)  46.8 us
    dot_general x8, matrix products, attend_blocks(): jnp.einsum('qbd,qkd->qbk', query_rows, picked_keys, preferred_element_typ...  28.8 us
    gather x8, local copies, waits for them, and re-layouts, attend_blocks(): value_table[listing].reshape(members, -1, value_table.shape[-1])  24.3 us
    gather x8, local copies, waits for them, and re-layouts, attend_blocks(): picked_keys = key_table[listing].reshape(members, -1, key_table.shape[-1])  24.2 us
    sub x8, other arithmetic, attend_blocks(): powers = jnp.exp(scores - highest)  18.5 us
    another operation x1, loops' own time, on_device(): results = lax.map(one_head, jnp.arange(local_heads, dtype=jnp.int32))  16.6 us
  transfers between devices with their start and end apart: 6, of which 6 were waited for; matrix products, arithmetic and copies ran while one was open for 3% of the time, Pallas kernels for 0%

commit v1 on v0

v1 whole, which is shorter than its diff:
```python
import functools
import math

import jax
import jax.numpy as jnp
from jax import lax
from jax.experimental import pallas as pl
from jax.experimental.pallas import tpu as pltpu
from jax.sharding import PartitionSpec as P

BLOCK = 128
WIDTH = 128
SHARD_BLOCKS = 16
REMOTE = 4
LISTED = 8
KV = 8
SHARING = 8
LOCAL = 2
ROWS = LOCAL * BLOCK
PIECES = 8
CHUNKS = (3, 3, 2)
FACTOR = math.log2(math.e) / math.sqrt(WIDTH)
NT = (((1,), (1,)), ((), ()))

X_UP = [(i, (i + 2) % 8) for i in range(8)]
X_DOWN = [(i, (i - 2) % 8) for i in range(8)]
Y_SWAP = [(i, i ^ 1) for i in range(8)]


def over_heads(array, route):
    return lax.ppermute(array, "heads", route)


def split_kernel(keys, values, *rest):
    outs, wide = rest[:-1], rest[-1]
    for which, source in enumerate((keys, values)):
        wide[...] = source[...].astype(jnp.float32).reshape(ROWS * KV, WIDTH)
        head = 0
        for out in outs:
            for place in range(out.shape[1]):
                rows = wide[pl.ds(head, ROWS, stride=KV), :]
                out[which, place] = rows.astype(jnp.bfloat16)
                head += 1


def split_heads(keys, values):
    return pl.pallas_call(
        split_kernel,
        out_shape=[jax.ShapeDtypeStruct((2, size, ROWS, WIDTH), jnp.bfloat16) for size in CHUNKS],
        scratch_shapes=[pltpu.VMEM((ROWS * KV, WIDTH), jnp.float32)],
        name="split_heads",
    )(keys, values)


def pick_kernel(places, *refs):
    pieces, out, sems = refs[:PIECES], refs[PIECES], refs[PIECES + 1]
    size = out.shape[1]

    def copy(piece, head, slot, half):
        return pltpu.make_async_copy(
            piece.at[:, head, pl.ds(half * BLOCK, BLOCK), :],
            out.at[:, head, pl.ds(slot * BLOCK, BLOCK), :],
            sems.at[head, slot],
        )

    for head in range(size):
        for slot in range(REMOTE):
            place = places[head * REMOTE + slot]
            for number in range(PIECES):

                @pl.when(place // LOCAL == number)
                def _():
                    copy(pieces[number], head, slot, place % LOCAL).start()

    for head in range(size):
        for slot in range(REMOTE):
            copy(pieces[0], head, slot, 0).wait()


def pick_blocks(places, pieces):
    size = pieces[0].shape[1]
    anywhere = pl.BlockSpec(memory_space=pl.ANY)
    return pl.pallas_call(
        pick_kernel,
        out_shape=jax.ShapeDtypeStruct((2, size, REMOTE * BLOCK, WIDTH), jnp.bfloat16),
        in_specs=[pl.BlockSpec(memory_space=pltpu.SMEM)] + [anywhere] * PIECES,
        out_specs=anywhere,
        scratch_shapes=[pltpu.SemaphoreType.DMA((size, REMOTE))],
        cost_estimate=pl.CostEstimate(flops=0, bytes_accessed=size * 2**20, transcendentals=0),
        name="pick_blocks",
    )(places, *pieces)


def attend_kernel(first, aliased, slots, *refs):
    pieces, picked = refs[:PIECES], refs[PIECES]
    queries = refs[PIECES + 1]
    out, table, wide, mixed = refs[PIECES + 2 + aliased :]
    head, block = pl.program_id(0), pl.program_id(1)

    @pl.when(block == 0)
    def _():
        for number, piece in enumerate(pieces):
            table[:, pl.ds(number * ROWS, ROWS), :] = piece[:, 0]
        table[:, pl.ds(PIECES * ROWS, REMOTE * BLOCK), :] = picked[:, 0]

    wide[...] = queries[...].astype(jnp.float32).reshape(BLOCK * SHARING, WIDTH)
    base = (block * KV + first + head) * (SHARING * LISTED)

    def two(which, member, pair):
        at = [slots[base + member * LISTED + 2 * pair + i] for i in range(2)]
        return jnp.concatenate(
            [table[which, pl.ds(pl.multiple_of(s * BLOCK, BLOCK), BLOCK), :] for s in at], 0
        )

    def scores_of(member):
        rows = wide[pl.ds(member, BLOCK, stride=SHARING), :].astype(jnp.bfloat16)
        return [
            lax.dot_general(rows, two(0, member, pair), NT, preferred_element_type=jnp.float32)
            for pair in range(LISTED // 2)
        ]

    def powers_of(scores):
        highest = jnp.max(functools.reduce(jnp.maximum, scores), axis=1, keepdims=True)
        powers = [jnp.exp2((part - highest) * FACTOR) for part in scores]
        totals = jnp.sum(functools.reduce(jnp.add, powers), axis=1, keepdims=True)
        return [part.astype(jnp.bfloat16) for part in powers], totals

    def mix(member, powers, totals):
        total = jnp.zeros((BLOCK, WIDTH), jnp.float32)
        for pair in range(LISTED // 2):
            total += jnp.dot(powers[pair], two(1, member, pair), preferred_element_type=jnp.float32)
        mixed[pl.ds(member, BLOCK, stride=SHARING), :] = total * (1.0 / totals)

    scores, before = scores_of(0), None
    for member in range(SHARING):
        later = scores_of(member + 1) if member + 1 < SHARING else None
        now = powers_of(scores)
        if before is not None:
            mix(member - 1, *before)
        before, scores = now, later
    mix(SHARING - 1, *before)
    out[...] = mixed[...].reshape(BLOCK, SHARING, WIDTH).astype(jnp.bfloat16)


def attend(first, slots, pieces, picked, queries, earlier):
    size = pieces[0].shape[1]
    aliased = earlier is not None
    per_head = lambda rows: pl.BlockSpec((2, 1, rows, WIDTH), lambda head, block, _: (0, head, 0, 0))
    per_block = pl.BlockSpec(
        (BLOCK, SHARING, WIDTH), lambda head, block, _: (block, first + head, 0)
    )
    return pl.pallas_call(
        functools.partial(attend_kernel, first, aliased),
        grid_spec=pltpu.PrefetchScalarGridSpec(
            num_scalar_prefetch=1,
            grid=(size, LOCAL),
            in_specs=[per_head(ROWS)] * PIECES
            + [per_head(REMOTE * BLOCK), per_block]
            + [pl.BlockSpec(memory_space=pl.ANY)] * aliased,
            out_specs=per_block,
            scratch_shapes=[
                pltpu.VMEM((2, (SHARD_BLOCKS + REMOTE) * BLOCK, WIDTH), jnp.bfloat16),
                pltpu.VMEM((BLOCK * SHARING, WIDTH), jnp.float32),
                pltpu.VMEM((BLOCK * SHARING, WIDTH), jnp.float32),
            ],
        ),
        out_shape=jax.ShapeDtypeStruct(queries.shape, queries.dtype),
        input_output_aliases={PIECES + 3: 0} if aliased else {},
        compiler_params=pltpu.CompilerParams(vmem_limit_bytes=24 * 2**20),
        cost_estimate=pl.CostEstimate(
            flops=size * 2 * 2 * 2**30, bytes_accessed=size * 4 * 2**20, transcendentals=size * 2**21
        ),
        name=f"attend_{first}",
    )(slots, *pieces, picked, queries, *([earlier] if aliased else []))


def on_device(queries, key_states, value_states, block_lists):
    shard, member = lax.axis_index("blk"), lax.axis_index("heads")
    mine_x, mine_y = member // 2, member % 2
    own = split_heads(key_states, value_states)

    def place_of(block):
        across = (block // 4 - mine_x) % 4
        return across * 4 + ((block // 2) % 2 ^ mine_y) * 2 + block % 2

    local = (block_lists - (shard - 1) * SHARD_BLOCKS).reshape(LOCAL, KV, SHARING, LISTED)
    behind = jnp.arange(SHARD_BLOCKS, dtype=jnp.int32)
    listed = (local[..., None] == behind).any((0, 2, 3))
    rank = jnp.sum(listed[:, None, :] & (behind[None, :] < behind[:, None]), -1, dtype=jnp.int32)
    wanted = jnp.sum(
        jnp.where(
            listed[:, None, :] & (rank[:, None, :] == jnp.arange(REMOTE, dtype=jnp.int32)[:, None]),
            behind,
            0,
        ),
        -1,
        dtype=jnp.int32,
    )
    asked = lax.ppermute(wanted, "blk", [(i + 1, i) for i in range(lax.axis_size("blk") - 1)])
    ranks = jnp.sum(
        listed[None, :, None, None, :] & (behind < local[..., None]), -1, dtype=jnp.int32
    )
    slots = jnp.where(
        local >= SHARD_BLOCKS, place_of(local - SHARD_BLOCKS), SHARD_BLOCKS + ranks
    ).reshape(-1)
    places = place_of(asked).reshape(-1)
    onward = [(i, i + 1) for i in range(lax.axis_size("blk") - 1)]

    result, first = None, 0
    for a in own:
        size = a.shape[1]
        b = over_heads(a, Y_SWAP)
        a_down, a_up = over_heads(a, X_UP), over_heads(a, X_DOWN)
        b_down, b_up = over_heads(b, X_UP), over_heads(b, X_DOWN)
        a_far, b_far = over_heads(a_down, X_UP), over_heads(b_up, X_DOWN)
        pieces = [a, b, a_up, b_up, a_far, b_far, a_down, b_down]
        chosen = pick_blocks(places[first * REMOTE : (first + size) * REMOTE], pieces)
        picked = lax.ppermute(chosen, "blk", onward)
        result = attend(first, slots, pieces, picked, queries, result)
        first += size
    return result


def solution(mesh):
    spec = P(("blk", "heads"), None, None)
    return jax.shard_map(
        on_device,
        mesh=mesh,
        in_specs=(spec,) * 4,
        out_specs=spec,
        check_vma=False,
    )
```

time: 394 us -> 193 us (0.49)
  matrix products: 123 us -> 0 us
  Pallas kernels: 0 us -> 108 us
  local copies, waits for them, and re-layouts: 88.6 us -> 14.1 us
  blocking collectives: 56.9 us -> 0 us
  waiting for transfers between devices: 60 us -> 27.4 us
  loops' own time: 16.6 us -> 0 us
  other arithmetic: 19.4 us -> 7.03 us
  starting transfers between devices: 27.9 us -> 35.9 us
    dot_general x16 -> x0, matrix products: 123 us -> none  [the longest x8 94.3 us: attend_blocks(): jnp.einsum('qbk,qkd->qbd', weights, picked_values, preferred_element_type...]
    pallas_call x0 -> x7, Pallas kernels: none -> 108 us  [the longest x3 69.1 us: pick_blocks(): pl.pallas_call(pick_kernel, out_shape=jax.ShapeDtypeStruct((2, size, REMO...]
    all_to_all x1 -> x0, blocking collectives: 56.9 us -> none  [on_device(): lax.all_to_all(arranged, 'heads', split_axis=0, concat_axis=1, tiled=True)]
    gather x16 -> x0, local copies, waits for them, and re-layouts: 48.5 us -> none  [the longest x8 24.3 us: attend_blocks(): value_table[listing].reshape(members, -1, value_table.shape[-1])]
    ppermute x2 -> x25, starting transfers between devices: 8.52 us -> 35.9 us  [the longest x21 22.8 us: over_heads(): return lax.ppermute(array, 'heads', route)]
    ppermute x2 -> x25, waiting for transfers between devices: 46.8 us -> 27.4 us  [the longest x21 25.3 us: over_heads(): return lax.ppermute(array, 'heads', route)]
    all_to_all x4 -> x0, starting transfers between devices: 19.4 us -> none  [the longest x1 7.48 us: on_device(): lax.all_to_all(block_lists, 'heads', split_axis=1, concat_axis=0, tiled=T...]
    sub x9 -> x1, other arithmetic: 18.5 us -> 1.3 us  [on_device(): local - SHARD_BLOCKS]
  transfers between devices with their start and end apart: 6 -> 25, of which waited for: 6 -> 7; matrix products, arithmetic and copies ran while one was open for 3% -> 9% of each run, Pallas kernels for 0% -> 50%
where the time goes in v1:
time: 193 us
  Pallas kernels  108 us (56%)
  starting transfers between devices  35.9 us (19%)
  waiting for transfers between devices  27.4 us (14%)
  local copies, waits for them, and re-layouts  14.1 us (7%)
  other arithmetic  7.03 us (4%)
    pallas_call x3, Pallas kernels, pick_blocks(): pl.pallas_call(pick_kernel, out_shape=jax.ShapeDtypeStruct((2, size, REMO...  69.1 us
    pallas_call x3, Pallas kernels, attend(): pl.pallas_call(functools.partial(attend_kernel, first, aliased), grid_spe...  35.9 us
    ppermute x21, waiting for transfers between devices, over_heads(): return lax.ppermute(array, 'heads', route)  25.3 us
    ppermute x21, starting transfers between devices, over_heads(): return lax.ppermute(array, 'heads', route)  22.8 us
    ppermute x3, starting transfers between devices, on_device(): picked = lax.ppermute(chosen, 'blk', onward)  8.29 us
    slice x8, local copies, waits for them, and re-layouts, on_device(): chosen = pick_blocks(places[first * REMOTE:(first + size) * REMOTE], pieces)  4.91 us
    ppermute x1, starting transfers between devices, on_device(): lax.ppermute(wanted, 'blk', [(i + 1, i) for i in range(lax.axis_size('blk...  4.88 us
  transfers between devices with their start and end apart: 25, of which 7 were waited for; matrix products, arithmetic and copies ran while one was open for 9% of the time, Pallas kernels for 50%

profile of v1, /device:TPU:1, one launch (start us, length us, event | category | flops | bytes accessed | tf_op | source)
XLA Modules:
  0.0 192.6 jit_solution(13029615912972108935)
XLA Ops:
  0.0 2.6 %split_heads.1 = (bf16[2,3,256,128]{3,2,1,0:T(8,128)(2,1)}, bf16[2,3,256,128]{3,2,1,0:T(8,128)(2,1)}, bf16[2,2,256,128]{3,2,1,0:T(8,128)(2,1)}) custom-call(bf16[256,8,128]{2,1,0:T(8,128)(2,1)} %keys.1, bf16[256,8,128]{2,1,0:T(8,128)(2,1)} %values.1), custom_call_target="tpu_custom_call" | custom-call | tf_op jit(solution)/shard_map/split_heads/pallas_call | solution.py:47
  2.6 3.7 %collective-permute-start.17 = (bf16[2,3,256,128]{3,2,1,0:T(8,128)(2,1)}, bf16[2,3,256,128]{3,2,1,0:T(8,128)(2,1)S(1)}, u32[]{:S(2)}, u32[]{:S(2)}) collective-permute-start(bf16[2,3,256,128]{3,2,1,0:T(8,128)(2,1)} %get-tuple-element.10.refs_0_), channel_id=1, source_target_pairs={{0,16},{16,0},{32,48},{48,32},{64,80},{80,64},{96,112},{112,96},{1... | collective-permute-start | bytes 1179656 | tf_op jit(solution)/shard_map/ppermute | solution.py:31
  6.4 1.2 collective-permute-start.20
  7.6 0.1 collective-permute-start
  7.6 1.3 broadcast_add_fusion.1
  8.9 0.1 copy.17
  9.0 0.2 fusion
  9.3 5.9 %collective-permute-done.17.refs_1_ = bf16[2,3,256,128]{3,2,1,0:T(8,128)(2,1)S(1)} collective-permute-done((bf16[2,3,256,128]{3,2,1,0:T(8,128)(2,1)}, bf16[2,3,256,128]{3,2,1,0:T(8,128)(2,1)S(1)}, u32[]{:S(2)}, u32[]{:S(2)}) %collective-permute-start.17) | collective-permute-done | bytes 393248 | tf_op jit(solution)/shard_map/ppermute | solution.py:31
  15.1 2.5 %collective-permute-start.19 = (bf16[2,3,256,128]{3,2,1,0:T(8,128)(2,1)S(1)}, bf16[2,3,256,128]{3,2,1,0:T(8,128)(2,1)S(1)}, u32[]{:S(2)}, u32[]{:S(2)}) collective-permute-start(bf16[2,3,256,128]{3,2,1,0:T(8,128)(2,1)S(1)} %collective-permute-done.17.refs_1_), channel_id=1, source_target_pairs={{0,96},{16,112},{32,0},{48,16},{64,32},{80,48},{96,64},{112,80},{1... | collective-permute-start | bytes 1179656 | tf_op jit(solution)/shard_map/ppermute | solution.py:31
  17.6 0.2 convert_reduce_fusion.1
  17.8 0.1 select_reduce_fusion
  18.0 4.9 %collective-permute-start.7 = (s32[8,4]{0,1:T(4,128)S(1)}, s32[8,4]{0,1:T(4,128)S(1)}, u32[]{:S(2)}, u32[]{:S(2)}) collective-permute-start(s32[8,4]{0,1:T(4,128)S(1)} %select_reduce_fusion), channel_id=1, source_target_pairs={{1,0},{2,1},{3,2},{4,3},{5,4},{6,5},{7,6},{8,7},{9,8},{10,9},{11,1... | collective-permute-start | bytes 392 | tf_op jit(solution)/shard_map/ppermute | solution.py:199
  22.9 0.6 collective-permute-start.18
  23.5 2.1 %collective-permute-done.7 = s32[8,4]{0,1:T(4,128)S(1)} collective-permute-done((s32[8,4]{0,1:T(4,128)S(1)}, s32[8,4]{0,1:T(4,128)S(1)}, u32[]{:S(2)}, u32[]{:S(2)}) %collective-permute-start.7) | collective-permute-done | bytes 160 | tf_op jit(solution)/shard_map/ppermute | solution.py:199
  25.6 2.6 %collective-permute-start.9 = (bf16[2,3,256,128]{3,2,1,0:T(8,128)(2,1)}, bf16[2,3,256,128]{3,2,1,0:T(8,128)(2,1)S(1)}, u32[]{:S(2)}, u32[]{:S(2)}) collective-permute-start(bf16[2,3,256,128]{3,2,1,0:T(8,128)(2,1)} %get-tuple-element.9.refs_0_), channel_id=1, source_target_pairs={{0,16},{16,0},{32,48},{48,32},{64,80},{80,64},{96,112},{112,96},{1... | collective-permute-start | bytes 1179656 | tf_op jit(solution)/shard_map/ppermute | solution.py:31
  28.2 0.0 collective-permute-start.23
  28.2 0.0 collective-permute-done.20.refs_6_
  28.3 0.2 collective-permute-start.21
  28.4 0.0 collective-permute-done.19.refs_3_
  28.4 2.6 %collective-permute-start.22 = (bf16[2,3,256,128]{3,2,1,0:T(8,128)(2,1)S(1)}, bf16[2,3,256,128]{3,2,1,0:T(8,128)(2,1)S(1)}, u32[]{:S(2)}, u32[]{:S(2)}) collective-permute-start(bf16[2,3,256,128]{3,2,1,0:T(8,128)(2,1)S(1)} %collective-permute-done.19.refs_3_), channel_id=1, source_target_pairs={{0,96},{16,112},{32,0},{48,16},{64,32},{80,48},{96,64},{112,80},{1... | collective-permute-start | bytes 1179656 | tf_op jit(solution)/shard_map/ppermute | solution.py:31
  31.0 3.3 %collective-permute-done.18.refs_2_ = bf16[2,3,256,128]{3,2,1,0:T(8,128)(2,1)S(1)} collective-permute-done((bf16[2,3,256,128]{3,2,1,0:T(8,128)(2,1)}, bf16[2,3,256,128]{3,2,1,0:T(8,128)(2,1)S(1)}, u32[]{:S(2)}, u32[]{:S(2)}) %collective-permute-start.18) | collective-permute-done | bytes 393248 | tf_op jit(solution)/shard_map/ppermute | solution.py:31
  34.4 2.7 %collective-permute-done.9.refs_1_ = bf16[2,3,256,128]{3,2,1,0:T(8,128)(2,1)S(1)} collective-permute-done((bf16[2,3,256,128]{3,2,1,0:T(8,128)(2,1)}, bf16[2,3,256,128]{3,2,1,0:T(8,128)(2,1)S(1)}, u32[]{:S(2)}, u32[]{:S(2)}) %collective-permute-start.9) | collective-permute-done | bytes 393248 | tf_op jit(solution)/shard_map/ppermute | solution.py:31
  37.0 0.3 collective-permute-start.3
  37.3 3.2 %collective-permute-done.23.refs_7_ = bf16[2,3,256,128]{3,2,1,0:T(8,128)(2,1)S(1)} collective-permute-done((bf16[2,3,256,128]{3,2,1,0:T(8,128)(2,1)S(1)}, bf16[2,3,256,128]{3,2,1,0:T(8,128)(2,1)S(1)}, u32[]{:S(2)}, u32[]{:S(2)}) %collective-permute-start.23) | collective-permute-done | bytes 393248 | tf_op jit(solution)/shard_map/ppermute | solution.py:31
  40.5 0.0 collective-permute-start.1
  40.5 8.5 %collective-permute-done.21.refs_4_ = bf16[2,3,256,128]{3,2,1,0:T(8,128)(2,1)S(1)} collective-permute-done((bf16[2,3,256,128]{3,2,1,0:T(8,128)(2,1)S(1)}, bf16[2,3,256,128]{3,2,1,0:T(8,128)(2,1)S(1)}, u32[]{:S(2)}, u32[]{:S(2)}) %collective-permute-start.21) | collective-permute-done | bytes 393248 | tf_op jit(solution)/shard_map/ppermute | solution.py:31
  49.1 0.1 collective-permute-start.11
  49.2 0.5 copy-done.22
  49.7 0.7 fusion.23
  50.4 0.8 copy.16
  51.1 0.6 slice.23.places
  51.8 25.7 %pick_blocks.5 = bf16[2,3,512,128]{3,2,1,0:T(8,128)(2,1)} custom-call(s32[12]{0:T(128)} %slice.23.places, bf16[2,3,256,128]{3,2,1,0:T(8,128)(2,1)} %get-tuple-element.10.refs_0_, bf16[2,3,256,128]{3,2,1,0:T(8,128)(2,1)} %copy-done.3, bf16[2,3,256,128]{3,2,1,0:T(8,128)(2,1)} %copy-done.11, bf16[2,3,256,128]{3,2,1,0:T(8,128)(2,1)} %copy-done.7, ...), custom_call_target="tpu_custom_call" | custom-call | bytes 3145728 | tf_op jit(solution)/shard_map/pick_blocks/pallas_call | solution.py:83
  77.6 1.5 collective-permute-start.6
  79.1 1.0 collective-permute-start.4
  80.1 1.7 collective-permute-start.5
  81.8 2.4 %collective-permute-start.24 = (bf16[2,3,512,128]{3,2,1,0:T(8,128)(2,1)}, bf16[2,3,512,128]{3,2,1,0:T(8,128)(2,1)}, u32[]{:S(2)}, u32[]{:S(2)}) collective-permute-start(bf16[2,3,512,128]{3,2,1,0:T(8,128)(2,1)} %pick_blocks.5), channel_id=1, source_target_pairs={{0,1},{1,2},{2,3},{3,4},{4,5},{5,6},{6,7},{7,8},{8,9},{9,10},{10,1... | collective-permute-start | bytes 2359304 | tf_op jit(solution)/shard_map/ppermute | solution.py:218
  84.2 3.2 %convert_reduce_fusion = s32[2,8,8,8]{3,2,1,0:T(8,128)S(1)} fusion(s32[2,8,8,8]{3,2,1,0:T(8,128)} %bitcast.4, pred[8,16]{1,0:T(8,128)(4,1)S(1)} %fusion), kind=kLoop, calls=%fused_computation | loop fusion | flops 64512 | bytes 8320 | tf_op jit(solution)/shard_map/reduce_sum | solution.py:200
  87.4 0.6 broadcast_add_fusion
  88.0 1.5 add.74
  89.6 1.7 collective-permute-start.10
  91.2 1.7 collective-permute-done.4.refs_4_
  92.9 0.4 collective-permute-start.15
  93.3 0.8 collective-permute-start.13
  94.0 1.9 collective-permute-start.14
  96.0 0.6 broadcast_compare_fusion
  96.5 0.8 copy.11
  97.3 0.7 ge.8
  98.0 1.4 copy.12
  99.4 0.9 sub.55
  100.3 0.7 fusion.9.slots
  101.0 0.7 slice.18
  101.8 0.8 copy.15
  102.5 0.6 slice.21.places
  103.2 0.1 copy.14
  103.3 0.6 slice.19.places
  103.9 17.7 %pick_blocks.3 = bf16[2,2,512,128]{3,2,1,0:T(8,128)(2,1)} custom-call(s32[8]{0:T(128)} %slice.19.places, bf16[2,2,256,128]{3,2,1,0:T(8,128)(2,1)} %get-tuple-element.8.refs_0_, bf16[2,2,256,128]{3,2,1,0:T(8,128)(2,1)} %collective-permute-done.refs_1_, bf16[2,2,256,128]{3,2,1,0:T(8,128)(2,1)} %collective-permute-done.1.refs_2_, ...), custom_call_target="tpu_custom_call" | custom-call | bytes 2097152 | tf_op jit(solution)/shard_map/pick_blocks/pallas_call | solution.py:83
  121.6 3.8 %collective-permute-start.8 = (bf16[2,2,512,128]{3,2,1,0:T(8,128)(2,1)}, bf16[2,2,512,128]{3,2,1,0:T(8,128)(2,1)}, u32[]{:S(2)}, u32[]{:S(2)}) collective-permute-start(bf16[2,2,512,128]{3,2,1,0:T(8,128)(2,1)} %pick_blocks.3), channel_id=1, source_target_pairs={{0,1},{1,2},{2,3},{3,4},{4,5},{5,6},{6,7},{7,8},{8,9},{9,10},{10,1... | collective-permute-start | bytes 1572872 | tf_op jit(solution)/shard_map/ppermute | solution.py:218
  125.5 25.7 %pick_blocks.4 = bf16[2,3,512,128]{3,2,1,0:T(8,128)(2,1)} custom-call(s32[12]{0:T(128)} %slice.21.places, bf16[2,3,256,128]{3,2,1,0:T(8,128)(2,1)} %get-tuple-element.9.refs_0_, bf16[2,3,256,128]{3,2,1,0:T(8,128)(2,1)} %copy-done.9, bf16[2,3,256,128]{3,2,1,0:T(8,128)(2,1)} %collective-permute-done.10.refs_2_, ...), custom_call_target="tpu_custom_call" | custom-call | bytes 3145728 | tf_op jit(solution)/shard_map/pick_blocks/pallas_call | solution.py:83
  151.3 2.1 %collective-permute-start.16 = (bf16[2,3,512,128]{3,2,1,0:T(8,128)(2,1)}, bf16[2,3,512,128]{3,2,1,0:T(8,128)(2,1)S(1)}, u32[]{:S(2)}, u32[]{:S(2)}) collective-permute-start(bf16[2,3,512,128]{3,2,1,0:T(8,128)(2,1)} %pick_blocks.4), channel_id=1, source_target_pairs={{0,1},{1,2},{2,3},{3,4},{4,5},{5,6},{6,7},{7,8},{8,9},{9,10},{10,1... | collective-permute-start | bytes 2359304 | tf_op jit(solution)/shard_map/ppermute | solution.py:218
  153.4 1.0 copy-done.18
  154.4 2.2 %copy-done.20 = bf16[256,64,128]{2,1,0:T(8,128)(2,1)S(1)} copy-done((bf16[256,64,128]{2,1,0:T(8,128)(2,1)S(1)}, bf16[256,64,128]{2,1,0:T(8,128)(2,1)}, u32[]{:S(2)}) %copy-start.20) | copy-done | bytes 4194328
  156.6 13.0 %attend_0.1.refs_10_ = bf16[256,64,128]{2,1,0:T(8,128)(2,1)} custom-call(s32[1024]{0:T(1024)S(1)} %fusion.9.slots, bf16[2,3,256,128]{3,2,1,0:T(8,128)(2,1)S(1)} %copy-done.2, bf16[2,3,256,128]{3,2,1,0:T(8,128)(2,1)S(1)} %copy-done.4, bf16[2,3,256,128]{3,2,1,0:T(8,128)(2,1)S(1)} %copy-done.12, bf16[2,3,256,128]{3,2,1,0:T(8,128)(2,1)S(1)} %copy-done.8, ...), custom_call_target="tpu_custom_call" | custom-call | flops 12884901888 | bytes 12582912 | tf_op jit(solution)/shard_map/attend_0/pallas_call | solution.py:152
  169.6 13.2 %attend_3.1.refs_10_ = bf16[256,64,128]{2,1,0:T(8,128)(2,1)} custom-call(s32[1024]{0:T(1024)S(1)} %fusion.9.slots, bf16[2,3,256,128]{3,2,1,0:T(8,128)(2,1)S(1)} %copy-done.1, bf16[2,3,256,128]{3,2,1,0:T(8,128)(2,1)S(1)} %copy-done.10, bf16[2,3,256,128]{3,2,1,0:T(8,128)(2,1)} %collective-permute-done.10.refs_2_, ...), custom_call_target="tpu_custom_call", output_to_operand_aliasing={{}: (11, {})} | custom-call | flops 12884901888 | bytes 12582912 | tf_op jit(solution)/shard_map/attend_3/pallas_call | solution.py:152
  182.9 9.7 %attend_6.1 = bf16[256,64,128]{2,1,0:T(8,128)(2,1)} custom-call(s32[1024]{0:T(1024)S(1)} %fusion.9.slots, bf16[2,2,256,128]{3,2,1,0:T(8,128)(2,1)S(1)} %copy-done.19, bf16[2,2,256,128]{3,2,1,0:T(8,128)(2,1)} %collective-permute-done.refs_1_, bf16[2,2,256,128]{3,2,1,0:T(8,128)(2,1)} %collective-permute-done.1.refs_2_, ...), custom_call_target="tpu_custom_call", output_to_operand_aliasing={{}: (11, {})} | custom-call | flops 8589934592 | bytes 8388608 | tf_op jit(solution)/shard_map/attend_6/pallas_call | solution.py:152
  (63 shorter events, 0.2 us)
Async XLA Ops:
  2.6 86.9 %copy-start = (bf16[2,3,256,128]{3,2,1,0:T(8,128)(2,1)S(1)}, bf16[2,3,256,128]{3,2,1,0:T(8,128)(2,1)}, u32[]{:S(2)}) copy-start(bf16[2,3,256,128]{3,2,1,0:T(8,128)(2,1)} %get-tuple-element.9.refs_0_) | copy-start | bytes 1179652
  2.6 12.5 %collective-permute-start.17 = (bf16[2,3,256,128]{3,2,1,0:T(8,128)(2,1)}, bf16[2,3,256,128]{3,2,1,0:T(8,128)(2,1)S(1)}, u32[]{:S(2)}, u32[]{:S(2)}) collective-permute-start(bf16[2,3,256,128]{3,2,1,0:T(8,128)(2,1)} %get-tuple-element.10.refs_0_), channel_id=1, source_target_pairs={{0,16},{16,0},{32,48},{48,32},{64,80},{80,64},{96,112},{112,96},{1... | collective-permute-start | bytes 1179656 | tf_op jit(solution)/shard_map/ppermute | solution.py:31
  6.4 21.9 %collective-permute-start.20 = (bf16[2,3,256,128]{3,2,1,0:T(8,128)(2,1)}, bf16[2,3,256,128]{3,2,1,0:T(8,128)(2,1)S(1)}, u32[]{:S(2)}, u32[]{:S(2)}) collective-permute-start(bf16[2,3,256,128]{3,2,1,0:T(8,128)(2,1)} %get-tuple-element.10.refs_0_), channel_id=1, source_target_pairs={{0,32},{16,48},{32,64},{48,80},{64,96},{80,112},{96,0},{112,16},{1... | collective-permute-start | bytes 1179656 | tf_op jit(solution)/shard_map/ppermute | solution.py:31
  7.6 20.7 %collective-permute-start = (bf16[2,2,256,128]{3,2,1,0:T(8,128)(2,1)}, bf16[2,2,256,128]{3,2,1,0:T(8,128)(2,1)}, u32[]{:S(2)}, u32[]{:S(2)}) collective-permute-start(bf16[2,2,256,128]{3,2,1,0:T(8,128)(2,1)} %get-tuple-element.8.refs_0_), channel_id=1, source_target_pairs={{0,16},{16,0},{32,48},{48,32},{64,80},{80,64},{96,112},{112,96},{1... | collective-permute-start | bytes 786440 | tf_op jit(solution)/shard_map/ppermute | solution.py:31
  9.0 16.6 %copy-start.21 = (s32[2,64,8]{2,1,0:T(8,128)}, s32[2,64,8]{2,1,0:T(8,128)S(1)}, u32[]{:S(2)}) copy-start(s32[2,64,8]{2,1,0:T(8,128)S(1)} %copy.17) | copy-start | bytes 12292
  15.1 36.6 %copy-start.3 = (bf16[2,3,256,128]{3,2,1,0:T(8,128)(2,1)}, bf16[2,3,256,128]{3,2,1,0:T(8,128)(2,1)S(1)}, u32[]{:S(2)}) copy-start(bf16[2,3,256,128]{3,2,1,0:T(8,128)(2,1)S(1)} %collective-permute-done.17.refs_1_) | copy-start | bytes 1179652
  15.1 13.3 %collective-permute-start.19 = (bf16[2,3,256,128]{3,2,1,0:T(8,128)(2,1)S(1)}, bf16[2,3,256,128]{3,2,1,0:T(8,128)(2,1)S(1)}, u32[]{:S(2)}, u32[]{:S(2)}) collective-permute-start(bf16[2,3,256,128]{3,2,1,0:T(8,128)(2,1)S(1)} %collective-permute-done.17.refs_1_), channel_id=1, source_target_pairs={{0,96},{16,112},{32,0},{48,16},{64,32},{80,48},{96,64},{112,80},{1... | collective-permute-start | bytes 1179656 | tf_op jit(solution)/shard_map/ppermute | solution.py:31
  18.0 7.6 %collective-permute-start.7 = (s32[8,4]{0,1:T(4,128)S(1)}, s32[8,4]{0,1:T(4,128)S(1)}, u32[]{:S(2)}, u32[]{:S(2)}) collective-permute-start(s32[8,4]{0,1:T(4,128)S(1)} %select_reduce_fusion), channel_id=1, source_target_pairs={{1,0},{2,1},{3,2},{4,3},{5,4},{6,5},{7,6},{8,7},{9,8},{10,9},{11,1... | collective-permute-start | bytes 392 | tf_op jit(solution)/shard_map/ppermute | solution.py:199
  22.9 11.5 %collective-permute-start.18 = (bf16[2,3,256,128]{3,2,1,0:T(8,128)(2,1)}, bf16[2,3,256,128]{3,2,1,0:T(8,128)(2,1)S(1)}, u32[]{:S(2)}, u32[]{:S(2)}) collective-permute-start(bf16[2,3,256,128]{3,2,1,0:T(8,128)(2,1)} %get-tuple-element.10.refs_0_), channel_id=1, source_target_pairs={{0,96},{16,112},{32,0},{48,16},{64,32},{80,48},{96,64},{112,80},{1... | collective-permute-start | bytes 1179656 | tf_op jit(solution)/shard_map/ppermute | solution.py:31
  25.6 11.4 %collective-permute-start.9 = (bf16[2,3,256,128]{3,2,1,0:T(8,128)(2,1)}, bf16[2,3,256,128]{3,2,1,0:T(8,128)(2,1)S(1)}, u32[]{:S(2)}, u32[]{:S(2)}) collective-permute-start(bf16[2,3,256,128]{3,2,1,0:T(8,128)(2,1)} %get-tuple-element.9.refs_0_), channel_id=1, source_target_pairs={{0,16},{16,0},{32,48},{48,32},{64,80},{80,64},{96,112},{112,96},{1... | collective-permute-start | bytes 1179656 | tf_op jit(solution)/shard_map/ppermute | solution.py:31
  28.2 12.3 %collective-permute-start.23 = (bf16[2,3,256,128]{3,2,1,0:T(8,128)(2,1)S(1)}, bf16[2,3,256,128]{3,2,1,0:T(8,128)(2,1)S(1)}, u32[]{:S(2)}, u32[]{:S(2)}) collective-permute-start(bf16[2,3,256,128]{3,2,1,0:T(8,128)(2,1)S(1)} %collective-permute-done.17.refs_1_), channel_id=1, source_target_pairs={{0,32},{16,48},{32,64},{48,80},{64,96},{80,112},{96,0},{112,16},{1... | collective-permute-start | bytes 1179656 | tf_op jit(solution)/shard_map/ppermute | solution.py:31
  28.2 23.5 %copy-start.5 = (bf16[2,3,256,128]{3,2,1,0:T(8,128)(2,1)}, bf16[2,3,256,128]{3,2,1,0:T(8,128)(2,1)S(1)}, u32[]{:S(2)}) copy-start(bf16[2,3,256,128]{3,2,1,0:T(8,128)(2,1)S(1)} %collective-permute-done.20.refs_6_) | copy-start | bytes 1179652
  28.3 20.8 %collective-permute-start.21 = (bf16[2,3,256,128]{3,2,1,0:T(8,128)(2,1)S(1)}, bf16[2,3,256,128]{3,2,1,0:T(8,128)(2,1)S(1)}, u32[]{:S(2)}, u32[]{:S(2)}) collective-permute-start(bf16[2,3,256,128]{3,2,1,0:T(8,128)(2,1)S(1)} %collective-permute-done.20.refs_6_), channel_id=1, source_target_pairs={{0,32},{16,48},{32,64},{48,80},{64,96},{80,112},{96,0},{112,16},{1... | collective-permute-start | bytes 1179656 | tf_op jit(solution)/shard_map/ppermute | solution.py:31
  28.4 23.3 %copy-start.7 = (bf16[2,3,256,128]{3,2,1,0:T(8,128)(2,1)}, bf16[2,3,256,128]{3,2,1,0:T(8,128)(2,1)S(1)}, u32[]{:S(2)}) copy-start(bf16[2,3,256,128]{3,2,1,0:T(8,128)(2,1)S(1)} %collective-permute-done.19.refs_3_) | copy-start | bytes 1179652
  28.4 20.6 %collective-permute-start.22 = (bf16[2,3,256,128]{3,2,1,0:T(8,128)(2,1)S(1)}, bf16[2,3,256,128]{3,2,1,0:T(8,128)(2,1)S(1)}, u32[]{:S(2)}, u32[]{:S(2)}) collective-permute-start(bf16[2,3,256,128]{3,2,1,0:T(8,128)(2,1)S(1)} %collective-permute-done.19.refs_3_), channel_id=1, source_target_pairs={{0,96},{16,112},{32,0},{48,16},{64,32},{80,48},{96,64},{112,80},{1... | collective-permute-start | bytes 1179656 | tf_op jit(solution)/shard_map/ppermute | solution.py:31
  34.4 17.4 %copy-start.11 = (bf16[2,3,256,128]{3,2,1,0:T(8,128)(2,1)}, bf16[2,3,256,128]{3,2,1,0:T(8,128)(2,1)S(1)}, u32[]{:S(2)}) copy-start(bf16[2,3,256,128]{3,2,1,0:T(8,128)(2,1)S(1)} %collective-permute-done.18.refs_2_) | copy-start | bytes 1179652
  34.4 47.4 %collective-permute-start.12 = (bf16[2,3,256,128]{3,2,1,0:T(8,128)(2,1)}, bf16[2,3,256,128]{3,2,1,0:T(8,128)(2,1)}, u32[]{:S(2)}, u32[]{:S(2)}) collective-permute-start(bf16[2,3,256,128]{3,2,1,0:T(8,128)(2,1)} %get-tuple-element.9.refs_0_), channel_id=1, source_target_pairs={{0,32},{16,48},{32,64},{48,80},{64,96},{80,112},{96,0},{112,16},{1... | collective-permute-start | bytes 1179656 | tf_op jit(solution)/shard_map/ppermute | solution.py:31
  37.0 88.5 %copy-start.9 = (bf16[2,3,256,128]{3,2,1,0:T(8,128)(2,1)}, bf16[2,3,256,128]{3,2,1,0:T(8,128)(2,1)S(1)}, u32[]{:S(2)}) copy-start(bf16[2,3,256,128]{3,2,1,0:T(8,128)(2,1)S(1)} %collective-permute-done.9.refs_1_) | copy-start | bytes 1179652
  37.0 40.6 %collective-permute-start.3 = (bf16[2,2,256,128]{3,2,1,0:T(8,128)(2,1)}, bf16[2,2,256,128]{3,2,1,0:T(8,128)(2,1)}, u32[]{:S(2)}, u32[]{:S(2)}) collective-permute-start(bf16[2,2,256,128]{3,2,1,0:T(8,128)(2,1)} %get-tuple-element.8.refs_0_), channel_id=1, source_target_pairs={{0,32},{16,48},{32,64},{48,80},{64,96},{80,112},{96,0},{112,16},{1... | collective-permute-start | bytes 786440 | tf_op jit(solution)/shard_map/ppermute | solution.py:31
  40.5 11.3 %copy-start.13 = (bf16[2,3,256,128]{3,2,1,0:T(8,128)(2,1)}, bf16[2,3,256,128]{3,2,1,0:T(8,128)(2,1)S(1)}, u32[]{:S(2)}) copy-start(bf16[2,3,256,128]{3,2,1,0:T(8,128)(2,1)S(1)} %collective-permute-done.23.refs_7_) | copy-start | bytes 1179652
  40.5 38.6 %collective-permute-start.1 = (bf16[2,2,256,128]{3,2,1,0:T(8,128)(2,1)}, bf16[2,2,256,128]{3,2,1,0:T(8,128)(2,1)}, u32[]{:S(2)}, u32[]{:S(2)}) collective-permute-start(bf16[2,2,256,128]{3,2,1,0:T(8,128)(2,1)} %get-tuple-element.8.refs_0_), channel_id=1, source_target_pairs={{0,96},{16,112},{32,0},{48,16},{64,32},{80,48},{96,64},{112,80},{1... | collective-permute-start | bytes 786440 | tf_op jit(solution)/shard_map/ppermute | solution.py:31
  49.0 2.7 %copy-start.15 = (bf16[2,3,256,128]{3,2,1,0:T(8,128)(2,1)}, bf16[2,3,256,128]{3,2,1,0:T(8,128)(2,1)S(1)}, u32[]{:S(2)}) copy-start(bf16[2,3,256,128]{3,2,1,0:T(8,128)(2,1)S(1)} %collective-permute-done.21.refs_4_) | copy-start | bytes 1179652
  49.0 31.0 %collective-permute-start.2 = (bf16[2,2,256,128]{3,2,1,0:T(8,128)(2,1)}, bf16[2,2,256,128]{3,2,1,0:T(8,128)(2,1)}, u32[]{:S(2)}, u32[]{:S(2)}) collective-permute-start(bf16[2,2,256,128]{3,2,1,0:T(8,128)(2,1)} %collective-permute-done.refs_1_), channel_id=1, source_target_pairs={{0,96},{16,112},{32,0},{48,16},{64,32},{80,48},{96,64},{112,80},{1... | collective-permute-start | bytes 786440 | tf_op jit(solution)/shard_map/ppermute | solution.py:31
  49.1 0.6 copy-start.22
  49.1 2.7 %copy-start.17 = (bf16[2,3,256,128]{3,2,1,0:T(8,128)(2,1)}, bf16[2,3,256,128]{3,2,1,0:T(8,128)(2,1)S(1)}, u32[]{:S(2)}) copy-start(bf16[2,3,256,128]{3,2,1,0:T(8,128)(2,1)S(1)} %collective-permute-done.22.refs_5_) | copy-start | bytes 1179652
  49.1 44.9 %collective-permute-start.11 = (bf16[2,3,256,128]{3,2,1,0:T(8,128)(2,1)S(1)}, bf16[2,3,256,128]{3,2,1,0:T(8,128)(2,1)}, u32[]{:S(2)}, u32[]{:S(2)}) collective-permute-start(bf16[2,3,256,128]{3,2,1,0:T(8,128)(2,1)S(1)} %collective-permute-done.9.refs_1_), channel_id=1, source_target_pairs={{0,96},{16,112},{32,0},{48,16},{64,32},{80,48},{96,64},{112,80},{1... | collective-permute-start | bytes 1179656 | tf_op jit(solution)/shard_map/ppermute | solution.py:31
  77.5 75.8 %copy-start.2 = (bf16[2,3,256,128]{3,2,1,0:T(8,128)(2,1)S(1)}, bf16[2,3,256,128]{3,2,1,0:T(8,128)(2,1)}, u32[]{:S(2)}) copy-start(bf16[2,3,256,128]{3,2,1,0:T(8,128)(2,1)} %get-tuple-element.10.refs_0_) | copy-start | bytes 1179652
  77.5 75.8 %copy-start.4 = (bf16[2,3,256,128]{3,2,1,0:T(8,128)(2,1)S(1)}, bf16[2,3,256,128]{3,2,1,0:T(8,128)(2,1)}, u32[]{:S(2)}) copy-start(bf16[2,3,256,128]{3,2,1,0:T(8,128)(2,1)} %copy-done.3) | copy-start | bytes 1179652
  77.5 75.8 %copy-start.6 = (bf16[2,3,256,128]{3,2,1,0:T(8,128)(2,1)S(1)}, bf16[2,3,256,128]{3,2,1,0:T(8,128)(2,1)}, u32[]{:S(2)}) copy-start(bf16[2,3,256,128]{3,2,1,0:T(8,128)(2,1)} %copy-done.5) | copy-start | bytes 1179652
  77.6 75.8 %copy-start.8 = (bf16[2,3,256,128]{3,2,1,0:T(8,128)(2,1)S(1)}, bf16[2,3,256,128]{3,2,1,0:T(8,128)(2,1)}, u32[]{:S(2)}) copy-start(bf16[2,3,256,128]{3,2,1,0:T(8,128)(2,1)} %copy-done.7) | copy-start | bytes 1179652
  77.6 75.8 %copy-start.12 = (bf16[2,3,256,128]{3,2,1,0:T(8,128)(2,1)S(1)}, bf16[2,3,256,128]{3,2,1,0:T(8,128)(2,1)}, u32[]{:S(2)}) copy-start(bf16[2,3,256,128]{3,2,1,0:T(8,128)(2,1)} %copy-done.11) | copy-start | bytes 1179652
  77.6 75.8 %copy-start.14 = (bf16[2,3,256,128]{3,2,1,0:T(8,128)(2,1)S(1)}, bf16[2,3,256,128]{3,2,1,0:T(8,128)(2,1)}, u32[]{:S(2)}) copy-start(bf16[2,3,256,128]{3,2,1,0:T(8,128)(2,1)} %copy-done.13) | copy-start | bytes 1179652
  77.6 75.8 %copy-start.16 = (bf16[2,3,256,128]{3,2,1,0:T(8,128)(2,1)S(1)}, bf16[2,3,256,128]{3,2,1,0:T(8,128)(2,1)}, u32[]{:S(2)}) copy-start(bf16[2,3,256,128]{3,2,1,0:T(8,128)(2,1)} %copy-done.15) | copy-start | bytes 1179652
  77.6 11.9 %collective-permute-start.6 = (bf16[2,2,256,128]{3,2,1,0:T(8,128)(2,1)}, bf16[2,2,256,128]{3,2,1,0:T(8,128)(2,1)}, u32[]{:S(2)}, u32[]{:S(2)}) collective-permute-start(bf16[2,2,256,128]{3,2,1,0:T(8,128)(2,1)} %collective-permute-done.refs_1_), channel_id=1, source_target_pairs={{0,32},{16,48},{32,64},{48,80},{64,96},{80,112},{96,0},{112,16},{1... | collective-permute-start | bytes 786440 | tf_op jit(solution)/shard_map/ppermute | solution.py:31
  79.1 13.8 %collective-permute-start.4 = (bf16[2,2,256,128]{3,2,1,0:T(8,128)(2,1)}, bf16[2,2,256,128]{3,2,1,0:T(8,128)(2,1)}, u32[]{:S(2)}, u32[]{:S(2)}) collective-permute-start(bf16[2,2,256,128]{3,2,1,0:T(8,128)(2,1)} %collective-permute-done.3.refs_6_), channel_id=1, source_target_pairs={{0,32},{16,48},{32,64},{48,80},{64,96},{80,112},{96,0},{112,16},{1... | collective-permute-start | bytes 786440 | tf_op jit(solution)/shard_map/ppermute | solution.py:31
  80.1 13.2 %collective-permute-start.5 = (bf16[2,2,256,128]{3,2,1,0:T(8,128)(2,1)}, bf16[2,2,256,128]{3,2,1,0:T(8,128)(2,1)}, u32[]{:S(2)}, u32[]{:S(2)}) collective-permute-start(bf16[2,2,256,128]{3,2,1,0:T(8,128)(2,1)} %collective-permute-done.2.refs_3_), channel_id=1, source_target_pairs={{0,96},{16,112},{32,0},{48,16},{64,32},{80,48},{96,64},{112,80},{1... | collective-permute-start | bytes 786440 | tf_op jit(solution)/shard_map/ppermute | solution.py:31
  81.8 71.6 %collective-permute-start.24 = (bf16[2,3,512,128]{3,2,1,0:T(8,128)(2,1)}, bf16[2,3,512,128]{3,2,1,0:T(8,128)(2,1)}, u32[]{:S(2)}, u32[]{:S(2)}) collective-permute-start(bf16[2,3,512,128]{3,2,1,0:T(8,128)(2,1)} %pick_blocks.5), channel_id=1, source_target_pairs={{0,1},{1,2},{2,3},{3,4},{4,5},{5,6},{6,7},{7,8},{8,9},{9,10},{10,1... | collective-permute-start | bytes 2359304 | tf_op jit(solution)/shard_map/ppermute | solution.py:218
  89.6 32.1 %collective-permute-start.10 = (bf16[2,3,256,128]{3,2,1,0:T(8,128)(2,1)S(1)}, bf16[2,3,256,128]{3,2,1,0:T(8,128)(2,1)}, u32[]{:S(2)}, u32[]{:S(2)}) collective-permute-start(bf16[2,3,256,128]{3,2,1,0:T(8,128)(2,1)S(1)} %copy-done), channel_id=1, source_target_pairs={{0,96},{16,112},{32,0},{48,16},{64,32},{80,48},{96,64},{112,80},{1... | collective-permute-start | bytes 1179656 | tf_op jit(solution)/shard_map/ppermute | solution.py:31
  92.9 32.6 %collective-permute-start.15 = (bf16[2,3,256,128]{3,2,1,0:T(8,128)(2,1)S(1)}, bf16[2,3,256,128]{3,2,1,0:T(8,128)(2,1)}, u32[]{:S(2)}, u32[]{:S(2)}) collective-permute-start(bf16[2,3,256,128]{3,2,1,0:T(8,128)(2,1)S(1)} %collective-permute-done.9.refs_1_), channel_id=1, source_target_pairs={{0,32},{16,48},{32,64},{48,80},{64,96},{80,112},{96,0},{112,16},{1... | collective-permute-start | bytes 1179656 | tf_op jit(solution)/shard_map/ppermute | solution.py:31
  93.3 32.2 %collective-permute-start.13 = (bf16[2,3,256,128]{3,2,1,0:T(8,128)(2,1)}, bf16[2,3,256,128]{3,2,1,0:T(8,128)(2,1)}, u32[]{:S(2)}, u32[]{:S(2)}) collective-permute-start(bf16[2,3,256,128]{3,2,1,0:T(8,128)(2,1)} %collective-permute-done.12.refs_6_), channel_id=1, source_target_pairs={{0,32},{16,48},{32,64},{48,80},{64,96},{80,112},{96,0},{112,16},{1... | collective-permute-start | bytes 1179656 | tf_op jit(solution)/shard_map/ppermute | solution.py:31
  94.0 31.5 %collective-permute-start.14 = (bf16[2,3,256,128]{3,2,1,0:T(8,128)(2,1)}, bf16[2,3,256,128]{3,2,1,0:T(8,128)(2,1)}, u32[]{:S(2)}, u32[]{:S(2)}) collective-permute-start(bf16[2,3,256,128]{3,2,1,0:T(8,128)(2,1)} %collective-permute-done.11.refs_3_), channel_id=1, source_target_pairs={{0,96},{16,112},{32,0},{48,16},{64,32},{80,48},{96,64},{112,80},{1... | collective-permute-start | bytes 1179656 | tf_op jit(solution)/shard_map/ppermute | solution.py:31
  121.6 61.2 %collective-permute-start.8 = (bf16[2,2,512,128]{3,2,1,0:T(8,128)(2,1)}, bf16[2,2,512,128]{3,2,1,0:T(8,128)(2,1)}, u32[]{:S(2)}, u32[]{:S(2)}) collective-permute-start(bf16[2,2,512,128]{3,2,1,0:T(8,128)(2,1)} %pick_blocks.3), channel_id=1, source_target_pairs={{0,1},{1,2},{2,3},{3,4},{4,5},{5,6},{6,7},{7,8},{8,9},{9,10},{10,1... | collective-permute-start | bytes 1572872 | tf_op jit(solution)/shard_map/ppermute | solution.py:218
  151.2 18.4 %copy-start.1 = (bf16[2,3,256,128]{3,2,1,0:T(8,128)(2,1)S(1)}, bf16[2,3,256,128]{3,2,1,0:T(8,128)(2,1)}, u32[]{:S(2)}) copy-start(bf16[2,3,256,128]{3,2,1,0:T(8,128)(2,1)} %get-tuple-element.9.refs_0_) | copy-start | bytes 1179652
  151.3 18.4 %copy-start.10 = (bf16[2,3,256,128]{3,2,1,0:T(8,128)(2,1)S(1)}, bf16[2,3,256,128]{3,2,1,0:T(8,128)(2,1)}, u32[]{:S(2)}) copy-start(bf16[2,3,256,128]{3,2,1,0:T(8,128)(2,1)} %copy-done.9) | copy-start | bytes 1179652
  151.3 18.4 %collective-permute-start.16 = (bf16[2,3,512,128]{3,2,1,0:T(8,128)(2,1)}, bf16[2,3,512,128]{3,2,1,0:T(8,128)(2,1)S(1)}, u32[]{:S(2)}, u32[]{:S(2)}) collective-permute-start(bf16[2,3,512,128]{3,2,1,0:T(8,128)(2,1)} %pick_blocks.4), channel_id=1, source_target_pairs={{0,1},{1,2},{2,3},{3,4},{4,5},{5,6},{6,7},{7,8},{8,9},{9,10},{10,1... | collective-permute-start | bytes 2359304 | tf_op jit(solution)/shard_map/ppermute | solution.py:218
  153.4 1.0 copy-start.18
  154.4 2.2 %copy-start.20 = (bf16[256,64,128]{2,1,0:T(8,128)(2,1)S(1)}, bf16[256,64,128]{2,1,0:T(8,128)(2,1)}, u32[]{:S(2)}) copy-start(bf16[256,64,128]{2,1,0:T(8,128)(2,1)} %refs_9_.5) | copy-start | bytes 12582916
  169.6 13.3 %copy-start.19 = (bf16[2,2,256,128]{3,2,1,0:T(8,128)(2,1)S(1)}, bf16[2,2,256,128]{3,2,1,0:T(8,128)(2,1)}, u32[]{:S(2)}) copy-start(bf16[2,2,256,128]{3,2,1,0:T(8,128)(2,1)} %get-tuple-element.8.refs_0_) | copy-start | bytes 786436

commit v2 on v1

v2 whole, which is shorter than its diff:
```python
import functools
import math

import jax
import jax.numpy as jnp
from jax import lax
from jax.experimental import pallas as pl
from jax.experimental.pallas import tpu as pltpu
from jax.sharding import PartitionSpec as P

BLOCK = 128
WIDTH = 128
SHARD_BLOCKS = 16
REMOTE = 4
LISTED = 8
KV = 8
SHARING = 8
LOCAL = 2
ROWS = LOCAL * BLOCK
PIECES = 8
EARLY, CROSS, LATE = 2, 2, 4
GROUPS = ((0, EARLY + CROSS), (0, EARLY), (EARLY + CROSS, KV))
FACTOR = math.log2(math.e) / math.sqrt(WIDTH)
NT = (((1,), (1,)), ((), ()))

X_UP = [(i, (i + 2) % 8) for i in range(8)]
X_DOWN = [(i, (i - 2) % 8) for i in range(8)]
Y_SWAP = [(i, i ^ 1) for i in range(8)]


def over_heads(array, route):
    return lax.ppermute(array, "heads", route)


def split_kernel(keys, values, *rest):
    outs, wide = rest[:-1], rest[-1]
    for which, source in enumerate((keys, values)):
        wide[...] = source[...].astype(jnp.float32).reshape(ROWS * KV, WIDTH)
        for head in range(KV):
            rows = wide[pl.ds(head, ROWS, stride=KV), :].astype(jnp.bfloat16)
            for out, (first, last) in zip(outs, GROUPS):
                if first <= head < last:
                    out[which, head - first] = rows


def split_heads(keys, values):
    return pl.pallas_call(
        split_kernel,
        out_shape=[
            jax.ShapeDtypeStruct((2, last - first, ROWS, WIDTH), jnp.bfloat16)
            for first, last in GROUPS
        ],
        scratch_shapes=[pltpu.VMEM((ROWS * KV, WIDTH), jnp.float32)],
        cost_estimate=pl.CostEstimate(flops=1, bytes_accessed=1, transcendentals=0),
        name="split_heads",
    )(keys, values)


def plan_kernel(where, lists, table, wanted):
    base, mine_x, mine_y = where[0], where[1], where[2]
    table[KV * 2 * SHARD_BLOCKS] = base

    def place_of(number):
        across = (number // 4 - mine_x) & 3
        return across * 4 + ((number // 2) % 2 ^ mine_y) * 2 + number % 2

    places = [place_of(number) for number in range(SHARD_BLOCKS)]

    def one_head(head, carry):
        mask = jnp.int32(0)
        for block in range(LOCAL):
            for member in range(SHARING):
                for entry in range(LISTED):
                    local = lists[block, entry, head * SHARING + member] - base
                    bit = lax.shift_left(jnp.int32(1), jnp.minimum(local, SHARD_BLOCKS))
                    mask = mask | bit
        for slot in range(REMOTE):
            wanted[head * REMOTE + slot] = 0
        count = jnp.int32(0)
        for number in range(SHARD_BLOCKS):
            table[head * 2 * SHARD_BLOCKS + number] = SHARD_BLOCKS + count
            listed = lax.shift_right_logical(mask, jnp.int32(number)) & 1

            @pl.when(listed == 1)
            def _():
                wanted[head * REMOTE + count] = places[number]

            count = count + listed
            table[head * 2 * SHARD_BLOCKS + SHARD_BLOCKS + number] = places[number]
        return carry

    lax.fori_loop(0, KV, one_head, 0)


def plan(where, lists):
    scalars = pl.BlockSpec(memory_space=pltpu.SMEM)
    return pl.pallas_call(
        plan_kernel,
        out_shape=[
            jax.ShapeDtypeStruct((KV * 2 * SHARD_BLOCKS + 1,), jnp.int32),
            jax.ShapeDtypeStruct((KV * REMOTE,), jnp.int32),
        ],
        in_specs=[scalars, scalars],
        out_specs=[scalars, scalars],
        cost_estimate=pl.CostEstimate(flops=1, bytes_accessed=1, transcendentals=0),
        name="plan",
    )(where, lists)


def join(table, pieces, head):
    if len(pieces) == PIECES:
        for number, piece in enumerate(pieces):
            table[:, pl.ds(number * ROWS, ROWS), :] = piece[:, head]
    else:
        for across in range(4):
            for number, piece in enumerate(pieces):
                table[:, pl.ds((2 * across + number) * ROWS, ROWS), :] = piece[across, :, head]


def per_head(array, within=0):
    if array.ndim == 5:
        return pl.BlockSpec((4, 2, 1, ROWS, WIDTH), lambda head, *_: (0, 0, within + head, 0, 0))
    return pl.BlockSpec((2, 1, array.shape[2], WIDTH), lambda head, *_: (0, within + head, 0, 0))


def pick_kernel(first, within, asked, *refs):
    pieces, (out, joined) = refs[:-2], refs[-2:]
    head = within + pl.program_id(0)
    join(joined, pieces, head)
    head = first + head
    for slot in range(REMOTE):
        place = asked[head * REMOTE + slot]
        rows = pl.ds(pl.multiple_of(place * BLOCK, BLOCK), BLOCK)
        out[:, 0, pl.ds(slot * BLOCK, BLOCK), :] = joined[:, rows, :]


def pick_blocks(first, within, size, asked, pieces):
    return pl.pallas_call(
        functools.partial(pick_kernel, first, within),
        grid_spec=pltpu.PrefetchScalarGridSpec(
            num_scalar_prefetch=1,
            grid=(size,),
            in_specs=[pl.BlockSpec(memory_space=pltpu.VMEM)] * len(pieces),
            out_specs=pl.BlockSpec(
                (2, 1, REMOTE * BLOCK, WIDTH), lambda head, *_: (0, head, 0, 0)
            ),
            scratch_shapes=[pltpu.VMEM((2, SHARD_BLOCKS * BLOCK, WIDTH), jnp.bfloat16)],
        ),
        out_shape=jax.ShapeDtypeStruct((2, size, REMOTE * BLOCK, WIDTH), jnp.bfloat16),
        cost_estimate=pl.CostEstimate(flops=1, bytes_accessed=1, transcendentals=0),
        compiler_params=pltpu.CompilerParams(vmem_limit_bytes=16 * 2**20),
        name=f"pick_blocks_{first + within}",
    )(asked, *pieces)


def attend_kernel(first, within, picked_within, aliased, lists, places, *refs):
    out, table, wide, mixed = refs[-4:]
    *pieces, picked, queries = refs[: -4 - aliased]
    head, block = pl.program_id(0), pl.program_id(1)

    @pl.when(block == 0)
    def _():
        join(table, pieces, within + head)
        table[:, pl.ds(PIECES * ROWS, REMOTE * BLOCK), :] = picked[:, picked_within + head]

    wide[...] = queries[...].astype(jnp.float32).reshape(BLOCK * SHARING, WIDTH)
    base, group = places[KV * 2 * SHARD_BLOCKS], first + within + head

    def slot_of(member, entry):
        local = lists[block, entry, group * SHARING + member] - base
        return places[group * 2 * SHARD_BLOCKS + local]

    def two(which, member, pair):
        at = [slot_of(member, 2 * pair + i) for i in range(2)]
        return jnp.concatenate(
            [table[which, pl.ds(pl.multiple_of(s * BLOCK, BLOCK), BLOCK), :] for s in at], 0
        )

    def scores_of(member):
        rows = wide[pl.ds(member, BLOCK, stride=SHARING), :].astype(jnp.bfloat16)
        return [
            lax.dot_general(rows, two(0, member, pair), NT, preferred_element_type=jnp.float32)
            for pair in range(LISTED // 2)
        ]

    def powers_of(scores):
        highest = jnp.max(functools.reduce(jnp.maximum, scores), axis=1, keepdims=True)
        powers = [jnp.exp2((part - highest) * FACTOR) for part in scores]
        totals = jnp.sum(functools.reduce(jnp.add, powers), axis=1, keepdims=True)
        return [part.astype(jnp.bfloat16) for part in powers], totals

    def mix(member, powers, totals):
        total = jnp.zeros((BLOCK, WIDTH), jnp.float32)
        for pair in range(LISTED // 2):
            total += jnp.dot(powers[pair], two(1, member, pair), preferred_element_type=jnp.float32)
        mixed[pl.ds(member, BLOCK, stride=SHARING), :] = total * (1.0 / totals)

    scores, before = scores_of(0), None
    for member in range(SHARING):
        later = scores_of(member + 1) if member + 1 < SHARING else None
        now = powers_of(scores)
        if before is not None:
            mix(member - 1, *before)
        before, scores = now, later
    mix(SHARING - 1, *before)
    out[...] = mixed[...].reshape(BLOCK, SHARING, WIDTH).astype(jnp.bfloat16)


def attend(first, within, size, scalars, pieces, picked, picked_within, queries, earlier):
    aliased = earlier is not None
    per_block = pl.BlockSpec(
        (BLOCK, SHARING, WIDTH), lambda head, block, *_: (block, first + within + head, 0)
    )
    return pl.pallas_call(
        functools.partial(attend_kernel, first, within, picked_within, aliased),
        grid_spec=pltpu.PrefetchScalarGridSpec(
            num_scalar_prefetch=2,
            grid=(size, LOCAL),
            in_specs=[pl.BlockSpec(memory_space=pltpu.VMEM)] * (len(pieces) + 1)
            + [per_block]
            + [pl.BlockSpec(memory_space=pl.ANY)] * aliased,
            out_specs=per_block,
            scratch_shapes=[
                pltpu.VMEM((2, (SHARD_BLOCKS + REMOTE) * BLOCK, WIDTH), jnp.bfloat16),
                pltpu.VMEM((BLOCK * SHARING, WIDTH), jnp.float32),
                pltpu.VMEM((BLOCK * SHARING, WIDTH), jnp.float32),
            ],
        ),
        out_shape=jax.ShapeDtypeStruct(queries.shape, queries.dtype),
        input_output_aliases={len(pieces) + 4: 0} if aliased else {},
        compiler_params=pltpu.CompilerParams(vmem_limit_bytes=16 * 2**20),
        cost_estimate=pl.CostEstimate(
            flops=size * 2**30, bytes_accessed=1, transcendentals=0
        ),
        name=f"attend_{first + within}",
    )(*scalars, *pieces, picked, queries, *([earlier] if aliased else []))


def after(array, *others):
    return lax.optimization_barrier((array, *others))[0]


def on_device(queries, key_states, value_states, block_lists):
    shard, member = lax.axis_index("blk"), lax.axis_index("heads")
    where = jnp.stack([(shard - 1) * SHARD_BLOCKS, member // 2, member % 2]).astype(jnp.int32)
    lists = jnp.transpose(block_lists, (0, 2, 1))
    most, early, late = split_heads(key_states, value_states)
    table, wanted = plan(where, lists)
    shards = lax.axis_size("blk")
    asked = lax.ppermute(wanted, "blk", [(i + 1, i) for i in range(shards - 1)])

    def fetch(first, within, size, pieces):
        chosen = pick_blocks(first, within, size, asked, pieces)
        return lax.ppermute(chosen, "blk", [(i, i + 1) for i in range(shards - 1)])

    def heads(first, within, size, pieces, arrived, earlier):
        return attend(first, within, size, (lists, table), pieces, arrived, 0, queries, earlier)

    swapped = over_heads(early, Y_SWAP)
    down, up = over_heads(most, X_UP), over_heads(most, X_DOWN)
    done = (swapped, down, up, asked)

    swapped = after(swapped, *done)
    swapped_down, swapped_up = over_heads(swapped, X_UP), over_heads(swapped, X_DOWN)
    half = CROSS // 2
    far = over_heads(after(down[:, : EARLY + half], *done), X_UP)
    far_rest = over_heads(after(up[:, EARLY + half :], *done), X_DOWN)
    late_swapped = over_heads(after(late, *done), Y_SWAP)
    row = jnp.stack(
        [
            most[:, EARLY:],
            up[:, EARLY:],
            jnp.concatenate([far[:, EARLY:], far_rest], 1),
            down[:, EARLY:],
        ]
    )
    done = (swapped_down, swapped_up, far, late_swapped, row)

    swapped_far = over_heads(swapped_up, X_DOWN)
    cross = [row, over_heads(after(row, *done), Y_SWAP)]
    late_down, late_up = (over_heads(after(late, *done), route) for route in (X_UP, X_DOWN))
    first = [most, swapped, up, swapped_up, far, swapped_far, down, swapped_down]
    arrived = fetch(0, 0, EARLY, first)

    late_swapped = after(late_swapped, late_down, late_up, swapped_far)
    late_swapped_down, late_swapped_up = (
        over_heads(late_swapped, route) for route in (X_UP, X_DOWN)
    )
    result = heads(0, 0, EARLY, first, after(arrived, late_down, late_up), None)
    done = (late_down, late_up, late_swapped_down, late_swapped_up)

    late_far = over_heads(after(late_down, *done), X_UP)
    late_swapped_far = over_heads(after(late_swapped_up, *done), X_DOWN)
    arrived = fetch(EARLY, 0, CROSS, cross)
    result = heads(EARLY, 0, CROSS, cross, arrived, result)

    last = [late, late_swapped, late_up, late_swapped_up]
    last += [after(late_far, result), late_swapped_far, late_down, late_swapped_down]
    begin, half = EARLY + CROSS, LATE // 2
    arrived = [fetch(begin, 0, half, last), fetch(begin, half, LATE - half, last)]
    result = heads(begin, 0, half, last, arrived[0], result)
    return heads(begin, half, LATE - half, last, arrived[1], result)


def solution(mesh):
    spec = P(("blk", "heads"), None, None)
    return jax.shard_map(
        on_device,
        mesh=mesh,
        in_specs=(spec,) * 4,
        out_specs=spec,
        check_vma=False,
    )
```

time: 193 us -> 123 us (0.64)
  Pallas kernels: 108 us -> 44.1 us
  starting transfers between devices: 35.9 us -> 50.7 us
  local copies, waits for them, and re-layouts: 14.1 us -> 1.08 us
  other arithmetic: 7.03 us -> 0.82 us
  waiting for transfers between devices: 27.4 us -> 25 us
    pallas_call x7 -> x10, Pallas kernels: 108 us -> 44.1 us  [the longest x4 34 us: attend(): pl.pallas_call(functools.partial(attend_kernel, first, within, picked_wit...]
    ppermute x4 -> x5, starting transfers between devices: 13.2 us -> 24.1 us  [the longest x4 21 us: fetch(): return lax.ppermute(chosen, 'blk', [(i, i + 1) for i in range(shards - 1)])]
    ppermute x21 -> x16, waiting for transfers between devices: 25.3 us -> 20.3 us  [over_heads(): return lax.ppermute(array, 'heads', route)]
    slice x8 -> x3, local copies, waits for them, and re-layouts: 4.91 us -> 0.05 us  [the longest x1 0.03 us: on_device(): far = over_heads(after(down[:, :EARLY + half], *done), X_UP)]
    ppermute x21 -> x16, starting transfers between devices: 22.8 us -> 26.6 us  [over_heads(): return lax.ppermute(array, 'heads', route)]
    unnamed x46 -> x10, local copies, waits for them, and re-layouts: 3.77 us -> 0.02 us
    reduce_sum x3 -> x0, other arithmetic: 3.59 us -> none  [the longest x1 3.23 us: on_device(): jnp.sum(listed[None, :, None, None, :] & (behind < local[..., None]), -1,...]
    ppermute x4 -> x5, waiting for transfers between devices: 2.12 us -> 4.67 us  [the longest x4 3.43 us: fetch(): return lax.ppermute(chosen, 'blk', [(i, i + 1) for i in range(shards - 1)])]
  transfers between devices with their start and end apart: 25 -> 21, of which waited for: 7 -> 7; matrix products, arithmetic and copies ran while one was open for 9% -> 2% of each run, Pallas kernels for 50% -> 26%
where the time goes in v2:
time: 123 us; the launch traced here: 122 us
  starting transfers between devices  50.7 us (41%)
  Pallas kernels  44.1 us (36%)
  waiting for transfers between devices  25 us (20%)
    pallas_call x4, Pallas kernels, attend(): pl.pallas_call(functools.partial(attend_kernel, first, within, picked_wit...  34 us
    ppermute x16, starting transfers between devices, over_heads(): return lax.ppermute(array, 'heads', route)  26.6 us
    ppermute x4, starting transfers between devices, fetch(): return lax.ppermute(chosen, 'blk', [(i, i + 1) for i in range(shards - 1)])  21 us
    ppermute x16, waiting for transfers between devices, over_heads(): return lax.ppermute(array, 'heads', route)  20.3 us
    pallas_call x1, Pallas kernels, plan(): pl.pallas_call(plan_kernel, out_shape=[jax.ShapeDtypeStruct((KV * 2 * SHA...  4.23 us
    ppermute x4, waiting for transfers between devices, fetch(): return lax.ppermute(chosen, 'blk', [(i, i + 1) for i in range(shards - 1)])  3.43 us
    pallas_call x4, Pallas kernels, pick_blocks(): pl.pallas_call(functools.partial(pick_kernel, first, within), grid_spec=p...  3.18 us
    ppermute x1, starting transfers between devices, on_device(): asked = lax.ppermute(wanted, 'blk', [(i + 1, i) for i in range(shards - 1)])  3.14 us
  transfers between devices with their start and end apart: 21, of which 7 were waited for; matrix products, arithmetic and copies ran while one was open for 2% of the time, Pallas kernels for 26%

profile of v2, /device:TPU:1, one launch (start us, length us, event | category | flops | bytes accessed | tf_op | source)
XLA Modules:
  0.0 121.9 jit_solution(14670437521526751150)
XLA Ops:
  0.0 2.7 %split_heads.1 = (bf16[2,4,256,128]{3,2,1,0:T(8,128)(2,1)}, bf16[2,2,256,128]{3,2,1,0:T(8,128)(2,1)}, bf16[2,4,256,128]{3,2,1,0:T(8,128)(2,1)}) custom-call(bf16[256,8,128]{2,1,0:T(8,128)(2,1)} %keys.1, bf16[256,8,128]{2,1,0:T(8,128)(2,1)} %values.1), custom_call_target="tpu_custom_call" | custom-call | flops 1 | bytes 1 | tf_op jit(solution)/shard_map/split_heads/pallas_call | solution.py:47
  2.7 0.0 copy-start.1
  2.7 3.3 %collective-permute-start.2 = (bf16[2,4,256,128]{3,2,1,0:T(8,128)(2,1)}, bf16[2,4,256,128]{3,2,1,0:T(8,128)(2,1)S(1)}, u32[]{:S(2)}, u32[]{:S(2)}) collective-permute-start(bf16[2,4,256,128]{3,2,1,0:T(8,128)(2,1)} %get-tuple-element.24.refs_0_), channel_id=1, source_target_pairs={{0,96},{16,112},{32,0},{48,16},{64,32},{80,48},{96,64},{112,80},{1... | collective-permute-start | bytes 1572872 | tf_op jit(solution)/shard_map/ppermute | solution.py:32
  6.0 0.0 collective-permute-start.1
  6.0 2.9 %collective-permute-start = (bf16[2,2,256,128]{3,2,1,0:T(8,128)(2,1)}, bf16[2,2,256,128]{3,2,1,0:T(8,128)(2,1)S(1)}, u32[]{:S(2)}, u32[]{:S(2)}) collective-permute-start(bf16[2,2,256,128]{3,2,1,0:T(8,128)(2,1)} %get-tuple-element.23), channel_id=1, source_target_pairs={{0,16},{16,0},{32,48},{48,32},{64,80},{80,64},{96,112},{112,96},{1... | collective-permute-start | bytes 786440 | tf_op jit(solution)/shard_map/ppermute | solution.py:32
  8.9 0.7 pad_add_fusion.where
  9.6 4.2 %plan.1 = (s32[257]{0:T(512)}, s32[32]{0:T(128)}) custom-call(s32[3]{0:T(128)} %pad_add_fusion.where, s32[2,8,64]{2,1,0:T(8,128)} %bitcast.12), custom_call_target="tpu_custom_call" | custom-call | flops 1 | bytes 1 | tf_op jit(solution)/shard_map/plan/pallas_call | solution.py:97
  13.8 3.1 %collective-permute-start.3 = (s32[32]{0:T(128)}, s32[32]{0:T(128)S(1)}, u32[]{:S(2)}, u32[]{:S(2)}) collective-permute-start(s32[32]{0:T(128)} %get-tuple-element.25), channel_id=1, source_target_pairs={{1,0},{2,1},{3,2},{4,3},{5,4},{6,5},{7,6},{8,7},{9,8},{10,9},{11,1... | collective-permute-start | bytes 392 | tf_op jit(solution)/shard_map/ppermute | solution.py:250
  17.0 1.0 slice_bitcast_fusion.2
  18.0 1.2 %collective-permute-done.3.asked = s32[32]{0:T(128)S(1)} collective-permute-done((s32[32]{0:T(128)}, s32[32]{0:T(128)S(1)}, u32[]{:S(2)}, u32[]{:S(2)}) %collective-permute-start.3) | collective-permute-done | bytes 160 | tf_op jit(solution)/shard_map/ppermute | solution.py:250
  19.2 0.0 collective-permute-done.refs_1_
  19.2 0.0 collective-permute-done.2.refs_2_
  19.2 0.7 collective-permute-done.1.refs_6_
  19.9 0.0 collective-permute-start.5
  19.9 2.7 %collective-permute-start.6 = (bf16[2,2,256,128]{3,2,1,0:T(8,128)(2,1)S(1)}, bf16[2,2,256,128]{3,2,1,0:T(8,128)(2,1)S(1)}, u32[]{:S(2)}, u32[]{:S(2)}) collective-permute-start(bf16[2,2,256,128]{3,2,1,0:T(8,128)(2,1)S(1)} %collective-permute-done.refs_1_), channel_id=1, source_target_pairs={{0,96},{16,112},{32,0},{48,16},{64,32},{80,48},{96,64},{112,80},{1... | collective-permute-start | bytes 786440 | tf_op jit(solution)/shard_map/ppermute | solution.py:32
  22.6 0.7 collective-permute-start.8
  23.3 0.9 collective-permute-start.7
  24.2 2.9 %collective-permute-start.4 = (bf16[2,4,256,128]{3,2,1,0:T(8,128)(2,1)}, bf16[2,4,256,128]{3,2,1,0:T(8,128)(2,1)S(1)}, u32[]{:S(2)}, u32[]{:S(2)}) collective-permute-start(bf16[2,4,256,128]{3,2,1,0:T(8,128)(2,1)} %get-tuple-element.30.refs_0_), channel_id=1, source_target_pairs={{0,16},{16,0},{32,48},{48,32},{64,80},{80,64},{96,112},{112,96},{1... | collective-permute-start | bytes 1572872 | tf_op jit(solution)/shard_map/ppermute | solution.py:32
  27.2 8.5 %collective-permute-done.7.refs_4_ = bf16[2,3,256,128]{3,2,1,0:T(8,128)(2,1)S(1)} collective-permute-done((bf16[2,3,256,128]{3,2,1,0:T(8,128)(2,1)S(1)}, bf16[2,3,256,128]{3,2,1,0:T(8,128)(2,1)S(1)}, u32[]{:S(2)}, u32[]{:S(2)}) %collective-permute-start.7) | collective-permute-done | bytes 393248 | tf_op jit(solution)/shard_map/ppermute | solution.py:32
  35.7 0.0 collective-permute-done.8
  35.8 0.0 copy-start
  35.8 0.0 copy-start.3
  35.8 0.0 copy-start.4
  35.8 0.1 pad_maximum_fusion.refs_0_
  36.0 0.0 collective-permute-done.5.refs_7_
  36.0 0.0 collective-permute-done.6.refs_3_
  36.0 0.4 collective-permute-done.4.refs_1_
  36.4 2.9 %collective-permute-start.15 = (bf16[4,2,2,256,128]{4,3,2,1,0:T(8,128)(2,1)S(1)}, bf16[4,2,2,256,128]{4,3,2,1,0:T(8,128)(2,1)S(1)}, u32[]{:S(2)}, u32[]{:S(2)}) collective-permute-start(bf16[4,2,2,256,128]{4,3,2,1,0:T(8,128)(2,1)S(1)} %pad_maximum_fusion.refs_0_), channel_id=1, source_target_pairs={{0,16},{16,0},{32,48},{48,32},{64,80},{80,64},{96,112},{112,96},{1... | collective-permute-start | bytes 3145736 | tf_op jit(solution)/shard_map/ppermute | solution.py:32
  39.3 0.0 copy-done.1
  39.3 1.5 %collective-permute-start.10 = (bf16[2,4,256,128]{3,2,1,0:T(8,128)(2,1)S(1)}, bf16[2,4,256,128]{3,2,1,0:T(8,128)(2,1)S(1)}, u32[]{:S(2)}, u32[]{:S(2)}) collective-permute-start(bf16[2,4,256,128]{3,2,1,0:T(8,128)(2,1)S(1)} %copy-done.1), channel_id=1, source_target_pairs={{0,96},{16,112},{32,0},{48,16},{64,32},{80,48},{96,64},{112,80},{1... | collective-permute-start | bytes 1572872 | tf_op jit(solution)/shard_map/ppermute | solution.py:32
  40.8 0.0 collective-permute-start.9
  40.8 2.7 %collective-permute-start.11 = (bf16[2,2,256,128]{3,2,1,0:T(8,128)(2,1)S(1)}, bf16[2,2,256,128]{3,2,1,0:T(8,128)(2,1)S(1)}, u32[]{:S(2)}, u32[]{:S(2)}) collective-permute-start(bf16[2,2,256,128]{3,2,1,0:T(8,128)(2,1)S(1)} %collective-permute-done.6.refs_3_), channel_id=1, source_target_pairs={{0,96},{16,112},{32,0},{48,16},{64,32},{80,48},{96,64},{112,80},{1... | collective-permute-start | bytes 786440 | tf_op jit(solution)/shard_map/ppermute | solution.py:32
  43.5 10.7 %collective-permute-done.11.refs_5_ = bf16[2,2,256,128]{3,2,1,0:T(8,128)(2,1)S(1)} collective-permute-done((bf16[2,2,256,128]{3,2,1,0:T(8,128)(2,1)S(1)}, bf16[2,2,256,128]{3,2,1,0:T(8,128)(2,1)S(1)}, u32[]{:S(2)}, u32[]{:S(2)}) %collective-permute-start.11) | collective-permute-done | bytes 262176 | tf_op jit(solution)/shard_map/ppermute | solution.py:32
  54.1 0.0 collective-permute-done.10.refs_2_
  54.1 0.0 collective-permute-done.9.refs_6_
  54.1 3.0 %collective-permute-start.12 = (bf16[2,4,256,128]{3,2,1,0:T(8,128)(2,1)S(1)}, bf16[2,4,256,128]{3,2,1,0:T(8,128)(2,1)S(1)}, u32[]{:S(2)}, u32[]{:S(2)}) collective-permute-start(bf16[2,4,256,128]{3,2,1,0:T(8,128)(2,1)S(1)} %collective-permute-done.4.refs_1_), channel_id=1, source_target_pairs={{0,96},{16,112},{32,0},{48,16},{64,32},{80,48},{96,64},{112,80},{1... | collective-permute-start | bytes 1572872 | tf_op jit(solution)/shard_map/ppermute | solution.py:32
  57.2 0.0 collective-permute-start.13
  57.2 0.0 copy-done.2
  57.2 0.8 pick_blocks_0.1
  58.0 8.7 %collective-permute-start.17 = (bf16[2,2,512,128]{3,2,1,0:T(8,128)(2,1)S(1)}, bf16[2,2,512,128]{3,2,1,0:T(8,128)(2,1)S(1)}, u32[]{:S(2)}, u32[]{:S(2)}) collective-permute-start(bf16[2,2,512,128]{3,2,1,0:T(8,128)(2,1)S(1)} %pick_blocks_0.1), channel_id=1, source_target_pairs={{0,1},{1,2},{2,3},{3,4},{4,5},{5,6},{6,7},{7,8},{8,9},{9,10},{10,1... | collective-permute-start | bytes 1572872 | tf_op jit(solution)/shard_map/ppermute | solution.py:254
  66.7 0.0 collective-permute-done.15.refs_1_
  66.7 0.8 pick_blocks_2.1
  67.5 1.9 %collective-permute-start.16 = (bf16[2,2,512,128]{3,2,1,0:T(8,128)(2,1)S(1)}, bf16[2,2,512,128]{3,2,1,0:T(8,128)(2,1)S(1)}, u32[]{:S(2)}, u32[]{:S(2)}) collective-permute-start(bf16[2,2,512,128]{3,2,1,0:T(8,128)(2,1)S(1)} %pick_blocks_2.1), channel_id=1, source_target_pairs={{0,1},{1,2},{2,3},{3,4},{4,5},{5,6},{6,7},{7,8},{8,9},{9,10},{10,1... | collective-permute-start | bytes 1572872 | tf_op jit(solution)/shard_map/ppermute | solution.py:254
  69.4 0.0 collective-permute-done.12.refs_3_
  69.4 0.0 collective-permute-done.13.refs_7_
  69.4 0.1 collective-permute-start.14
  69.5 3.0 %collective-permute-start.18 = (bf16[2,4,256,128]{3,2,1,0:T(8,128)(2,1)S(1)}, bf16[2,4,256,128]{3,2,1,0:T(8,128)(2,1)S(1)}, u32[]{:S(2)}, u32[]{:S(2)}) collective-permute-start(bf16[2,4,256,128]{3,2,1,0:T(8,128)(2,1)S(1)} %collective-permute-done.12.refs_3_), channel_id=1, source_target_pairs={{0,96},{16,112},{32,0},{48,16},{64,32},{80,48},{96,64},{112,80},{1... | collective-permute-start | bytes 1572872 | tf_op jit(solution)/shard_map/ppermute | solution.py:32
  72.5 0.2 collective-permute-done.17.refs_8_
  72.8 0.0 copy-done
  72.8 0.0 copy-done.3
  72.8 0.0 copy-done.4
  72.8 8.5 %attend_0.1.refs_4_ = bf16[256,64,128]{2,1,0:T(8,128)(2,1)} custom-call(s32[2,8,64]{2,1,0:T(8,128)S(1)} %bitcast.13, s32[257]{0:T(512)S(1)} %copy-done.4, bf16[2,4,256,128]{3,2,1,0:T(8,128)(2,1)S(1)} %copy-done.2, bf16[2,2,256,128]{3,2,1,0:T(8,128)(2,1)S(1)} %collective-permute-done.refs_1_, bf16[2,4,256,128]{3,2,1,0:T(8,128)(2,1)S(1)} %collective-permute-done.2.refs_2_, ...), custom_call_target="tpu_custom_call" | custom-call | flops 2147483648 | bytes 1 | tf_op jit(solution)/shard_map/attend_0/pallas_call | solution.py:214
  81.3 0.0 collective-permute-done.16.refs_2_
  81.3 8.5 %attend_2.1.refs_10_ = bf16[256,64,128]{2,1,0:T(8,128)(2,1)} custom-call(s32[2,8,64]{2,1,0:T(8,128)S(1)} %bitcast.14, s32[257]{0:T(512)S(1)} %copy-done.4, bf16[4,2,2,256,128]{4,3,2,1,0:T(8,128)(2,1)S(1)} %pad_maximum_fusion.refs_0_, bf16[4,2,2,256,128]{4,3,2,1,0:T(8,128)(2,1)S(1)} %collective-permute-done.15.refs_1_, ...), custom_call_target="tpu_custom_call", output_to_operand_aliasing={{}: (6, {})} | custom-call | flops 2147483648 | bytes 1 | tf_op jit(solution)/shard_map/attend_2/pallas_call | solution.py:214
  89.8 0.0 collective-permute-done.14.refs_4_
  89.8 0.0 collective-permute-done.18.refs_5_
  89.8 0.8 pick_blocks_4.1
  90.6 8.2 %collective-permute-start.20 = (bf16[2,2,512,128]{3,2,1,0:T(8,128)(2,1)S(1)}, bf16[2,2,512,128]{3,2,1,0:T(8,128)(2,1)S(1)}, u32[]{:S(2)}, u32[]{:S(2)}) collective-permute-start(bf16[2,2,512,128]{3,2,1,0:T(8,128)(2,1)S(1)} %pick_blocks_4.1), channel_id=1, source_target_pairs={{0,1},{1,2},{2,3},{3,4},{4,5},{5,6},{6,7},{7,8},{8,9},{9,10},{10,1... | collective-permute-start | bytes 1572872 | tf_op jit(solution)/shard_map/ppermute | solution.py:254
  98.8 0.8 pick_blocks_6.1
  99.6 2.1 %collective-permute-start.19 = (bf16[2,2,512,128]{3,2,1,0:T(8,128)(2,1)S(1)}, bf16[2,2,512,128]{3,2,1,0:T(8,128)(2,1)S(1)}, u32[]{:S(2)}, u32[]{:S(2)}) collective-permute-start(bf16[2,2,512,128]{3,2,1,0:T(8,128)(2,1)S(1)} %pick_blocks_6.1), channel_id=1, source_target_pairs={{0,1},{1,2},{2,3},{3,4},{4,5},{5,6},{6,7},{7,8},{8,9},{9,10},{10,1... | collective-permute-start | bytes 1572872 | tf_op jit(solution)/shard_map/ppermute | solution.py:254
  101.7 3.2 %collective-permute-done.20.refs_8_ = bf16[2,2,512,128]{3,2,1,0:T(8,128)(2,1)S(1)} collective-permute-done((bf16[2,2,512,128]{3,2,1,0:T(8,128)(2,1)S(1)}, bf16[2,2,512,128]{3,2,1,0:T(8,128)(2,1)S(1)}, u32[]{:S(2)}, u32[]{:S(2)}) %collective-permute-start.20) | collective-permute-done | bytes 524320 | tf_op jit(solution)/shard_map/ppermute | solution.py:254
  104.9 8.5 %attend_4.1.refs_10_ = bf16[256,64,128]{2,1,0:T(8,128)(2,1)} custom-call(s32[2,8,64]{2,1,0:T(8,128)S(1)} %bitcast.15, s32[257]{0:T(512)S(1)} %copy-done.4, bf16[2,4,256,128]{3,2,1,0:T(8,128)(2,1)S(1)} %copy-done.1, bf16[2,4,256,128]{3,2,1,0:T(8,128)(2,1)S(1)} %collective-permute-done.4.refs_1_, ...), custom_call_target="tpu_custom_call", output_to_operand_aliasing={{}: (12, {})} | custom-call | flops 2147483648 | bytes 1 | tf_op jit(solution)/shard_map/attend_4/pallas_call | solution.py:214
  113.4 0.0 collective-permute-done.19.refs_8_
  113.4 8.5 %attend_6.1 = bf16[256,64,128]{2,1,0:T(8,128)(2,1)} custom-call(s32[2,8,64]{2,1,0:T(8,128)S(1)} %bitcast.16, s32[257]{0:T(512)S(1)} %copy-done.4, bf16[2,4,256,128]{3,2,1,0:T(8,128)(2,1)S(1)} %copy-done.1, bf16[2,4,256,128]{3,2,1,0:T(8,128)(2,1)S(1)} %collective-permute-done.4.refs_1_, ...), custom_call_target="tpu_custom_call", output_to_operand_aliasing={{}: (12, {})} | custom-call | flops 2147483648 | bytes 1 | tf_op jit(solution)/shard_map/attend_6/pallas_call | solution.py:214
  (7 shorter events, 0.1 us)
Async XLA Ops:
  2.7 36.6 %copy-start.1 = (bf16[2,4,256,128]{3,2,1,0:T(8,128)(2,1)S(1)}, bf16[2,4,256,128]{3,2,1,0:T(8,128)(2,1)}, u32[]{:S(2)}) copy-start(bf16[2,4,256,128]{3,2,1,0:T(8,128)(2,1)} %get-tuple-element.30.refs_0_) | copy-start | bytes 1572868
  2.7 54.5 %copy-start.2 = (bf16[2,4,256,128]{3,2,1,0:T(8,128)(2,1)S(1)}, bf16[2,4,256,128]{3,2,1,0:T(8,128)(2,1)}, u32[]{:S(2)}) copy-start(bf16[2,4,256,128]{3,2,1,0:T(8,128)(2,1)} %get-tuple-element.24.refs_0_) | copy-start | bytes 1572868
  2.7 16.5 %collective-permute-start.2 = (bf16[2,4,256,128]{3,2,1,0:T(8,128)(2,1)}, bf16[2,4,256,128]{3,2,1,0:T(8,128)(2,1)S(1)}, u32[]{:S(2)}, u32[]{:S(2)}) collective-permute-start(bf16[2,4,256,128]{3,2,1,0:T(8,128)(2,1)} %get-tuple-element.24.refs_0_), channel_id=1, source_target_pairs={{0,96},{16,112},{32,0},{48,16},{64,32},{80,48},{96,64},{112,80},{1... | collective-permute-start | bytes 1572872 | tf_op jit(solution)/shard_map/ppermute | solution.py:32
  6.0 13.9 %collective-permute-start.1 = (bf16[2,4,256,128]{3,2,1,0:T(8,128)(2,1)}, bf16[2,4,256,128]{3,2,1,0:T(8,128)(2,1)S(1)}, u32[]{:S(2)}, u32[]{:S(2)}) collective-permute-start(bf16[2,4,256,128]{3,2,1,0:T(8,128)(2,1)} %get-tuple-element.24.refs_0_), channel_id=1, source_target_pairs={{0,32},{16,48},{32,64},{48,80},{64,96},{80,112},{96,0},{112,16},{1... | collective-permute-start | bytes 1572872 | tf_op jit(solution)/shard_map/ppermute | solution.py:32
  6.0 13.2 %collective-permute-start = (bf16[2,2,256,128]{3,2,1,0:T(8,128)(2,1)}, bf16[2,2,256,128]{3,2,1,0:T(8,128)(2,1)S(1)}, u32[]{:S(2)}, u32[]{:S(2)}) collective-permute-start(bf16[2,2,256,128]{3,2,1,0:T(8,128)(2,1)} %get-tuple-element.23), channel_id=1, source_target_pairs={{0,16},{16,0},{32,48},{48,32},{64,80},{80,64},{96,112},{112,96},{1... | collective-permute-start | bytes 786440 | tf_op jit(solution)/shard_map/ppermute | solution.py:32
  13.8 5.4 %collective-permute-start.3 = (s32[32]{0:T(128)}, s32[32]{0:T(128)S(1)}, u32[]{:S(2)}, u32[]{:S(2)}) collective-permute-start(s32[32]{0:T(128)} %get-tuple-element.25), channel_id=1, source_target_pairs={{1,0},{2,1},{3,2},{4,3},{5,4},{6,5},{7,6},{8,7},{9,8},{10,9},{11,1... | collective-permute-start | bytes 392 | tf_op jit(solution)/shard_map/ppermute | solution.py:250
  19.9 16.1 %collective-permute-start.5 = (bf16[2,2,256,128]{3,2,1,0:T(8,128)(2,1)S(1)}, bf16[2,2,256,128]{3,2,1,0:T(8,128)(2,1)S(1)}, u32[]{:S(2)}, u32[]{:S(2)}) collective-permute-start(bf16[2,2,256,128]{3,2,1,0:T(8,128)(2,1)S(1)} %collective-permute-done.refs_1_), channel_id=1, source_target_pairs={{0,32},{16,48},{32,64},{48,80},{64,96},{80,112},{96,0},{112,16},{1... | collective-permute-start | bytes 786440 | tf_op jit(solution)/shard_map/ppermute | solution.py:32
  19.9 16.1 %collective-permute-start.6 = (bf16[2,2,256,128]{3,2,1,0:T(8,128)(2,1)S(1)}, bf16[2,2,256,128]{3,2,1,0:T(8,128)(2,1)S(1)}, u32[]{:S(2)}, u32[]{:S(2)}) collective-permute-start(bf16[2,2,256,128]{3,2,1,0:T(8,128)(2,1)S(1)} %collective-permute-done.refs_1_), channel_id=1, source_target_pairs={{0,96},{16,112},{32,0},{48,16},{64,32},{80,48},{96,64},{112,80},{1... | collective-permute-start | bytes 786440 | tf_op jit(solution)/shard_map/ppermute | solution.py:32
  22.6 13.1 %collective-permute-start.8 = (bf16[2,1,256,128]{3,2,1,0:T(8,128)(2,1)S(1)}, bf16[2,1,256,128]{3,2,1,0:T(8,128)(2,1)S(1)}, u32[]{:S(2)}, u32[]{:S(2)}) collective-permute-start(bf16[2,1,256,128]{3,2,1,0:T(8,128)(2,1)S(1)} %slice.27), channel_id=1, source_target_pairs={{0,96},{16,112},{32,0},{48,16},{64,32},{80,48},{96,64},{112,80},{1... | collective-permute-start | bytes 393224 | tf_op jit(solution)/shard_map/ppermute | solution.py:32
  23.3 12.4 %collective-permute-start.7 = (bf16[2,3,256,128]{3,2,1,0:T(8,128)(2,1)S(1)}, bf16[2,3,256,128]{3,2,1,0:T(8,128)(2,1)S(1)}, u32[]{:S(2)}, u32[]{:S(2)}) collective-permute-start(bf16[2,3,256,128]{3,2,1,0:T(8,128)(2,1)S(1)} %slice.24), channel_id=1, source_target_pairs={{0,32},{16,48},{32,64},{48,80},{64,96},{80,112},{96,0},{112,16},{1... | collective-permute-start | bytes 1179656 | tf_op jit(solution)/shard_map/ppermute | solution.py:32
  24.2 12.1 %collective-permute-start.4 = (bf16[2,4,256,128]{3,2,1,0:T(8,128)(2,1)}, bf16[2,4,256,128]{3,2,1,0:T(8,128)(2,1)S(1)}, u32[]{:S(2)}, u32[]{:S(2)}) collective-permute-start(bf16[2,4,256,128]{3,2,1,0:T(8,128)(2,1)} %get-tuple-element.30.refs_0_), channel_id=1, source_target_pairs={{0,16},{16,0},{32,48},{48,32},{64,80},{80,64},{96,112},{112,96},{1... | collective-permute-start | bytes 1572872 | tf_op jit(solution)/shard_map/ppermute | solution.py:32
  35.8 37.0 %copy-start = (bf16[256,64,128]{2,1,0:T(8,128)(2,1)S(1)}, bf16[256,64,128]{2,1,0:T(8,128)(2,1)}, u32[]{:S(2)}) copy-start(bf16[256,64,128]{2,1,0:T(8,128)(2,1)} %refs_9_.5) | copy-start | bytes 12582916
  35.8 37.0 %copy-start.3 = (s32[2,64,8]{1,2,0:T(8,128)S(1)}, s32[2,64,8]{1,2,0:T(8,128)}, u32[]{:S(2)}) copy-start(s32[2,64,8]{1,2,0:T(8,128)} %param.7) | copy-start | bytes 12292
  35.8 37.0 %copy-start.4 = (s32[257]{0:T(512)S(1)}, s32[257]{0:T(512)}, u32[]{:S(2)}) copy-start(s32[257]{0:T(512)} %get-tuple-element.21.places) | copy-start | bytes 3088
  36.4 30.3 %collective-permute-start.15 = (bf16[4,2,2,256,128]{4,3,2,1,0:T(8,128)(2,1)S(1)}, bf16[4,2,2,256,128]{4,3,2,1,0:T(8,128)(2,1)S(1)}, u32[]{:S(2)}, u32[]{:S(2)}) collective-permute-start(bf16[4,2,2,256,128]{4,3,2,1,0:T(8,128)(2,1)S(1)} %pad_maximum_fusion.refs_0_), channel_id=1, source_target_pairs={{0,16},{16,0},{32,48},{48,32},{64,80},{80,64},{96,112},{112,96},{1... | collective-permute-start | bytes 3145736 | tf_op jit(solution)/shard_map/ppermute | solution.py:32
  39.3 14.8 %collective-permute-start.10 = (bf16[2,4,256,128]{3,2,1,0:T(8,128)(2,1)S(1)}, bf16[2,4,256,128]{3,2,1,0:T(8,128)(2,1)S(1)}, u32[]{:S(2)}, u32[]{:S(2)}) collective-permute-start(bf16[2,4,256,128]{3,2,1,0:T(8,128)(2,1)S(1)} %copy-done.1), channel_id=1, source_target_pairs={{0,96},{16,112},{32,0},{48,16},{64,32},{80,48},{96,64},{112,80},{1... | collective-permute-start | bytes 1572872 | tf_op jit(solution)/shard_map/ppermute | solution.py:32
  40.8 13.3 %collective-permute-start.9 = (bf16[2,4,256,128]{3,2,1,0:T(8,128)(2,1)S(1)}, bf16[2,4,256,128]{3,2,1,0:T(8,128)(2,1)S(1)}, u32[]{:S(2)}, u32[]{:S(2)}) collective-permute-start(bf16[2,4,256,128]{3,2,1,0:T(8,128)(2,1)S(1)} %copy-done.1), channel_id=1, source_target_pairs={{0,32},{16,48},{32,64},{48,80},{64,96},{80,112},{96,0},{112,16},{1... | collective-permute-start | bytes 1572872 | tf_op jit(solution)/shard_map/ppermute | solution.py:32
  40.8 13.3 %collective-permute-start.11 = (bf16[2,2,256,128]{3,2,1,0:T(8,128)(2,1)S(1)}, bf16[2,2,256,128]{3,2,1,0:T(8,128)(2,1)S(1)}, u32[]{:S(2)}, u32[]{:S(2)}) collective-permute-start(bf16[2,2,256,128]{3,2,1,0:T(8,128)(2,1)S(1)} %collective-permute-done.6.refs_3_), channel_id=1, source_target_pairs={{0,96},{16,112},{32,0},{48,16},{64,32},{80,48},{96,64},{112,80},{1... | collective-permute-start | bytes 786440 | tf_op jit(solution)/shard_map/ppermute | solution.py:32
  54.1 15.3 %collective-permute-start.12 = (bf16[2,4,256,128]{3,2,1,0:T(8,128)(2,1)S(1)}, bf16[2,4,256,128]{3,2,1,0:T(8,128)(2,1)S(1)}, u32[]{:S(2)}, u32[]{:S(2)}) collective-permute-start(bf16[2,4,256,128]{3,2,1,0:T(8,128)(2,1)S(1)} %collective-permute-done.4.refs_1_), channel_id=1, source_target_pairs={{0,96},{16,112},{32,0},{48,16},{64,32},{80,48},{96,64},{112,80},{1... | collective-permute-start | bytes 1572872 | tf_op jit(solution)/shard_map/ppermute | solution.py:32
  57.2 12.3 %collective-permute-start.13 = (bf16[2,4,256,128]{3,2,1,0:T(8,128)(2,1)S(1)}, bf16[2,4,256,128]{3,2,1,0:T(8,128)(2,1)S(1)}, u32[]{:S(2)}, u32[]{:S(2)}) collective-permute-start(bf16[2,4,256,128]{3,2,1,0:T(8,128)(2,1)S(1)} %collective-permute-done.4.refs_1_), channel_id=1, source_target_pairs={{0,32},{16,48},{32,64},{48,80},{64,96},{80,112},{96,0},{112,16},{1... | collective-permute-start | bytes 1572872 | tf_op jit(solution)/shard_map/ppermute | solution.py:32
  58.0 14.8 %collective-permute-start.17 = (bf16[2,2,512,128]{3,2,1,0:T(8,128)(2,1)S(1)}, bf16[2,2,512,128]{3,2,1,0:T(8,128)(2,1)S(1)}, u32[]{:S(2)}, u32[]{:S(2)}) collective-permute-start(bf16[2,2,512,128]{3,2,1,0:T(8,128)(2,1)S(1)} %pick_blocks_0.1), channel_id=1, source_target_pairs={{0,1},{1,2},{2,3},{3,4},{4,5},{5,6},{6,7},{7,8},{8,9},{9,10},{10,1... | collective-permute-start | bytes 1572872 | tf_op jit(solution)/shard_map/ppermute | solution.py:254
  67.5 13.8 %collective-permute-start.16 = (bf16[2,2,512,128]{3,2,1,0:T(8,128)(2,1)S(1)}, bf16[2,2,512,128]{3,2,1,0:T(8,128)(2,1)S(1)}, u32[]{:S(2)}, u32[]{:S(2)}) collective-permute-start(bf16[2,2,512,128]{3,2,1,0:T(8,128)(2,1)S(1)} %pick_blocks_2.1), channel_id=1, source_target_pairs={{0,1},{1,2},{2,3},{3,4},{4,5},{5,6},{6,7},{7,8},{8,9},{9,10},{10,1... | collective-permute-start | bytes 1572872 | tf_op jit(solution)/shard_map/ppermute | solution.py:254
  69.4 20.3 %collective-permute-start.14 = (bf16[2,4,256,128]{3,2,1,0:T(8,128)(2,1)S(1)}, bf16[2,4,256,128]{3,2,1,0:T(8,128)(2,1)S(1)}, u32[]{:S(2)}, u32[]{:S(2)}) collective-permute-start(bf16[2,4,256,128]{3,2,1,0:T(8,128)(2,1)S(1)} %collective-permute-done.9.refs_6_), channel_id=1, source_target_pairs={{0,32},{16,48},{32,64},{48,80},{64,96},{80,112},{96,0},{112,16},{1... | collective-permute-start | bytes 1572872 | tf_op jit(solution)/shard_map/ppermute | solution.py:32
  69.5 20.3 %collective-permute-start.18 = (bf16[2,4,256,128]{3,2,1,0:T(8,128)(2,1)S(1)}, bf16[2,4,256,128]{3,2,1,0:T(8,128)(2,1)S(1)}, u32[]{:S(2)}, u32[]{:S(2)}) collective-permute-start(bf16[2,4,256,128]{3,2,1,0:T(8,128)(2,1)S(1)} %collective-permute-done.12.refs_3_), channel_id=1, source_target_pairs={{0,96},{16,112},{32,0},{48,16},{64,32},{80,48},{96,64},{112,80},{1... | collective-permute-start | bytes 1572872 | tf_op jit(solution)/shard_map/ppermute | solution.py:32
  90.6 14.3 %collective-permute-start.20 = (bf16[2,2,512,128]{3,2,1,0:T(8,128)(2,1)S(1)}, bf16[2,2,512,128]{3,2,1,0:T(8,128)(2,1)S(1)}, u32[]{:S(2)}, u32[]{:S(2)}) collective-permute-start(bf16[2,2,512,128]{3,2,1,0:T(8,128)(2,1)S(1)} %pick_blocks_4.1), channel_id=1, source_target_pairs={{0,1},{1,2},{2,3},{3,4},{4,5},{5,6},{6,7},{7,8},{8,9},{9,10},{10,1... | collective-permute-start | bytes 1572872 | tf_op jit(solution)/shard_map/ppermute | solution.py:254
  99.6 13.8 %collective-permute-start.19 = (bf16[2,2,512,128]{3,2,1,0:T(8,128)(2,1)S(1)}, bf16[2,2,512,128]{3,2,1,0:T(8,128)(2,1)S(1)}, u32[]{:S(2)}, u32[]{:S(2)}) collective-permute-start(bf16[2,2,512,128]{3,2,1,0:T(8,128)(2,1)S(1)} %pick_blocks_6.1), channel_id=1, source_target_pairs={{0,1},{1,2},{2,3},{3,4},{4,5},{5,6},{6,7},{7,8},{8,9},{9,10},{10,1... | collective-permute-start | bytes 1572872 | tf_op jit(solution)/shard_map/ppermute | solution.py:254

commit v3 on v2

--- a/solution.py
+++ b/solution.py
@@ -107,26 +107,20 @@
     )(where, lists)
 
 
-def join(table, pieces, head):
+def join(table, pieces, begins, head):
     if len(pieces) == PIECES:
-        for number, piece in enumerate(pieces):
-            table[:, pl.ds(number * ROWS, ROWS), :] = piece[:, head]
+        for number, (piece, begin) in enumerate(zip(pieces, begins)):
+            table[:, pl.ds(number * ROWS, ROWS), :] = piece[:, begin + head]
     else:
         for across in range(4):
             for number, piece in enumerate(pieces):
                 table[:, pl.ds((2 * across + number) * ROWS, ROWS), :] = piece[across, :, head]
 
 
-def per_head(array, within=0):
-    if array.ndim == 5:
-        return pl.BlockSpec((4, 2, 1, ROWS, WIDTH), lambda head, *_: (0, 0, within + head, 0, 0))
-    return pl.BlockSpec((2, 1, array.shape[2], WIDTH), lambda head, *_: (0, within + head, 0, 0))
-
-
-def pick_kernel(first, within, asked, *refs):
+def pick_kernel(first, begins, asked, *refs):
     pieces, (out, joined) = refs[:-2], refs[-2:]
-    head = within + pl.program_id(0)
-    join(joined, pieces, head)
+    head = pl.program_id(0)
+    join(joined, pieces, begins, head)
     head = first + head
     for slot in range(REMOTE):
         place = asked[head * REMOTE + slot]
@@ -134,9 +128,9 @@
         out[:, 0, pl.ds(slot * BLOCK, BLOCK), :] = joined[:, rows, :]
 
 
-def pick_blocks(first, within, size, asked, pieces):
+def pick_blocks(first, size, asked, pieces, begins):
     return pl.pallas_call(
-        functools.partial(pick_kernel, first, within),
+        functools.partial(pick_kernel, first, begins),
         grid_spec=pltpu.PrefetchScalarGridSpec(
             num_scalar_prefetch=1,
             grid=(size,),
@@ -149,24 +143,21 @@
         out_shape=jax.ShapeDtypeStruct((2, size, REMOTE * BLOCK, WIDTH), jnp.bfloat16),
         cost_estimate=pl.CostEstimate(flops=1, bytes_accessed=1, transcendentals=0),
         compiler_params=pltpu.CompilerParams(vmem_limit_bytes=16 * 2**20),
-        name=f"pick_blocks_{first + within}",
+        name=f"pick_blocks_{first}",
     )(asked, *pieces)
 
 
-def attend_kernel(first, within, picked_within, aliased, lists, places, *refs):
+def attend_kernel(first, begins, aliased, lists, places, *refs):
     out, table, wide, mixed = refs[-4:]
     *pieces, picked, queries = refs[: -4 - aliased]
-    head, block = pl.program_id(0), pl.program_id(1)
-
-    @pl.when(block == 0)
-    def _():
-        join(table, pieces, within + head)
-        table[:, pl.ds(PIECES * ROWS, REMOTE * BLOCK), :] = picked[:, picked_within + head]
-
-    wide[...] = queries[...].astype(jnp.float32).reshape(BLOCK * SHARING, WIDTH)
-    base, group = places[KV * 2 * SHARD_BLOCKS], first + within + head
+    head = pl.program_id(0)
+    join(table, pieces, begins, head)
+    table[:, pl.ds(PIECES * ROWS, REMOTE * BLOCK), :] = picked[:, head]
+    wide[...] = queries[...].astype(jnp.float32).reshape(ROWS * SHARING, WIDTH)
+    base, group = places[KV * 2 * SHARD_BLOCKS], first + head
 
     def slot_of(member, entry):
+        block, member = divmod(member, SHARING)
         local = lists[block, entry, group * SHARING + member] - base
         return places[group * 2 * SHARD_BLOCKS + local]
 
@@ -176,8 +167,12 @@
             [table[which, pl.ds(pl.multiple_of(s * BLOCK, BLOCK), BLOCK), :] for s in at], 0
         )
 
+    def rows_of(member):
+        block, member = divmod(member, SHARING)
+        return pl.ds(block * BLOCK * SHARING + member, BLOCK, stride=SHARING)
+
     def scores_of(member):
-        rows = wide[pl.ds(member, BLOCK, stride=SHARING), :].astype(jnp.bfloat16)
+        rows = wide[rows_of(member), :].astype(jnp.bfloat16)
         return [
             lax.dot_general(rows, two(0, member, pair), NT, preferred_element_type=jnp.float32)
             for pair in range(LISTED // 2)
@@ -193,37 +188,35 @@
         total = jnp.zeros((BLOCK, WIDTH), jnp.float32)
         for pair in range(LISTED // 2):
             total += jnp.dot(powers[pair], two(1, member, pair), preferred_element_type=jnp.float32)
-        mixed[pl.ds(member, BLOCK, stride=SHARING), :] = total * (1.0 / totals)
+        mixed[rows_of(member), :] = total * (1.0 / totals)
 
     scores, before = scores_of(0), None
-    for member in range(SHARING):
-        later = scores_of(member + 1) if member + 1 < SHARING else None
+    for member in range(LOCAL * SHARING):
+        later = scores_of(member + 1) if member + 1 < LOCAL * SHARING else None
         now = powers_of(scores)
         if before is not None:
             mix(member - 1, *before)
         before, scores = now, later
-    mix(SHARING - 1, *before)
-    out[...] = mixed[...].reshape(BLOCK, SHARING, WIDTH).astype(jnp.bfloat16)
-
-
-def attend(first, within, size, scalars, pieces, picked, picked_within, queries, earlier):
+    mix(LOCAL * SHARING - 1, *before)
+    out[...] = mixed[...].reshape(ROWS, SHARING, WIDTH).astype(jnp.bfloat16)
+
+
+def attend(first, size, scalars, pieces, begins, picked, queries, earlier):
     aliased = earlier is not None
-    per_block = pl.BlockSpec(
-        (BLOCK, SHARING, WIDTH), lambda head, block, *_: (block, first + within + head, 0)
-    )
+    per_group = pl.BlockSpec((ROWS, SHARING, WIDTH), lambda head, *_: (0, first + head, 0))
     return pl.pallas_call(
-        functools.partial(attend_kernel, first, within, picked_within, aliased),
+        functools.partial(attend_kernel, first, begins, aliased),
         grid_spec=pltpu.PrefetchScalarGridSpec(
             num_scalar_prefetch=2,
-            grid=(size, LOCAL),
+            grid=(size,),
             in_specs=[pl.BlockSpec(memory_space=pltpu.VMEM)] * (len(pieces) + 1)
-            + [per_block]
+            + [per_group]
             + [pl.BlockSpec(memory_space=pl.ANY)] * aliased,
-            out_specs=per_block,
+            out_specs=per_group,
             scratch_shapes=[
                 pltpu.VMEM((2, (SHARD_BLOCKS + REMOTE) * BLOCK, WIDTH), jnp.bfloat16),
-                pltpu.VMEM((BLOCK * SHARING, WIDTH), jnp.float32),
-                pltpu.VMEM((BLOCK * SHARING, WIDTH), jnp.float32),
+                pltpu.VMEM((ROWS * SHARING, WIDTH), jnp.float32),
+                pltpu.VMEM((ROWS * SHARING, WIDTH), jnp.float32),
             ],
         ),
         out_shape=jax.ShapeDtypeStruct(queries.shape, queries.dtype),
@@ -232,7 +225,7 @@
         cost_estimate=pl.CostEstimate(
             flops=size * 2**30, bytes_accessed=1, transcendentals=0
         ),
-        name=f"attend_{first + within}",
+        name=f"attend_{first}",
     )(*scalars, *pieces, picked, queries, *([earlier] if aliased else []))
 
 
@@ -249,12 +242,14 @@
     shards = lax.axis_size("blk")
     asked = lax.ppermute(wanted, "blk", [(i + 1, i) for i in range(shards - 1)])
 
-    def fetch(first, within, size, pieces):
-        chosen = pick_blocks(first, within, size, asked, pieces)
+    def choose(first, size, pieces, begins=(0,) * PIECES):
+        return pick_blocks(first, size, asked, pieces, begins)
+
+    def send(chosen):
         return lax.ppermute(chosen, "blk", [(i, i + 1) for i in range(shards - 1)])
 
-    def heads(first, within, size, pieces, arrived, earlier):
-        return attend(first, within, size, (lists, table), pieces, arrived, 0, queries, earlier)
+    def heads(first, size, pieces, arrived, earlier, begins=(0,) * PIECES):
+        return attend(first, size, (lists, table), pieces, begins, arrived, queries, earlier)
 
     swapped = over_heads(early, Y_SWAP)
     down, up = over_heads(most, X_UP), over_heads(most, X_DOWN)
@@ -274,32 +269,33 @@
             down[:, EARLY:],
         ]
     )
-    done = (swapped_down, swapped_up, far, late_swapped, row)
-
     swapped_far = over_heads(swapped_up, X_DOWN)
-    cross = [row, over_heads(after(row, *done), Y_SWAP)]
+    done = (swapped_down, far, late_swapped, row, swapped_far)
+    first = [most, swapped, up, swapped_up, far, swapped_far, down, swapped_down]
+    chosen = choose(0, EARLY, first)
+    arrived = send(chosen)
+
+    cross = [row, over_heads(after(row, chosen), Y_SWAP)]
     late_down, late_up = (over_heads(after(late, *done), route) for route in (X_UP, X_DOWN))
-    first = [most, swapped, up, swapped_up, far, swapped_far, down, swapped_down]
-    arrived = fetch(0, 0, EARLY, first)
-
-    late_swapped = after(late_swapped, late_down, late_up, swapped_far)
     late_swapped_down, late_swapped_up = (
-        over_heads(late_swapped, route) for route in (X_UP, X_DOWN)
+        over_heads(after(late_swapped, *done), route) for route in (X_UP, X_DOWN)
     )
-    result = heads(0, 0, EARLY, first, after(arrived, late_down, late_up), None)
-    done = (late_down, late_up, late_swapped_down, late_swapped_up)
-
+    result = heads(0, EARLY, first, arrived, None)
+
+    done = (late_down, late_up, late_swapped_down, late_swapped_up, result)
     late_far = over_heads(after(late_down, *done), X_UP)
     late_swapped_far = over_heads(after(late_swapped_up, *done), X_DOWN)
-    arrived = fetch(EARLY, 0, CROSS, cross)
-    result = heads(EARLY, 0, CROSS, cross, arrived, result)
-
+    cross[1] = after(cross[1], result)
+    cross_arrived = send(choose(EARLY, CROSS, cross))
     last = [late, late_swapped, late_up, late_swapped_up]
-    last += [after(late_far, result), late_swapped_far, late_down, late_swapped_down]
+    last += [late_far, late_swapped_far, late_down, late_swapped_down]
     begin, half = EARLY + CROSS, LATE // 2
-    arrived = [fetch(begin, 0, half, last), fetch(begin, half, LATE - half, last)]
-    result = heads(begin, 0, half, last, arrived[0], result)
-    return heads(begin, half, LATE - half, last, arrived[1], result)
+    chosen = choose(begin, half, last)
+    begins = (half,) * PIECES
+    chosen_more = choose(begin + half, LATE - half, last, begins)
+    result = heads(EARLY, CROSS, cross, after(cross_arrived, chosen, chosen_more), result)
+    result = heads(begin, half, last, send(chosen), result)
+    return heads(begin + half, LATE - half, last, send(chosen_more), result, begins)
 
 
 def solution(mesh):

time: 123 us -> 119 us (0.967)
  starting transfers between devices: 50.7 us -> 39.6 us
  waiting for transfers between devices: 25 us -> 32.6 us
  Pallas kernels: 44.1 us -> 42.3 us
    ppermute x16, starting transfers between devices: 26.6 us -> 19.9 us  [over_heads(): return lax.ppermute(array, 'heads', route)]
    ppermute x4, waiting for transfers between devices: 3.43 us -> 7.88 us  [send(): return lax.ppermute(chosen, 'blk', [(i, i + 1) for i in range(shards - 1)])]
    ppermute x4, starting transfers between devices: 21 us -> 16.6 us  [send(): return lax.ppermute(chosen, 'blk', [(i, i + 1) for i in range(shards - 1)])]
    ppermute x16, waiting for transfers between devices: 20.3 us -> 22.7 us  [over_heads(): return lax.ppermute(array, 'heads', route)]
    pallas_call x8, Pallas kernels: 37.2 us -> 35.4 us  [the longest x4 32.2 us: attend(): pl.pallas_call(functools.partial(attend_kernel, first, begins, aliased),...]
  transfers between devices with their start and end apart: 21 -> 21, of which waited for: 7 -> 8; matrix products, arithmetic and copies ran while one was open for 2% -> 2% of each run, Pallas kernels for 26% -> 27%
where the time goes in v3:
time: 119 us; the launch traced here: 118 us
  Pallas kernels  42.3 us (36%)
  starting transfers between devices  39.6 us (33%)
  waiting for transfers between devices  32.6 us (27%)
  local copies, waits for them, and re-layouts  2.12 us (2%)
    pallas_call x4, Pallas kernels, attend(): pl.pallas_call(functools.partial(attend_kernel, first, begins, aliased),...  32.2 us
    ppermute x16, waiting for transfers between devices, over_heads(): return lax.ppermute(array, 'heads', route)  22.7 us
    ppermute x16, starting transfers between devices, over_heads(): return lax.ppermute(array, 'heads', route)  19.9 us
    ppermute x4, starting transfers between devices, send(): return lax.ppermute(chosen, 'blk', [(i, i + 1) for i in range(shards - 1)])  16.6 us
    ppermute x4, waiting for transfers between devices, send(): return lax.ppermute(chosen, 'blk', [(i, i + 1) for i in range(shards - 1)])  7.88 us
    pallas_call x1, Pallas kernels, plan(): pl.pallas_call(plan_kernel, out_shape=[jax.ShapeDtypeStruct((KV * 2 * SHA...  4.23 us
    pallas_call x4, Pallas kernels, pick_blocks(): pl.pallas_call(functools.partial(pick_kernel, first, begins), grid_spec=p...  3.18 us
    ppermute x1, starting transfers between devices, on_device(): asked = lax.ppermute(wanted, 'blk', [(i + 1, i) for i in range(shards - 1)])  3.14 us
  transfers between devices with their start and end apart: 21, of which 8 were waited for; matrix products, arithmetic and copies ran while one was open for 2% of the time, Pallas kernels for 27%

profile of v3, /device:TPU:1, one launch (start us, length us, event | category | flops | bytes accessed | tf_op | source)
XLA Modules:
  0.0 117.6 jit_solution(12952574305200065964)
XLA Ops:
  0.0 2.7 %split_heads.1 = (bf16[2,4,256,128]{3,2,1,0:T(8,128)(2,1)}, bf16[2,2,256,128]{3,2,1,0:T(8,128)(2,1)}, bf16[2,4,256,128]{3,2,1,0:T(8,128)(2,1)}) custom-call(bf16[256,8,128]{2,1,0:T(8,128)(2,1)} %keys.1, bf16[256,8,128]{2,1,0:T(8,128)(2,1)} %values.1), custom_call_target="tpu_custom_call" | custom-call | flops 1 | bytes 1 | tf_op jit(solution)/shard_map/split_heads/pallas_call | solution.py:47
  2.7 3.3 %collective-permute-start.2 = (bf16[2,4,256,128]{3,2,1,0:T(8,128)(2,1)}, bf16[2,4,256,128]{3,2,1,0:T(8,128)(2,1)S(1)}, u32[]{:S(2)}, u32[]{:S(2)}) collective-permute-start(bf16[2,4,256,128]{3,2,1,0:T(8,128)(2,1)} %get-tuple-element.24.refs_0_), channel_id=1, source_target_pairs={{0,96},{16,112},{32,0},{48,16},{64,32},{80,48},{96,64},{112,80},{1... | collective-permute-start | bytes 1572872 | tf_op jit(solution)/shard_map/ppermute | solution.py:32
  6.0 0.0 collective-permute-start.1
  6.0 2.9 %collective-permute-start = (bf16[2,2,256,128]{3,2,1,0:T(8,128)(2,1)}, bf16[2,2,256,128]{3,2,1,0:T(8,128)(2,1)S(1)}, u32[]{:S(2)}, u32[]{:S(2)}) collective-permute-start(bf16[2,2,256,128]{3,2,1,0:T(8,128)(2,1)} %get-tuple-element.23), channel_id=1, source_target_pairs={{0,16},{16,0},{32,48},{48,32},{64,80},{80,64},{96,112},{112,96},{1... | collective-permute-start | bytes 786440 | tf_op jit(solution)/shard_map/ppermute | solution.py:32
  8.9 0.6 pad_add_fusion.where
  9.5 4.2 %plan.1 = (s32[257]{0:T(512)}, s32[32]{0:T(128)}) custom-call(s32[3]{0:T(128)} %pad_add_fusion.where, s32[2,8,64]{2,1,0:T(8,128)} %bitcast.12), custom_call_target="tpu_custom_call" | custom-call | flops 1 | bytes 1 | tf_op jit(solution)/shard_map/plan/pallas_call | solution.py:97
  13.7 3.1 %collective-permute-start.3 = (s32[32]{0:T(128)}, s32[32]{0:T(128)S(1)}, u32[]{:S(2)}, u32[]{:S(2)}) collective-permute-start(s32[32]{0:T(128)} %get-tuple-element.25), channel_id=1, source_target_pairs={{1,0},{2,1},{3,2},{4,3},{5,4},{6,5},{7,6},{8,7},{9,8},{10,9},{11,1... | collective-permute-start | bytes 392 | tf_op jit(solution)/shard_map/ppermute | solution.py:243
  16.9 2.1 %collective-permute-done.3.asked = s32[32]{0:T(128)S(1)} collective-permute-done((s32[32]{0:T(128)}, s32[32]{0:T(128)S(1)}, u32[]{:S(2)}, u32[]{:S(2)}) %collective-permute-start.3) | collective-permute-done | bytes 160 | tf_op jit(solution)/shard_map/ppermute | solution.py:243
  18.9 0.0 collective-permute-done.refs_1_
  19.0 0.0 collective-permute-done.2.refs_2_
  19.0 0.9 collective-permute-done.1.refs_6_
  19.9 1.6 %collective-permute-start.8 = (bf16[2,2,256,128]{3,2,1,0:T(8,128)(2,1)S(1)}, bf16[2,2,256,128]{3,2,1,0:T(8,128)(2,1)S(1)}, u32[]{:S(2)}, u32[]{:S(2)}) collective-permute-start(bf16[2,2,256,128]{3,2,1,0:T(8,128)(2,1)S(1)} %collective-permute-done.refs_1_), channel_id=1, source_target_pairs={{0,96},{16,112},{32,0},{48,16},{64,32},{80,48},{96,64},{112,80},{1... | collective-permute-start | bytes 786440 | tf_op jit(solution)/shard_map/ppermute | solution.py:32
  21.5 0.0 collective-permute-start.5
  21.5 0.0 copy-start.3
  21.5 0.0 copy-start.1
  21.5 0.0 copy-start
  21.5 0.1 collective-permute-start.6
  21.6 5.2 %collective-permute-done.8.refs_3_ = bf16[2,2,256,128]{3,2,1,0:T(8,128)(2,1)S(1)} collective-permute-done((bf16[2,2,256,128]{3,2,1,0:T(8,128)(2,1)S(1)}, bf16[2,2,256,128]{3,2,1,0:T(8,128)(2,1)S(1)}, u32[]{:S(2)}, u32[]{:S(2)}) %collective-permute-start.8) | collective-permute-done | bytes 262176 | tf_op jit(solution)/shard_map/ppermute | solution.py:32
  26.9 3.4 %collective-permute-start.9 = (bf16[2,2,256,128]{3,2,1,0:T(8,128)(2,1)S(1)}, bf16[2,2,256,128]{3,2,1,0:T(8,128)(2,1)S(1)}, u32[]{:S(2)}, u32[]{:S(2)}) collective-permute-start(bf16[2,2,256,128]{3,2,1,0:T(8,128)(2,1)S(1)} %collective-permute-done.8.refs_3_), channel_id=1, source_target_pairs={{0,96},{16,112},{32,0},{48,16},{64,32},{80,48},{96,64},{112,80},{1... | collective-permute-start | bytes 786440 | tf_op jit(solution)/shard_map/ppermute | solution.py:32
  30.3 1.0 slice_bitcast_fusion.2
  31.3 0.1 collective-permute-start.7
  31.4 0.8 collective-permute-start.4
  32.2 0.0 collective-permute-done.5.refs_7_
  32.2 6.2 %collective-permute-done.6.refs_4_ = bf16[2,3,256,128]{3,2,1,0:T(8,128)(2,1)S(1)} collective-permute-done((bf16[2,3,256,128]{3,2,1,0:T(8,128)(2,1)S(1)}, bf16[2,3,256,128]{3,2,1,0:T(8,128)(2,1)S(1)}, u32[]{:S(2)}, u32[]{:S(2)}) %collective-permute-start.6) | collective-permute-done | bytes 393248 | tf_op jit(solution)/shard_map/ppermute | solution.py:32
  38.4 0.0 collective-permute-done.9.refs_5_
  38.4 1.0 copy-done.2
  39.4 0.8 pick_blocks_0.1
  40.2 5.5 %collective-permute-start.14 = (bf16[2,2,512,128]{3,2,1,0:T(8,128)(2,1)S(1)}, bf16[2,2,512,128]{3,2,1,0:T(8,128)(2,1)S(1)}, u32[]{:S(2)}, u32[]{:S(2)}) collective-permute-start(bf16[2,2,512,128]{3,2,1,0:T(8,128)(2,1)S(1)} %pick_blocks_0.1), channel_id=1, source_target_pairs={{0,1},{1,2},{2,3},{3,4},{4,5},{5,6},{6,7},{7,8},{8,9},{9,10},{10,1... | collective-permute-start | bytes 1572872 | tf_op jit(solution)/shard_map/ppermute | solution.py:249
  45.8 0.0 collective-permute-done.7
  45.8 0.1 pad_maximum_fusion.refs_0_
  46.0 0.9 collective-permute-start.19
  46.9 0.0 collective-permute-done.4.refs_1_
  46.9 0.0 copy-done.1
  46.9 0.0 collective-permute-start.12
  46.9 2.7 %collective-permute-start.10 = (bf16[2,4,256,128]{3,2,1,0:T(8,128)(2,1)S(1)}, bf16[2,4,256,128]{3,2,1,0:T(8,128)(2,1)S(1)}, u32[]{:S(2)}, u32[]{:S(2)}) collective-permute-start(bf16[2,4,256,128]{3,2,1,0:T(8,128)(2,1)S(1)} %copy-done.1), channel_id=1, source_target_pairs={{0,96},{16,112},{32,0},{48,16},{64,32},{80,48},{96,64},{112,80},{1... | collective-permute-start | bytes 1572872 | tf_op jit(solution)/shard_map/ppermute | solution.py:32
  49.6 0.0 collective-permute-start.13
  49.6 7.9 %collective-permute-done.14.refs_8_ = bf16[2,2,512,128]{3,2,1,0:T(8,128)(2,1)S(1)} collective-permute-done((bf16[2,2,512,128]{3,2,1,0:T(8,128)(2,1)S(1)}, bf16[2,2,512,128]{3,2,1,0:T(8,128)(2,1)S(1)}, u32[]{:S(2)}, u32[]{:S(2)}) %collective-permute-start.14) | collective-permute-done | bytes 524320 | tf_op jit(solution)/shard_map/ppermute | solution.py:249
  57.4 1.5 %collective-permute-start.11 = (bf16[2,4,256,128]{3,2,1,0:T(8,128)(2,1)S(1)}, bf16[2,4,256,128]{3,2,1,0:T(8,128)(2,1)S(1)}, u32[]{:S(2)}, u32[]{:S(2)}) collective-permute-start(bf16[2,4,256,128]{3,2,1,0:T(8,128)(2,1)S(1)} %collective-permute-done.4.refs_1_), channel_id=1, source_target_pairs={{0,96},{16,112},{32,0},{48,16},{64,32},{80,48},{96,64},{112,80},{1... | collective-permute-start | bytes 1572872 | tf_op jit(solution)/shard_map/ppermute | solution.py:32
  58.9 0.0 copy-done.3
  58.9 0.0 copy-done.4
  58.9 0.0 copy-done.5
  58.9 0.0 copy-done
  58.9 8.0 %attend_0.1.refs_4_ = bf16[256,64,128]{2,1,0:T(8,128)(2,1)} custom-call(s32[2,8,64]{2,1,0:T(8,128)S(1)} %bitcast.13, s32[257]{0:T(512)S(1)} %copy-done.5, bf16[2,4,256,128]{3,2,1,0:T(8,128)(2,1)S(1)} %copy-done.3, bf16[2,2,256,128]{3,2,1,0:T(8,128)(2,1)S(1)} %collective-permute-done.refs_1_, bf16[2,4,256,128]{3,2,1,0:T(8,128)(2,1)S(1)} %collective-permute-done.2.refs_2_, ...), custom_call_target="tpu_custom_call" | custom-call | flops 2147483648 | bytes 1 | tf_op jit(solution)/shard_map/attend_0/pallas_call | solution.py:207
  67.0 0.0 collective-permute-done.12.refs_6_
  67.0 0.0 collective-permute-done.10.refs_2_
  67.0 5.2 %collective-permute-done.13.refs_7_ = bf16[2,4,256,128]{3,2,1,0:T(8,128)(2,1)S(1)} collective-permute-done((bf16[2,4,256,128]{3,2,1,0:T(8,128)(2,1)S(1)}, bf16[2,4,256,128]{3,2,1,0:T(8,128)(2,1)S(1)}, u32[]{:S(2)}, u32[]{:S(2)}) %collective-permute-start.13) | collective-permute-done | bytes 524320 | tf_op jit(solution)/shard_map/ppermute | solution.py:32
  72.2 0.0 collective-permute-done.11.refs_3_
  72.2 0.0 collective-permute-start.15
  72.2 2.7 %collective-permute-start.16 = (bf16[2,4,256,128]{3,2,1,0:T(8,128)(2,1)S(1)}, bf16[2,4,256,128]{3,2,1,0:T(8,128)(2,1)S(1)}, u32[]{:S(2)}, u32[]{:S(2)}) collective-permute-start(bf16[2,4,256,128]{3,2,1,0:T(8,128)(2,1)S(1)} %collective-permute-done.11.refs_3_), channel_id=1, source_target_pairs={{0,96},{16,112},{32,0},{48,16},{64,32},{80,48},{96,64},{112,80},{1... | collective-permute-start | bytes 1572872 | tf_op jit(solution)/shard_map/ppermute | solution.py:32
  74.9 0.7 collective-permute-done.19.refs_1_
  75.6 0.8 pick_blocks_2.1
  76.4 4.7 %collective-permute-start.20 = (bf16[2,2,512,128]{3,2,1,0:T(8,128)(2,1)S(1)}, bf16[2,2,512,128]{3,2,1,0:T(8,128)(2,1)S(1)}, u32[]{:S(2)}, u32[]{:S(2)}) collective-permute-start(bf16[2,2,512,128]{3,2,1,0:T(8,128)(2,1)S(1)} %pick_blocks_2.1), channel_id=1, source_target_pairs={{0,1},{1,2},{2,3},{3,4},{4,5},{5,6},{6,7},{7,8},{8,9},{9,10},{10,1... | collective-permute-start | bytes 1572872 | tf_op jit(solution)/shard_map/ppermute | solution.py:249
  81.1 4.3 %collective-permute-done.15.refs_4_ = bf16[2,4,256,128]{3,2,1,0:T(8,128)(2,1)S(1)} collective-permute-done((bf16[2,4,256,128]{3,2,1,0:T(8,128)(2,1)S(1)}, bf16[2,4,256,128]{3,2,1,0:T(8,128)(2,1)S(1)}, u32[]{:S(2)}, u32[]{:S(2)}) %collective-permute-start.15) | collective-permute-done | bytes 524320 | tf_op jit(solution)/shard_map/ppermute | solution.py:32
  85.4 0.0 collective-permute-done.16.refs_5_
  85.4 0.8 pick_blocks_4.1
  86.2 4.3 %collective-permute-start.18 = (bf16[2,2,512,128]{3,2,1,0:T(8,128)(2,1)S(1)}, bf16[2,2,512,128]{3,2,1,0:T(8,128)(2,1)S(1)}, u32[]{:S(2)}, u32[]{:S(2)}) collective-permute-start(bf16[2,2,512,128]{3,2,1,0:T(8,128)(2,1)S(1)} %pick_blocks_4.1), channel_id=1, source_target_pairs={{0,1},{1,2},{2,3},{3,4},{4,5},{5,6},{6,7},{7,8},{8,9},{9,10},{10,1... | collective-permute-start | bytes 1572872 | tf_op jit(solution)/shard_map/ppermute | solution.py:249
  90.5 0.8 pick_blocks_6.1
  91.3 2.1 %collective-permute-start.17 = (bf16[2,2,512,128]{3,2,1,0:T(8,128)(2,1)S(1)}, bf16[2,2,512,128]{3,2,1,0:T(8,128)(2,1)S(1)}, u32[]{:S(2)}, u32[]{:S(2)}) collective-permute-start(bf16[2,2,512,128]{3,2,1,0:T(8,128)(2,1)S(1)} %pick_blocks_6.1), channel_id=1, source_target_pairs={{0,1},{1,2},{2,3},{3,4},{4,5},{5,6},{6,7},{7,8},{8,9},{9,10},{10,1... | collective-permute-start | bytes 1572872 | tf_op jit(solution)/shard_map/ppermute | solution.py:249
  93.4 0.0 collective-permute-done.20.refs_2_
  93.4 8.1 %attend_2.1.refs_10_ = bf16[256,64,128]{2,1,0:T(8,128)(2,1)} custom-call(s32[2,8,64]{2,1,0:T(8,128)S(1)} %bitcast.14, s32[257]{0:T(512)S(1)} %copy-done.5, bf16[4,2,2,256,128]{4,3,2,1,0:T(8,128)(2,1)S(1)} %pad_maximum_fusion.refs_0_, bf16[4,2,2,256,128]{4,3,2,1,0:T(8,128)(2,1)S(1)} %collective-permute-done.19.refs_1_, ...), custom_call_target="tpu_custom_call", output_to_operand_aliasing={{}: (6, {})} | custom-call | flops 2147483648 | bytes 1 | tf_op jit(solution)/shard_map/attend_2/pallas_call | solution.py:207
  101.5 0.0 collective-permute-done.18.refs_8_
  101.5 8.0 %attend_4.1.refs_10_ = bf16[256,64,128]{2,1,0:T(8,128)(2,1)} custom-call(s32[2,8,64]{2,1,0:T(8,128)S(1)} %bitcast.15, s32[257]{0:T(512)S(1)} %copy-done.5, bf16[2,4,256,128]{3,2,1,0:T(8,128)(2,1)S(1)} %copy-done.1, bf16[2,4,256,128]{3,2,1,0:T(8,128)(2,1)S(1)} %collective-permute-done.4.refs_1_, ...), custom_call_target="tpu_custom_call", output_to_operand_aliasing={{}: (12, {})} | custom-call | flops 2147483648 | bytes 1 | tf_op jit(solution)/shard_map/attend_4/pallas_call | solution.py:207
  109.5 0.0 collective-permute-done.17.refs_8_
  109.5 8.0 %attend_6.1 = bf16[256,64,128]{2,1,0:T(8,128)(2,1)} custom-call(s32[2,8,64]{2,1,0:T(8,128)S(1)} %bitcast.16, s32[257]{0:T(512)S(1)} %copy-done.5, bf16[2,4,256,128]{3,2,1,0:T(8,128)(2,1)S(1)} %copy-done.1, bf16[2,4,256,128]{3,2,1,0:T(8,128)(2,1)S(1)} %collective-permute-done.4.refs_1_, ...), custom_call_target="tpu_custom_call", output_to_operand_aliasing={{}: (12, {})} | custom-call | flops 2147483648 | bytes 1 | tf_op jit(solution)/shard_map/attend_6/pallas_call | solution.py:207
  (9 shorter events, 0.1 us)
Async XLA Ops:
  2.7 16.3 %collective-permute-start.2 = (bf16[2,4,256,128]{3,2,1,0:T(8,128)(2,1)}, bf16[2,4,256,128]{3,2,1,0:T(8,128)(2,1)S(1)}, u32[]{:S(2)}, u32[]{:S(2)}) collective-permute-start(bf16[2,4,256,128]{3,2,1,0:T(8,128)(2,1)} %get-tuple-element.24.refs_0_), channel_id=1, source_target_pairs={{0,96},{16,112},{32,0},{48,16},{64,32},{80,48},{96,64},{112,80},{1... | collective-permute-start | bytes 1572872 | tf_op jit(solution)/shard_map/ppermute | solution.py:32
  6.0 13.9 %collective-permute-start.1 = (bf16[2,4,256,128]{3,2,1,0:T(8,128)(2,1)}, bf16[2,4,256,128]{3,2,1,0:T(8,128)(2,1)S(1)}, u32[]{:S(2)}, u32[]{:S(2)}) collective-permute-start(bf16[2,4,256,128]{3,2,1,0:T(8,128)(2,1)} %get-tuple-element.24.refs_0_), channel_id=1, source_target_pairs={{0,32},{16,48},{32,64},{48,80},{64,96},{80,112},{96,0},{112,16},{1... | collective-permute-start | bytes 1572872 | tf_op jit(solution)/shard_map/ppermute | solution.py:32
  6.0 12.9 %collective-permute-start = (bf16[2,2,256,128]{3,2,1,0:T(8,128)(2,1)}, bf16[2,2,256,128]{3,2,1,0:T(8,128)(2,1)S(1)}, u32[]{:S(2)}, u32[]{:S(2)}) collective-permute-start(bf16[2,2,256,128]{3,2,1,0:T(8,128)(2,1)} %get-tuple-element.23), channel_id=1, source_target_pairs={{0,16},{16,0},{32,48},{48,32},{64,80},{80,64},{96,112},{112,96},{1... | collective-permute-start | bytes 786440 | tf_op jit(solution)/shard_map/ppermute | solution.py:32
  13.7 5.2 %collective-permute-start.3 = (s32[32]{0:T(128)}, s32[32]{0:T(128)S(1)}, u32[]{:S(2)}, u32[]{:S(2)}) collective-permute-start(s32[32]{0:T(128)} %get-tuple-element.25), channel_id=1, source_target_pairs={{1,0},{2,1},{3,2},{4,3},{5,4},{6,5},{7,6},{8,7},{9,8},{10,9},{11,1... | collective-permute-start | bytes 392 | tf_op jit(solution)/shard_map/ppermute | solution.py:243
  19.9 7.0 %collective-permute-start.8 = (bf16[2,2,256,128]{3,2,1,0:T(8,128)(2,1)S(1)}, bf16[2,2,256,128]{3,2,1,0:T(8,128)(2,1)S(1)}, u32[]{:S(2)}, u32[]{:S(2)}) collective-permute-start(bf16[2,2,256,128]{3,2,1,0:T(8,128)(2,1)S(1)} %collective-permute-done.refs_1_), channel_id=1, source_target_pairs={{0,96},{16,112},{32,0},{48,16},{64,32},{80,48},{96,64},{112,80},{1... | collective-permute-start | bytes 786440 | tf_op jit(solution)/shard_map/ppermute | solution.py:32
  21.5 10.7 %collective-permute-start.5 = (bf16[2,2,256,128]{3,2,1,0:T(8,128)(2,1)S(1)}, bf16[2,2,256,128]{3,2,1,0:T(8,128)(2,1)S(1)}, u32[]{:S(2)}, u32[]{:S(2)}) collective-permute-start(bf16[2,2,256,128]{3,2,1,0:T(8,128)(2,1)S(1)} %collective-permute-done.refs_1_), channel_id=1, source_target_pairs={{0,32},{16,48},{32,64},{48,80},{64,96},{80,112},{96,0},{112,16},{1... | collective-permute-start | bytes 786440 | tf_op jit(solution)/shard_map/ppermute | solution.py:32
  21.5 37.4 %copy-start.3 = (bf16[2,4,256,128]{3,2,1,0:T(8,128)(2,1)S(1)}, bf16[2,4,256,128]{3,2,1,0:T(8,128)(2,1)}, u32[]{:S(2)}) copy-start(bf16[2,4,256,128]{3,2,1,0:T(8,128)(2,1)} %get-tuple-element.24.refs_0_) | copy-start | bytes 1572868
  21.5 37.4 %copy-start.4 = (s32[2,64,8]{1,2,0:T(8,128)S(1)}, s32[2,64,8]{1,2,0:T(8,128)}, u32[]{:S(2)}) copy-start(s32[2,64,8]{1,2,0:T(8,128)} %param.7) | copy-start | bytes 12292
  21.5 37.4 %copy-start.5 = (s32[257]{0:T(512)S(1)}, s32[257]{0:T(512)}, u32[]{:S(2)}) copy-start(s32[257]{0:T(512)} %get-tuple-element.21.places) | copy-start | bytes 3088
  21.5 25.4 %copy-start.1 = (bf16[2,4,256,128]{3,2,1,0:T(8,128)(2,1)S(1)}, bf16[2,4,256,128]{3,2,1,0:T(8,128)(2,1)}, u32[]{:S(2)}) copy-start(bf16[2,4,256,128]{3,2,1,0:T(8,128)(2,1)} %get-tuple-element.30.refs_0_) | copy-start | bytes 1572868
  21.5 37.4 %copy-start = (bf16[256,64,128]{2,1,0:T(8,128)(2,1)S(1)}, bf16[256,64,128]{2,1,0:T(8,128)(2,1)}, u32[]{:S(2)}) copy-start(bf16[256,64,128]{2,1,0:T(8,128)(2,1)} %refs_9_.5) | copy-start | bytes 12582916
  21.5 16.8 %collective-permute-start.6 = (bf16[2,3,256,128]{3,2,1,0:T(8,128)(2,1)S(1)}, bf16[2,3,256,128]{3,2,1,0:T(8,128)(2,1)S(1)}, u32[]{:S(2)}, u32[]{:S(2)}) collective-permute-start(bf16[2,3,256,128]{3,2,1,0:T(8,128)(2,1)S(1)} %slice.24), channel_id=1, source_target_pairs={{0,32},{16,48},{32,64},{48,80},{64,96},{80,112},{96,0},{112,16},{1... | collective-permute-start | bytes 1179656 | tf_op jit(solution)/shard_map/ppermute | solution.py:32
  26.9 11.5 %collective-permute-start.9 = (bf16[2,2,256,128]{3,2,1,0:T(8,128)(2,1)S(1)}, bf16[2,2,256,128]{3,2,1,0:T(8,128)(2,1)S(1)}, u32[]{:S(2)}, u32[]{:S(2)}) collective-permute-start(bf16[2,2,256,128]{3,2,1,0:T(8,128)(2,1)S(1)} %collective-permute-done.8.refs_3_), channel_id=1, source_target_pairs={{0,96},{16,112},{32,0},{48,16},{64,32},{80,48},{96,64},{112,80},{1... | collective-permute-start | bytes 786440 | tf_op jit(solution)/shard_map/ppermute | solution.py:32
  31.3 14.5 %collective-permute-start.7 = (bf16[2,1,256,128]{3,2,1,0:T(8,128)(2,1)S(1)}, bf16[2,1,256,128]{3,2,1,0:T(8,128)(2,1)S(1)}, u32[]{:S(2)}, u32[]{:S(2)}) collective-permute-start(bf16[2,1,256,128]{3,2,1,0:T(8,128)(2,1)S(1)} %slice.27), channel_id=1, source_target_pairs={{0,96},{16,112},{32,0},{48,16},{64,32},{80,48},{96,64},{112,80},{1... | collective-permute-start | bytes 393224 | tf_op jit(solution)/shard_map/ppermute | solution.py:32
  31.4 15.5 %collective-permute-start.4 = (bf16[2,4,256,128]{3,2,1,0:T(8,128)(2,1)}, bf16[2,4,256,128]{3,2,1,0:T(8,128)(2,1)S(1)}, u32[]{:S(2)}, u32[]{:S(2)}) collective-permute-start(bf16[2,4,256,128]{3,2,1,0:T(8,128)(2,1)} %get-tuple-element.30.refs_0_), channel_id=1, source_target_pairs={{0,16},{16,0},{32,48},{48,32},{64,80},{80,64},{96,112},{112,96},{1... | collective-permute-start | bytes 1572872 | tf_op jit(solution)/shard_map/ppermute | solution.py:32
  38.4 1.0 copy-start.2
  40.2 17.2 %collective-permute-start.14 = (bf16[2,2,512,128]{3,2,1,0:T(8,128)(2,1)S(1)}, bf16[2,2,512,128]{3,2,1,0:T(8,128)(2,1)S(1)}, u32[]{:S(2)}, u32[]{:S(2)}) collective-permute-start(bf16[2,2,512,128]{3,2,1,0:T(8,128)(2,1)S(1)} %pick_blocks_0.1), channel_id=1, source_target_pairs={{0,1},{1,2},{2,3},{3,4},{4,5},{5,6},{6,7},{7,8},{8,9},{9,10},{10,1... | collective-permute-start | bytes 1572872 | tf_op jit(solution)/shard_map/ppermute | solution.py:249
  46.0 29.6 %collective-permute-start.19 = (bf16[4,2,2,256,128]{4,3,2,1,0:T(8,128)(2,1)S(1)}, bf16[4,2,2,256,128]{4,3,2,1,0:T(8,128)(2,1)S(1)}, u32[]{:S(2)}, u32[]{:S(2)}) collective-permute-start(bf16[4,2,2,256,128]{4,3,2,1,0:T(8,128)(2,1)S(1)} %pad_maximum_fusion.refs_0_), channel_id=1, source_target_pairs={{0,16},{16,0},{32,48},{48,32},{64,80},{80,64},{96,112},{112,96},{1... | collective-permute-start | bytes 3145736 | tf_op jit(solution)/shard_map/ppermute | solution.py:32
  46.9 20.1 %collective-permute-start.12 = (bf16[2,4,256,128]{3,2,1,0:T(8,128)(2,1)S(1)}, bf16[2,4,256,128]{3,2,1,0:T(8,128)(2,1)S(1)}, u32[]{:S(2)}, u32[]{:S(2)}) collective-permute-start(bf16[2,4,256,128]{3,2,1,0:T(8,128)(2,1)S(1)} %copy-done.1), channel_id=1, source_target_pairs={{0,32},{16,48},{32,64},{48,80},{64,96},{80,112},{96,0},{112,16},{1... | collective-permute-start | bytes 1572872 | tf_op jit(solution)/shard_map/ppermute | solution.py:32
  46.9 20.1 %collective-permute-start.10 = (bf16[2,4,256,128]{3,2,1,0:T(8,128)(2,1)S(1)}, bf16[2,4,256,128]{3,2,1,0:T(8,128)(2,1)S(1)}, u32[]{:S(2)}, u32[]{:S(2)}) collective-permute-start(bf16[2,4,256,128]{3,2,1,0:T(8,128)(2,1)S(1)} %copy-done.1), channel_id=1, source_target_pairs={{0,96},{16,112},{32,0},{48,16},{64,32},{80,48},{96,64},{112,80},{1... | collective-permute-start | bytes 1572872 | tf_op jit(solution)/shard_map/ppermute | solution.py:32
  49.6 22.6 %collective-permute-start.13 = (bf16[2,4,256,128]{3,2,1,0:T(8,128)(2,1)S(1)}, bf16[2,4,256,128]{3,2,1,0:T(8,128)(2,1)S(1)}, u32[]{:S(2)}, u32[]{:S(2)}) collective-permute-start(bf16[2,4,256,128]{3,2,1,0:T(8,128)(2,1)S(1)} %collective-permute-done.4.refs_1_), channel_id=1, source_target_pairs={{0,32},{16,48},{32,64},{48,80},{64,96},{80,112},{96,0},{112,16},{1... | collective-permute-start | bytes 1572872 | tf_op jit(solution)/shard_map/ppermute | solution.py:32
  57.4 14.8 %collective-permute-start.11 = (bf16[2,4,256,128]{3,2,1,0:T(8,128)(2,1)S(1)}, bf16[2,4,256,128]{3,2,1,0:T(8,128)(2,1)S(1)}, u32[]{:S(2)}, u32[]{:S(2)}) collective-permute-start(bf16[2,4,256,128]{3,2,1,0:T(8,128)(2,1)S(1)} %collective-permute-done.4.refs_1_), channel_id=1, source_target_pairs={{0,96},{16,112},{32,0},{48,16},{64,32},{80,48},{96,64},{112,80},{1... | collective-permute-start | bytes 1572872 | tf_op jit(solution)/shard_map/ppermute | solution.py:32
  72.2 13.2 %collective-permute-start.15 = (bf16[2,4,256,128]{3,2,1,0:T(8,128)(2,1)S(1)}, bf16[2,4,256,128]{3,2,1,0:T(8,128)(2,1)S(1)}, u32[]{:S(2)}, u32[]{:S(2)}) collective-permute-start(bf16[2,4,256,128]{3,2,1,0:T(8,128)(2,1)S(1)} %collective-permute-done.12.refs_6_), channel_id=1, source_target_pairs={{0,32},{16,48},{32,64},{48,80},{64,96},{80,112},{96,0},{112,16},{1... | collective-permute-start | bytes 1572872 | tf_op jit(solution)/shard_map/ppermute | solution.py:32
  72.2 13.2 %collective-permute-start.16 = (bf16[2,4,256,128]{3,2,1,0:T(8,128)(2,1)S(1)}, bf16[2,4,256,128]{3,2,1,0:T(8,128)(2,1)S(1)}, u32[]{:S(2)}, u32[]{:S(2)}) collective-permute-start(bf16[2,4,256,128]{3,2,1,0:T(8,128)(2,1)S(1)} %collective-permute-done.11.refs_3_), channel_id=1, source_target_pairs={{0,96},{16,112},{32,0},{48,16},{64,32},{80,48},{96,64},{112,80},{1... | collective-permute-start | bytes 1572872 | tf_op jit(solution)/shard_map/ppermute | solution.py:32
  76.4 17.0 %collective-permute-start.20 = (bf16[2,2,512,128]{3,2,1,0:T(8,128)(2,1)S(1)}, bf16[2,2,512,128]{3,2,1,0:T(8,128)(2,1)S(1)}, u32[]{:S(2)}, u32[]{:S(2)}) collective-permute-start(bf16[2,2,512,128]{3,2,1,0:T(8,128)(2,1)S(1)} %pick_blocks_2.1), channel_id=1, source_target_pairs={{0,1},{1,2},{2,3},{3,4},{4,5},{5,6},{6,7},{7,8},{8,9},{9,10},{10,1... | collective-permute-start | bytes 1572872 | tf_op jit(solution)/shard_map/ppermute | solution.py:249
  86.2 15.3 %collective-permute-start.18 = (bf16[2,2,512,128]{3,2,1,0:T(8,128)(2,1)S(1)}, bf16[2,2,512,128]{3,2,1,0:T(8,128)(2,1)S(1)}, u32[]{:S(2)}, u32[]{:S(2)}) collective-permute-start(bf16[2,2,512,128]{3,2,1,0:T(8,128)(2,1)S(1)} %pick_blocks_4.1), channel_id=1, source_target_pairs={{0,1},{1,2},{2,3},{3,4},{4,5},{5,6},{6,7},{7,8},{8,9},{9,10},{10,1... | collective-permute-start | bytes 1572872 | tf_op jit(solution)/shard_map/ppermute | solution.py:249
  91.3 18.2 %collective-permute-start.17 = (bf16[2,2,512,128]{3,2,1,0:T(8,128)(2,1)S(1)}, bf16[2,2,512,128]{3,2,1,0:T(8,128)(2,1)S(1)}, u32[]{:S(2)}, u32[]{:S(2)}) collective-permute-start(bf16[2,2,512,128]{3,2,1,0:T(8,128)(2,1)S(1)} %pick_blocks_6.1), channel_id=1, source_target_pairs={{0,1},{1,2},{2,3},{3,4},{4,5},{5,6},{6,7},{7,8},{8,9},{9,10},{10,1... | collective-permute-start | bytes 1572872 | tf_op jit(solution)/shard_map/ppermute | solution.py:249

commit v4 on v3

--- a/solution.py
+++ b/solution.py
@@ -142,7 +142,7 @@
         ),
         out_shape=jax.ShapeDtypeStruct((2, size, REMOTE * BLOCK, WIDTH), jnp.bfloat16),
         cost_estimate=pl.CostEstimate(flops=1, bytes_accessed=1, transcendentals=0),
-        compiler_params=pltpu.CompilerParams(vmem_limit_bytes=16 * 2**20),
+        compiler_params=pltpu.CompilerParams(vmem_limit_bytes=8 * 2**20),
         name=f"pick_blocks_{first}",
     )(asked, *pieces)
 

time: 119 us -> 119 us (level)
  no operation moved by 1% of the time
where the time goes in v4:
time: 119 us; the launch traced here: 118 us
  Pallas kernels  42.3 us (36%)
  starting transfers between devices  39.6 us (33%)
  waiting for transfers between devices  32.6 us (27%)
  local copies, waits for them, and re-layouts  2.12 us (2%)
    pallas_call x4, Pallas kernels, attend(): pl.pallas_call(functools.partial(attend_kernel, first, begins, aliased),...  32.2 us
    ppermute x16, waiting for transfers between devices, over_heads(): return lax.ppermute(array, 'heads', route)  22.7 us
    ppermute x16, starting transfers between devices, over_heads(): return lax.ppermute(array, 'heads', route)  19.9 us
    ppermute x4, starting transfers between devices, send(): return lax.ppermute(chosen, 'blk', [(i, i + 1) for i in range(shards - 1)])  16.6 us
    ppermute x4, waiting for transfers between devices, send(): return lax.ppermute(chosen, 'blk', [(i, i + 1) for i in range(shards - 1)])  7.88 us
    pallas_call x1, Pallas kernels, plan(): pl.pallas_call(plan_kernel, out_shape=[jax.ShapeDtypeStruct((KV * 2 * SHA...  4.23 us
    pallas_call x4, Pallas kernels, pick_blocks(): pl.pallas_call(functools.partial(pick_kernel, first, begins), grid_spec=p...  3.18 us
    ppermute x1, starting transfers between devices, on_device(): asked = lax.ppermute(wanted, 'blk', [(i + 1, i) for i in range(shards - 1)])  3.14 us
  transfers between devices with their start and end apart: 21, of which 8 were waited for; matrix products, arithmetic and copies ran while one was open for 2% of the time, Pallas kernels for 27%

profile of v4, /device:TPU:1, one launch (start us, length us, event | category | flops | bytes accessed | tf_op | source)
XLA Modules:
  0.0 117.6 jit_solution(8614348123287464242)
XLA Ops:
  0.0 2.7 %split_heads.1 = (bf16[2,4,256,128]{3,2,1,0:T(8,128)(2,1)}, bf16[2,2,256,128]{3,2,1,0:T(8,128)(2,1)}, bf16[2,4,256,128]{3,2,1,0:T(8,128)(2,1)}) custom-call(bf16[256,8,128]{2,1,0:T(8,128)(2,1)} %keys.1, bf16[256,8,128]{2,1,0:T(8,128)(2,1)} %values.1), custom_call_target="tpu_custom_call" | custom-call | flops 1 | bytes 1 | tf_op jit(solution)/shard_map/split_heads/pallas_call | solution.py:47
  2.7 3.3 %collective-permute-start.2 = (bf16[2,4,256,128]{3,2,1,0:T(8,128)(2,1)}, bf16[2,4,256,128]{3,2,1,0:T(8,128)(2,1)S(1)}, u32[]{:S(2)}, u32[]{:S(2)}) collective-permute-start(bf16[2,4,256,128]{3,2,1,0:T(8,128)(2,1)} %get-tuple-element.24.refs_0_), channel_id=1, source_target_pairs={{0,96},{16,112},{32,0},{48,16},{64,32},{80,48},{96,64},{112,80},{1... | collective-permute-start | bytes 1572872 | tf_op jit(solution)/shard_map/ppermute | solution.py:32
  6.0 0.0 collective-permute-start.1
  6.0 2.9 %collective-permute-start = (bf16[2,2,256,128]{3,2,1,0:T(8,128)(2,1)}, bf16[2,2,256,128]{3,2,1,0:T(8,128)(2,1)S(1)}, u32[]{:S(2)}, u32[]{:S(2)}) collective-permute-start(bf16[2,2,256,128]{3,2,1,0:T(8,128)(2,1)} %get-tuple-element.23), channel_id=1, source_target_pairs={{0,16},{16,0},{32,48},{48,32},{64,80},{80,64},{96,112},{112,96},{1... | collective-permute-start | bytes 786440 | tf_op jit(solution)/shard_map/ppermute | solution.py:32
  8.9 0.6 pad_add_fusion.where
  9.5 4.2 %plan.1 = (s32[257]{0:T(512)}, s32[32]{0:T(128)}) custom-call(s32[3]{0:T(128)} %pad_add_fusion.where, s32[2,8,64]{2,1,0:T(8,128)} %bitcast.12), custom_call_target="tpu_custom_call" | custom-call | flops 1 | bytes 1 | tf_op jit(solution)/shard_map/plan/pallas_call | solution.py:97
  13.7 3.1 %collective-permute-start.3 = (s32[32]{0:T(128)}, s32[32]{0:T(128)S(1)}, u32[]{:S(2)}, u32[]{:S(2)}) collective-permute-start(s32[32]{0:T(128)} %get-tuple-element.25), channel_id=1, source_target_pairs={{1,0},{2,1},{3,2},{4,3},{5,4},{6,5},{7,6},{8,7},{9,8},{10,9},{11,1... | collective-permute-start | bytes 392 | tf_op jit(solution)/shard_map/ppermute | solution.py:243
  16.9 2.1 %collective-permute-done.3.asked = s32[32]{0:T(128)S(1)} collective-permute-done((s32[32]{0:T(128)}, s32[32]{0:T(128)S(1)}, u32[]{:S(2)}, u32[]{:S(2)}) %collective-permute-start.3) | collective-permute-done | bytes 160 | tf_op jit(solution)/shard_map/ppermute | solution.py:243
  18.9 0.0 collective-permute-done.refs_1_
  19.0 0.0 collective-permute-done.2.refs_2_
  19.0 0.9 collective-permute-done.1.refs_6_
  19.9 1.6 %collective-permute-start.8 = (bf16[2,2,256,128]{3,2,1,0:T(8,128)(2,1)S(1)}, bf16[2,2,256,128]{3,2,1,0:T(8,128)(2,1)S(1)}, u32[]{:S(2)}, u32[]{:S(2)}) collective-permute-start(bf16[2,2,256,128]{3,2,1,0:T(8,128)(2,1)S(1)} %collective-permute-done.refs_1_), channel_id=1, source_target_pairs={{0,96},{16,112},{32,0},{48,16},{64,32},{80,48},{96,64},{112,80},{1... | collective-permute-start | bytes 786440 | tf_op jit(solution)/shard_map/ppermute | solution.py:32
  21.5 0.0 collective-permute-start.5
  21.5 0.0 copy-start.3
  21.5 0.0 copy-start.1
  21.5 0.0 copy-start
  21.5 0.1 collective-permute-start.6
  21.6 5.2 %collective-permute-done.8.refs_3_ = bf16[2,2,256,128]{3,2,1,0:T(8,128)(2,1)S(1)} collective-permute-done((bf16[2,2,256,128]{3,2,1,0:T(8,128)(2,1)S(1)}, bf16[2,2,256,128]{3,2,1,0:T(8,128)(2,1)S(1)}, u32[]{:S(2)}, u32[]{:S(2)}) %collective-permute-start.8) | collective-permute-done | bytes 262176 | tf_op jit(solution)/shard_map/ppermute | solution.py:32
  26.9 3.4 %collective-permute-start.9 = (bf16[2,2,256,128]{3,2,1,0:T(8,128)(2,1)S(1)}, bf16[2,2,256,128]{3,2,1,0:T(8,128)(2,1)S(1)}, u32[]{:S(2)}, u32[]{:S(2)}) collective-permute-start(bf16[2,2,256,128]{3,2,1,0:T(8,128)(2,1)S(1)} %collective-permute-done.8.refs_3_), channel_id=1, source_target_pairs={{0,96},{16,112},{32,0},{48,16},{64,32},{80,48},{96,64},{112,80},{1... | collective-permute-start | bytes 786440 | tf_op jit(solution)/shard_map/ppermute | solution.py:32
  30.3 1.0 slice_bitcast_fusion.2
  31.3 0.1 collective-permute-start.7
  31.4 0.8 collective-permute-start.4
  32.2 0.0 collective-permute-done.5.refs_7_
  32.2 6.2 %collective-permute-done.6.refs_4_ = bf16[2,3,256,128]{3,2,1,0:T(8,128)(2,1)S(1)} collective-permute-done((bf16[2,3,256,128]{3,2,1,0:T(8,128)(2,1)S(1)}, bf16[2,3,256,128]{3,2,1,0:T(8,128)(2,1)S(1)}, u32[]{:S(2)}, u32[]{:S(2)}) %collective-permute-start.6) | collective-permute-done | bytes 393248 | tf_op jit(solution)/shard_map/ppermute | solution.py:32
  38.4 0.0 collective-permute-done.9.refs_5_
  38.4 1.0 copy-done.2
  39.4 0.8 pick_blocks_0.1
  40.2 5.5 %collective-permute-start.14 = (bf16[2,2,512,128]{3,2,1,0:T(8,128)(2,1)S(1)}, bf16[2,2,512,128]{3,2,1,0:T(8,128)(2,1)S(1)}, u32[]{:S(2)}, u32[]{:S(2)}) collective-permute-start(bf16[2,2,512,128]{3,2,1,0:T(8,128)(2,1)S(1)} %pick_blocks_0.1), channel_id=1, source_target_pairs={{0,1},{1,2},{2,3},{3,4},{4,5},{5,6},{6,7},{7,8},{8,9},{9,10},{10,1... | collective-permute-start | bytes 1572872 | tf_op jit(solution)/shard_map/ppermute | solution.py:249
  45.8 0.0 collective-permute-done.7
  45.8 0.1 pad_maximum_fusion.refs_0_
  46.0 0.9 collective-permute-start.19
  46.9 0.0 collective-permute-done.4.refs_1_
  46.9 0.0 copy-done.1
  46.9 0.0 collective-permute-start.12
  46.9 2.7 %collective-permute-start.10 = (bf16[2,4,256,128]{3,2,1,0:T(8,128)(2,1)S(1)}, bf16[2,4,256,128]{3,2,1,0:T(8,128)(2,1)S(1)}, u32[]{:S(2)}, u32[]{:S(2)}) collective-permute-start(bf16[2,4,256,128]{3,2,1,0:T(8,128)(2,1)S(1)} %copy-done.1), channel_id=1, source_target_pairs={{0,96},{16,112},{32,0},{48,16},{64,32},{80,48},{96,64},{112,80},{1... | collective-permute-start | bytes 1572872 | tf_op jit(solution)/shard_map/ppermute | solution.py:32
  49.6 0.0 collective-permute-start.13
  49.6 7.9 %collective-permute-done.14.refs_8_ = bf16[2,2,512,128]{3,2,1,0:T(8,128)(2,1)S(1)} collective-permute-done((bf16[2,2,512,128]{3,2,1,0:T(8,128)(2,1)S(1)}, bf16[2,2,512,128]{3,2,1,0:T(8,128)(2,1)S(1)}, u32[]{:S(2)}, u32[]{:S(2)}) %collective-permute-start.14) | collective-permute-done | bytes 524320 | tf_op jit(solution)/shard_map/ppermute | solution.py:249
  57.4 1.5 %collective-permute-start.11 = (bf16[2,4,256,128]{3,2,1,0:T(8,128)(2,1)S(1)}, bf16[2,4,256,128]{3,2,1,0:T(8,128)(2,1)S(1)}, u32[]{:S(2)}, u32[]{:S(2)}) collective-permute-start(bf16[2,4,256,128]{3,2,1,0:T(8,128)(2,1)S(1)} %collective-permute-done.4.refs_1_), channel_id=1, source_target_pairs={{0,96},{16,112},{32,0},{48,16},{64,32},{80,48},{96,64},{112,80},{1... | collective-permute-start | bytes 1572872 | tf_op jit(solution)/shard_map/ppermute | solution.py:32
  58.9 0.0 copy-done.3
  58.9 0.0 copy-done.4
  58.9 0.0 copy-done.5
  58.9 0.0 copy-done
  58.9 8.0 %attend_0.1.refs_4_ = bf16[256,64,128]{2,1,0:T(8,128)(2,1)} custom-call(s32[2,8,64]{2,1,0:T(8,128)S(1)} %bitcast.13, s32[257]{0:T(512)S(1)} %copy-done.5, bf16[2,4,256,128]{3,2,1,0:T(8,128)(2,1)S(1)} %copy-done.3, bf16[2,2,256,128]{3,2,1,0:T(8,128)(2,1)S(1)} %collective-permute-done.refs_1_, bf16[2,4,256,128]{3,2,1,0:T(8,128)(2,1)S(1)} %collective-permute-done.2.refs_2_, ...), custom_call_target="tpu_custom_call" | custom-call | flops 2147483648 | bytes 1 | tf_op jit(solution)/shard_map/attend_0/pallas_call | solution.py:207
  67.0 0.0 collective-permute-done.12.refs_6_
  67.0 0.0 collective-permute-done.10.refs_2_
  67.0 5.2 %collective-permute-done.13.refs_7_ = bf16[2,4,256,128]{3,2,1,0:T(8,128)(2,1)S(1)} collective-permute-done((bf16[2,4,256,128]{3,2,1,0:T(8,128)(2,1)S(1)}, bf16[2,4,256,128]{3,2,1,0:T(8,128)(2,1)S(1)}, u32[]{:S(2)}, u32[]{:S(2)}) %collective-permute-start.13) | collective-permute-done | bytes 524320 | tf_op jit(solution)/shard_map/ppermute | solution.py:32
  72.2 0.0 collective-permute-done.11.refs_3_
  72.2 0.0 collective-permute-start.15
  72.2 2.7 %collective-permute-start.16 = (bf16[2,4,256,128]{3,2,1,0:T(8,128)(2,1)S(1)}, bf16[2,4,256,128]{3,2,1,0:T(8,128)(2,1)S(1)}, u32[]{:S(2)}, u32[]{:S(2)}) collective-permute-start(bf16[2,4,256,128]{3,2,1,0:T(8,128)(2,1)S(1)} %collective-permute-done.11.refs_3_), channel_id=1, source_target_pairs={{0,96},{16,112},{32,0},{48,16},{64,32},{80,48},{96,64},{112,80},{1... | collective-permute-start | bytes 1572872 | tf_op jit(solution)/shard_map/ppermute | solution.py:32
  74.9 0.7 collective-permute-done.19.refs_1_
  75.6 0.8 pick_blocks_2.1
  76.4 4.7 %collective-permute-start.20 = (bf16[2,2,512,128]{3,2,1,0:T(8,128)(2,1)S(1)}, bf16[2,2,512,128]{3,2,1,0:T(8,128)(2,1)S(1)}, u32[]{:S(2)}, u32[]{:S(2)}) collective-permute-start(bf16[2,2,512,128]{3,2,1,0:T(8,128)(2,1)S(1)} %pick_blocks_2.1), channel_id=1, source_target_pairs={{0,1},{1,2},{2,3},{3,4},{4,5},{5,6},{6,7},{7,8},{8,9},{9,10},{10,1... | collective-permute-start | bytes 1572872 | tf_op jit(solution)/shard_map/ppermute | solution.py:249
  81.1 4.3 %collective-permute-done.15.refs_4_ = bf16[2,4,256,128]{3,2,1,0:T(8,128)(2,1)S(1)} collective-permute-done((bf16[2,4,256,128]{3,2,1,0:T(8,128)(2,1)S(1)}, bf16[2,4,256,128]{3,2,1,0:T(8,128)(2,1)S(1)}, u32[]{:S(2)}, u32[]{:S(2)}) %collective-permute-start.15) | collective-permute-done | bytes 524320 | tf_op jit(solution)/shard_map/ppermute | solution.py:32
  85.4 0.0 collective-permute-done.16.refs_5_
  85.4 0.8 pick_blocks_4.1
  86.2 4.3 %collective-permute-start.18 = (bf16[2,2,512,128]{3,2,1,0:T(8,128)(2,1)S(1)}, bf16[2,2,512,128]{3,2,1,0:T(8,128)(2,1)S(1)}, u32[]{:S(2)}, u32[]{:S(2)}) collective-permute-start(bf16[2,2,512,128]{3,2,1,0:T(8,128)(2,1)S(1)} %pick_blocks_4.1), channel_id=1, source_target_pairs={{0,1},{1,2},{2,3},{3,4},{4,5},{5,6},{6,7},{7,8},{8,9},{9,10},{10,1... | collective-permute-start | bytes 1572872 | tf_op jit(solution)/shard_map/ppermute | solution.py:249
  90.5 0.8 pick_blocks_6.1
  91.3 2.1 %collective-permute-start.17 = (bf16[2,2,512,128]{3,2,1,0:T(8,128)(2,1)S(1)}, bf16[2,2,512,128]{3,2,1,0:T(8,128)(2,1)S(1)}, u32[]{:S(2)}, u32[]{:S(2)}) collective-permute-start(bf16[2,2,512,128]{3,2,1,0:T(8,128)(2,1)S(1)} %pick_blocks_6.1), channel_id=1, source_target_pairs={{0,1},{1,2},{2,3},{3,4},{4,5},{5,6},{6,7},{7,8},{8,9},{9,10},{10,1... | collective-permute-start | bytes 1572872 | tf_op jit(solution)/shard_map/ppermute | solution.py:249
  93.4 0.0 collective-permute-done.20.refs_2_
  93.4 8.0 %attend_2.1.refs_10_ = bf16[256,64,128]{2,1,0:T(8,128)(2,1)} custom-call(s32[2,8,64]{2,1,0:T(8,128)S(1)} %bitcast.14, s32[257]{0:T(512)S(1)} %copy-done.5, bf16[4,2,2,256,128]{4,3,2,1,0:T(8,128)(2,1)S(1)} %pad_maximum_fusion.refs_0_, bf16[4,2,2,256,128]{4,3,2,1,0:T(8,128)(2,1)S(1)} %collective-permute-done.19.refs_1_, ...), custom_call_target="tpu_custom_call", output_to_operand_aliasing={{}: (6, {})} | custom-call | flops 2147483648 | bytes 1 | tf_op jit(solution)/shard_map/attend_2/pallas_call | solution.py:207
  101.5 0.0 collective-permute-done.18.refs_8_
  101.5 8.0 %attend_4.1.refs_10_ = bf16[256,64,128]{2,1,0:T(8,128)(2,1)} custom-call(s32[2,8,64]{2,1,0:T(8,128)S(1)} %bitcast.15, s32[257]{0:T(512)S(1)} %copy-done.5, bf16[2,4,256,128]{3,2,1,0:T(8,128)(2,1)S(1)} %copy-done.1, bf16[2,4,256,128]{3,2,1,0:T(8,128)(2,1)S(1)} %collective-permute-done.4.refs_1_, ...), custom_call_target="tpu_custom_call", output_to_operand_aliasing={{}: (12, {})} | custom-call | flops 2147483648 | bytes 1 | tf_op jit(solution)/shard_map/attend_4/pallas_call | solution.py:207
  109.5 0.0 collective-permute-done.17.refs_8_
  109.5 8.0 %attend_6.1 = bf16[256,64,128]{2,1,0:T(8,128)(2,1)} custom-call(s32[2,8,64]{2,1,0:T(8,128)S(1)} %bitcast.16, s32[257]{0:T(512)S(1)} %copy-done.5, bf16[2,4,256,128]{3,2,1,0:T(8,128)(2,1)S(1)} %copy-done.1, bf16[2,4,256,128]{3,2,1,0:T(8,128)(2,1)S(1)} %collective-permute-done.4.refs_1_, ...), custom_call_target="tpu_custom_call", output_to_operand_aliasing={{}: (12, {})} | custom-call | flops 2147483648 | bytes 1 | tf_op jit(solution)/shard_map/attend_6/pallas_call | solution.py:207
  (9 shorter events, 0.1 us)
Async XLA Ops:
  2.7 16.3 %collective-permute-start.2 = (bf16[2,4,256,128]{3,2,1,0:T(8,128)(2,1)}, bf16[2,4,256,128]{3,2,1,0:T(8,128)(2,1)S(1)}, u32[]{:S(2)}, u32[]{:S(2)}) collective-permute-start(bf16[2,4,256,128]{3,2,1,0:T(8,128)(2,1)} %get-tuple-element.24.refs_0_), channel_id=1, source_target_pairs={{0,96},{16,112},{32,0},{48,16},{64,32},{80,48},{96,64},{112,80},{1... | collective-permute-start | bytes 1572872 | tf_op jit(solution)/shard_map/ppermute | solution.py:32
  6.0 13.9 %collective-permute-start.1 = (bf16[2,4,256,128]{3,2,1,0:T(8,128)(2,1)}, bf16[2,4,256,128]{3,2,1,0:T(8,128)(2,1)S(1)}, u32[]{:S(2)}, u32[]{:S(2)}) collective-permute-start(bf16[2,4,256,128]{3,2,1,0:T(8,128)(2,1)} %get-tuple-element.24.refs_0_), channel_id=1, source_target_pairs={{0,32},{16,48},{32,64},{48,80},{64,96},{80,112},{96,0},{112,16},{1... | collective-permute-start | bytes 1572872 | tf_op jit(solution)/shard_map/ppermute | solution.py:32
  6.0 12.9 %collective-permute-start = (bf16[2,2,256,128]{3,2,1,0:T(8,128)(2,1)}, bf16[2,2,256,128]{3,2,1,0:T(8,128)(2,1)S(1)}, u32[]{:S(2)}, u32[]{:S(2)}) collective-permute-start(bf16[2,2,256,128]{3,2,1,0:T(8,128)(2,1)} %get-tuple-element.23), channel_id=1, source_target_pairs={{0,16},{16,0},{32,48},{48,32},{64,80},{80,64},{96,112},{112,96},{1... | collective-permute-start | bytes 786440 | tf_op jit(solution)/shard_map/ppermute | solution.py:32
  13.7 5.2 %collective-permute-start.3 = (s32[32]{0:T(128)}, s32[32]{0:T(128)S(1)}, u32[]{:S(2)}, u32[]{:S(2)}) collective-permute-start(s32[32]{0:T(128)} %get-tuple-element.25), channel_id=1, source_target_pairs={{1,0},{2,1},{3,2},{4,3},{5,4},{6,5},{7,6},{8,7},{9,8},{10,9},{11,1... | collective-permute-start | bytes 392 | tf_op jit(solution)/shard_map/ppermute | solution.py:243
  19.9 7.0 %collective-permute-start.8 = (bf16[2,2,256,128]{3,2,1,0:T(8,128)(2,1)S(1)}, bf16[2,2,256,128]{3,2,1,0:T(8,128)(2,1)S(1)}, u32[]{:S(2)}, u32[]{:S(2)}) collective-permute-start(bf16[2,2,256,128]{3,2,1,0:T(8,128)(2,1)S(1)} %collective-permute-done.refs_1_), channel_id=1, source_target_pairs={{0,96},{16,112},{32,0},{48,16},{64,32},{80,48},{96,64},{112,80},{1... | collective-permute-start | bytes 786440 | tf_op jit(solution)/shard_map/ppermute | solution.py:32
  21.5 10.7 %collective-permute-start.5 = (bf16[2,2,256,128]{3,2,1,0:T(8,128)(2,1)S(1)}, bf16[2,2,256,128]{3,2,1,0:T(8,128)(2,1)S(1)}, u32[]{:S(2)}, u32[]{:S(2)}) collective-permute-start(bf16[2,2,256,128]{3,2,1,0:T(8,128)(2,1)S(1)} %collective-permute-done.refs_1_), channel_id=1, source_target_pairs={{0,32},{16,48},{32,64},{48,80},{64,96},{80,112},{96,0},{112,16},{1... | collective-permute-start | bytes 786440 | tf_op jit(solution)/shard_map/ppermute | solution.py:32
  21.5 37.4 %copy-start.3 = (bf16[2,4,256,128]{3,2,1,0:T(8,128)(2,1)S(1)}, bf16[2,4,256,128]{3,2,1,0:T(8,128)(2,1)}, u32[]{:S(2)}) copy-start(bf16[2,4,256,128]{3,2,1,0:T(8,128)(2,1)} %get-tuple-element.24.refs_0_) | copy-start | bytes 1572868
  21.5 37.4 %copy-start.4 = (s32[2,64,8]{1,2,0:T(8,128)S(1)}, s32[2,64,8]{1,2,0:T(8,128)}, u32[]{:S(2)}) copy-start(s32[2,64,8]{1,2,0:T(8,128)} %param.7) | copy-start | bytes 12292
  21.5 37.4 %copy-start.5 = (s32[257]{0:T(512)S(1)}, s32[257]{0:T(512)}, u32[]{:S(2)}) copy-start(s32[257]{0:T(512)} %get-tuple-element.21.places) | copy-start | bytes 3088
  21.5 25.4 %copy-start.1 = (bf16[2,4,256,128]{3,2,1,0:T(8,128)(2,1)S(1)}, bf16[2,4,256,128]{3,2,1,0:T(8,128)(2,1)}, u32[]{:S(2)}) copy-start(bf16[2,4,256,128]{3,2,1,0:T(8,128)(2,1)} %get-tuple-element.30.refs_0_) | copy-start | bytes 1572868
  21.5 37.4 %copy-start = (bf16[256,64,128]{2,1,0:T(8,128)(2,1)S(1)}, bf16[256,64,128]{2,1,0:T(8,128)(2,1)}, u32[]{:S(2)}) copy-start(bf16[256,64,128]{2,1,0:T(8,128)(2,1)} %refs_9_.5) | copy-start | bytes 12582916
  21.5 16.8 %collective-permute-start.6 = (bf16[2,3,256,128]{3,2,1,0:T(8,128)(2,1)S(1)}, bf16[2,3,256,128]{3,2,1,0:T(8,128)(2,1)S(1)}, u32[]{:S(2)}, u32[]{:S(2)}) collective-permute-start(bf16[2,3,256,128]{3,2,1,0:T(8,128)(2,1)S(1)} %slice.24), channel_id=1, source_target_pairs={{0,32},{16,48},{32,64},{48,80},{64,96},{80,112},{96,0},{112,16},{1... | collective-permute-start | bytes 1179656 | tf_op jit(solution)/shard_map/ppermute | solution.py:32
  26.9 11.5 %collective-permute-start.9 = (bf16[2,2,256,128]{3,2,1,0:T(8,128)(2,1)S(1)}, bf16[2,2,256,128]{3,2,1,0:T(8,128)(2,1)S(1)}, u32[]{:S(2)}, u32[]{:S(2)}) collective-permute-start(bf16[2,2,256,128]{3,2,1,0:T(8,128)(2,1)S(1)} %collective-permute-done.8.refs_3_), channel_id=1, source_target_pairs={{0,96},{16,112},{32,0},{48,16},{64,32},{80,48},{96,64},{112,80},{1... | collective-permute-start | bytes 786440 | tf_op jit(solution)/shard_map/ppermute | solution.py:32
  31.3 14.5 %collective-permute-start.7 = (bf16[2,1,256,128]{3,2,1,0:T(8,128)(2,1)S(1)}, bf16[2,1,256,128]{3,2,1,0:T(8,128)(2,1)S(1)}, u32[]{:S(2)}, u32[]{:S(2)}) collective-permute-start(bf16[2,1,256,128]{3,2,1,0:T(8,128)(2,1)S(1)} %slice.27), channel_id=1, source_target_pairs={{0,96},{16,112},{32,0},{48,16},{64,32},{80,48},{96,64},{112,80},{1... | collective-permute-start | bytes 393224 | tf_op jit(solution)/shard_map/ppermute | solution.py:32
  31.4 15.5 %collective-permute-start.4 = (bf16[2,4,256,128]{3,2,1,0:T(8,128)(2,1)}, bf16[2,4,256,128]{3,2,1,0:T(8,128)(2,1)S(1)}, u32[]{:S(2)}, u32[]{:S(2)}) collective-permute-start(bf16[2,4,256,128]{3,2,1,0:T(8,128)(2,1)} %get-tuple-element.30.refs_0_), channel_id=1, source_target_pairs={{0,16},{16,0},{32,48},{48,32},{64,80},{80,64},{96,112},{112,96},{1... | collective-permute-start | bytes 1572872 | tf_op jit(solution)/shard_map/ppermute | solution.py:32
  38.4 1.0 copy-start.2
  40.2 17.2 %collective-permute-start.14 = (bf16[2,2,512,128]{3,2,1,0:T(8,128)(2,1)S(1)}, bf16[2,2,512,128]{3,2,1,0:T(8,128)(2,1)S(1)}, u32[]{:S(2)}, u32[]{:S(2)}) collective-permute-start(bf16[2,2,512,128]{3,2,1,0:T(8,128)(2,1)S(1)} %pick_blocks_0.1), channel_id=1, source_target_pairs={{0,1},{1,2},{2,3},{3,4},{4,5},{5,6},{6,7},{7,8},{8,9},{9,10},{10,1... | collective-permute-start | bytes 1572872 | tf_op jit(solution)/shard_map/ppermute | solution.py:249
  46.0 29.6 %collective-permute-start.19 = (bf16[4,2,2,256,128]{4,3,2,1,0:T(8,128)(2,1)S(1)}, bf16[4,2,2,256,128]{4,3,2,1,0:T(8,128)(2,1)S(1)}, u32[]{:S(2)}, u32[]{:S(2)}) collective-permute-start(bf16[4,2,2,256,128]{4,3,2,1,0:T(8,128)(2,1)S(1)} %pad_maximum_fusion.refs_0_), channel_id=1, source_target_pairs={{0,16},{16,0},{32,48},{48,32},{64,80},{80,64},{96,112},{112,96},{1... | collective-permute-start | bytes 3145736 | tf_op jit(solution)/shard_map/ppermute | solution.py:32
  46.9 20.1 %collective-permute-start.12 = (bf16[2,4,256,128]{3,2,1,0:T(8,128)(2,1)S(1)}, bf16[2,4,256,128]{3,2,1,0:T(8,128)(2,1)S(1)}, u32[]{:S(2)}, u32[]{:S(2)}) collective-permute-start(bf16[2,4,256,128]{3,2,1,0:T(8,128)(2,1)S(1)} %copy-done.1), channel_id=1, source_target_pairs={{0,32},{16,48},{32,64},{48,80},{64,96},{80,112},{96,0},{112,16},{1... | collective-permute-start | bytes 1572872 | tf_op jit(solution)/shard_map/ppermute | solution.py:32
  46.9 20.1 %collective-permute-start.10 = (bf16[2,4,256,128]{3,2,1,0:T(8,128)(2,1)S(1)}, bf16[2,4,256,128]{3,2,1,0:T(8,128)(2,1)S(1)}, u32[]{:S(2)}, u32[]{:S(2)}) collective-permute-start(bf16[2,4,256,128]{3,2,1,0:T(8,128)(2,1)S(1)} %copy-done.1), channel_id=1, source_target_pairs={{0,96},{16,112},{32,0},{48,16},{64,32},{80,48},{96,64},{112,80},{1... | collective-permute-start | bytes 1572872 | tf_op jit(solution)/shard_map/ppermute | solution.py:32
  49.6 22.6 %collective-permute-start.13 = (bf16[2,4,256,128]{3,2,1,0:T(8,128)(2,1)S(1)}, bf16[2,4,256,128]{3,2,1,0:T(8,128)(2,1)S(1)}, u32[]{:S(2)}, u32[]{:S(2)}) collective-permute-start(bf16[2,4,256,128]{3,2,1,0:T(8,128)(2,1)S(1)} %collective-permute-done.4.refs_1_), channel_id=1, source_target_pairs={{0,32},{16,48},{32,64},{48,80},{64,96},{80,112},{96,0},{112,16},{1... | collective-permute-start | bytes 1572872 | tf_op jit(solution)/shard_map/ppermute | solution.py:32
  57.4 14.8 %collective-permute-start.11 = (bf16[2,4,256,128]{3,2,1,0:T(8,128)(2,1)S(1)}, bf16[2,4,256,128]{3,2,1,0:T(8,128)(2,1)S(1)}, u32[]{:S(2)}, u32[]{:S(2)}) collective-permute-start(bf16[2,4,256,128]{3,2,1,0:T(8,128)(2,1)S(1)} %collective-permute-done.4.refs_1_), channel_id=1, source_target_pairs={{0,96},{16,112},{32,0},{48,16},{64,32},{80,48},{96,64},{112,80},{1... | collective-permute-start | bytes 1572872 | tf_op jit(solution)/shard_map/ppermute | solution.py:32
  72.2 13.2 %collective-permute-start.15 = (bf16[2,4,256,128]{3,2,1,0:T(8,128)(2,1)S(1)}, bf16[2,4,256,128]{3,2,1,0:T(8,128)(2,1)S(1)}, u32[]{:S(2)}, u32[]{:S(2)}) collective-permute-start(bf16[2,4,256,128]{3,2,1,0:T(8,128)(2,1)S(1)} %collective-permute-done.12.refs_6_), channel_id=1, source_target_pairs={{0,32},{16,48},{32,64},{48,80},{64,96},{80,112},{96,0},{112,16},{1... | collective-permute-start | bytes 1572872 | tf_op jit(solution)/shard_map/ppermute | solution.py:32
  72.2 13.2 %collective-permute-start.16 = (bf16[2,4,256,128]{3,2,1,0:T(8,128)(2,1)S(1)}, bf16[2,4,256,128]{3,2,1,0:T(8,128)(2,1)S(1)}, u32[]{:S(2)}, u32[]{:S(2)}) collective-permute-start(bf16[2,4,256,128]{3,2,1,0:T(8,128)(2,1)S(1)} %collective-permute-done.11.refs_3_), channel_id=1, source_target_pairs={{0,96},{16,112},{32,0},{48,16},{64,32},{80,48},{96,64},{112,80},{1... | collective-permute-start | bytes 1572872 | tf_op jit(solution)/shard_map/ppermute | solution.py:32
  76.4 17.0 %collective-permute-start.20 = (bf16[2,2,512,128]{3,2,1,0:T(8,128)(2,1)S(1)}, bf16[2,2,512,128]{3,2,1,0:T(8,128)(2,1)S(1)}, u32[]{:S(2)}, u32[]{:S(2)}) collective-permute-start(bf16[2,2,512,128]{3,2,1,0:T(8,128)(2,1)S(1)} %pick_blocks_2.1), channel_id=1, source_target_pairs={{0,1},{1,2},{2,3},{3,4},{4,5},{5,6},{6,7},{7,8},{8,9},{9,10},{10,1... | collective-permute-start | bytes 1572872 | tf_op jit(solution)/shard_map/ppermute | solution.py:249
  86.2 15.3 %collective-permute-start.18 = (bf16[2,2,512,128]{3,2,1,0:T(8,128)(2,1)S(1)}, bf16[2,2,512,128]{3,2,1,0:T(8,128)(2,1)S(1)}, u32[]{:S(2)}, u32[]{:S(2)}) collective-permute-start(bf16[2,2,512,128]{3,2,1,0:T(8,128)(2,1)S(1)} %pick_blocks_4.1), channel_id=1, source_target_pairs={{0,1},{1,2},{2,3},{3,4},{4,5},{5,6},{6,7},{7,8},{8,9},{9,10},{10,1... | collective-permute-start | bytes 1572872 | tf_op jit(solution)/shard_map/ppermute | solution.py:249
  91.3 18.2 %collective-permute-start.17 = (bf16[2,2,512,128]{3,2,1,0:T(8,128)(2,1)S(1)}, bf16[2,2,512,128]{3,2,1,0:T(8,128)(2,1)S(1)}, u32[]{:S(2)}, u32[]{:S(2)}) collective-permute-start(bf16[2,2,512,128]{3,2,1,0:T(8,128)(2,1)S(1)} %pick_blocks_6.1), channel_id=1, source_target_pairs={{0,1},{1,2},{2,3},{3,4},{4,5},{5,6},{6,7},{7,8},{8,9},{9,10},{10,1... | collective-permute-start | bytes 1572872 | tf_op jit(solution)/shard_map/ppermute | solution.py:249
